TPU v7x, 32 devices: a whole 2x2x4 slice. The times are simulated.
32 devices in a mesh: seq: 8 (over z, y), mp: 4 (over x, core).
Axes of the slice: x: 2, y: 2, z: 4, core: 2. Of those that a mesh axis runs over, the one named last changes fastest.
Arguments:
- out_grad: bfloat16 [4096, 8192], P('seq', 'mp'), may hold values from -6 to 6
- out_weight: bfloat16 [4096, 8192], P('mp'), may hold values from -0.0625 to 0.0625
- queries: bfloat16 [4096, 4096], P('seq', 'mp'), may hold values from -5 to 5
- keys: bfloat16 [16, 128, 4096], P('seq', None, 'mp'), may hold values from -5 to 5
- values: bfloat16 [16, 128, 4096], P('seq', None, 'mp'), may hold values from -6 to 6
- retrieval: int32 [64, 2], replicated, may hold values from 0 to 15, as said below
- counts: int32 [64], P('seq'), may hold values from 1 to 2
Outputs:
- query_grad: bfloat16 [4096, 4096], P('seq', 'mp')
- key_grad: bfloat16 [16, 128, 4096], P('seq', None, 'mp')
- value_grad: bfloat16 [16, 128, 4096], P('seq', None, 'mp')
Inputs may be any that keep to these rules, and one draw needn't show every extreme that they name: `retrieval`: entry e is held by index e // 2 of seq. The 16 neighbour places of one index's blocks name entries of any one owner at most 2 times, and some owner is named exactly 2 times by the blocks of every index.
All inputs are finite; a program needn't handle non-finite values.
Results may differ from a plain program's by a relative error of at most 0.0091.
Values may be sent and summed in bfloat16 or wider, within the bound.
No kernel may reach another device: no remote copies, remote signals or barrier semaphores. Data moves between devices by JAX's collectives and lax.ppermute only.
A program may use at most 128 MiB of HBM per device.

v0:
```python
import math

import jax
import jax.numpy as jnp
from jax import lax
from jax.sharding import PartitionSpec as P

HEAD = 128
BLOCK = 64
NEIGH = 2


def rank_slots(owners):
    slot_total = owners.shape[-1]
    earlier_mask = jnp.arange(slot_total)[None, :] < jnp.arange(slot_total)[:, None]
    same_owner = owners[..., :, None] == owners[..., None, :]
    return jnp.sum(same_owner & earlier_mask, axis=-1)


def on_device(out_grad, out_weight, queries, keys, values, retrieval, counts):
    seq_count = lax.axis_size("seq")
    my_index = lax.axis_index("seq")
    tok_rows, head_cols = queries.shape
    entries_here = keys.shape[0]
    nbr_rows = keys.shape[1]
    heads_here = head_cols // HEAD
    blocks_here = tok_rows // BLOCK
    slot_count = blocks_here * NEIGH
    slot_cap = (slot_count + seq_count - 1) // seq_count
    score_scale = 1.0 / math.sqrt(HEAD)
    grad_out = lax.dot_general(
        lax.all_gather(out_grad, "mp", axis=1, tiled=True),
        out_weight,
        (((1,), (1,)), ((), ())),
        preferred_element_type=jnp.float32,
    ).astype(jnp.bfloat16)
    all_lists = retrieval.reshape(seq_count, slot_count)
    owners = all_lists // entries_here
    all_ranks = rank_slots(owners)
    my_lists = lax.dynamic_index_in_dim(all_lists, my_index, 0, keepdims=False)
    my_owner = my_lists // entries_here
    my_rank = lax.dynamic_index_in_dim(all_ranks, my_index, 0, keepdims=False)
    flat_slot = my_owner * slot_cap + my_rank
    chosen = (owners == my_index)[:, None, :] & (
        all_ranks[:, None, :] == jnp.arange(slot_cap)[None, :, None]
    )
    filled = jnp.any(chosen, axis=2)
    picked = jnp.sum(jnp.where(chosen, all_lists[:, None, :] % entries_here, 0), axis=2)
    all_keys, all_values = (
        lax.all_gather(keys, "seq", axis=0, tiled=True),
        lax.all_gather(values, "seq", axis=0, tiled=True),
    )
    slot_keys = jnp.take(all_keys, my_lists, axis=0)
    slot_values = jnp.take(all_values, my_lists, axis=0)
    query_rows = queries.reshape(blocks_here, BLOCK, heads_here, HEAD)
    grad_rows = grad_out.reshape(blocks_here, BLOCK, heads_here, HEAD)
    key_rows = slot_keys.reshape(blocks_here, NEIGH * nbr_rows, heads_here, HEAD)
    value_rows = slot_values.reshape(blocks_here, NEIGH * nbr_rows, heads_here, HEAD)
    live_keys = jnp.arange(NEIGH * nbr_rows)[None, :] < (counts * nbr_rows)[:, None]
    live_mask = live_keys[:, None, None, :]
    scores = (
        jnp.einsum("cqhe,ckhe->chqk", query_rows, key_rows, preferred_element_type=jnp.float32)
        * score_scale
    )
    row_max = jnp.max(jnp.where(live_mask, scores, -jnp.inf), axis=-1, keepdims=True)
    raised = jnp.where(live_mask, jnp.exp(scores - row_max), 0.0)
    attn_weights = raised / jnp.sum(raised, axis=-1, keepdims=True)
    weights_low = attn_weights.astype(jnp.bfloat16)
    attn_out = jnp.einsum(
        "chqk,ckhe->cqhe", weights_low, value_rows, preferred_element_type=jnp.float32
    )
    row_dot = jnp.sum(grad_rows.astype(jnp.float32) * attn_out, axis=-1)
    grad_weights = jnp.einsum(
        "cqhe,ckhe->chqk", grad_rows, value_rows, preferred_element_type=jnp.float32
    )
    grad_scores = attn_weights * (grad_weights - jnp.transpose(row_dot, (0, 2, 1))[..., None])
    grad_low = grad_scores.astype(jnp.bfloat16)
    query_grad = (
        (
            jnp.einsum("chqk,ckhe->cqhe", grad_low, key_rows, preferred_element_type=jnp.float32)
            * score_scale
        )
        .astype(jnp.bfloat16)
        .reshape(tok_rows, head_cols)
    )
    key_terms = (
        (
            jnp.einsum("chqk,cqhe->ckhe", grad_low, query_rows, preferred_element_type=jnp.float32)
            * score_scale
        )
        .astype(jnp.bfloat16)
        .reshape(slot_count, nbr_rows, head_cols)
    )
    value_terms = (
        jnp.einsum("chqk,cqhe->ckhe", weights_low, grad_rows, preferred_element_type=jnp.float32)
        .astype(jnp.bfloat16)
        .reshape(slot_count, nbr_rows, head_cols)
    )
    key_back = (
        jnp.zeros((seq_count * slot_cap, nbr_rows, head_cols), jnp.bfloat16)
        .at[flat_slot]
        .set(key_terms)
        .reshape(seq_count, slot_cap, nbr_rows, head_cols)
    )
    value_back = (
        jnp.zeros((seq_count * slot_cap, nbr_rows, head_cols), jnp.bfloat16)
        .at[flat_slot]
        .set(value_terms)
        .reshape(seq_count, slot_cap, nbr_rows, head_cols)
    )
    back_keys, back_values = (
        lax.all_to_all(key_back, "seq", split_axis=0, concat_axis=0, tiled=True),
        lax.all_to_all(value_back, "seq", split_axis=0, concat_axis=0, tiled=True),
    )
    summing = (
        ((picked[None, :, :] == jnp.arange(entries_here)[:, None, None]) & filled[None, :, :])
        .astype(jnp.bfloat16)
        .reshape(entries_here, seq_count * slot_cap)
    )
    key_grad = (
        jnp.dot(
            summing,
            back_keys.reshape(seq_count * slot_cap, nbr_rows * head_cols),
            preferred_element_type=jnp.float32,
        )
        .astype(jnp.bfloat16)
        .reshape(entries_here, nbr_rows, head_cols)
    )
    value_grad = (
        jnp.dot(
            summing,
            back_values.reshape(seq_count * slot_cap, nbr_rows * head_cols),
            preferred_element_type=jnp.float32,
        )
        .astype(jnp.bfloat16)
        .reshape(entries_here, nbr_rows, head_cols)
    )
    return (query_grad, key_grad, value_grad)


def solution(mesh):
    return jax.shard_map(
        on_device,
        mesh=mesh,
        in_specs=(
            P("seq", "mp"),
            P("mp", None),
            P("seq", "mp"),
            P("seq", None, "mp"),
            P("seq", None, "mp"),
            P(),
            P("seq"),
        ),
        out_specs=(P("seq", "mp"), P("seq", None, "mp"), P("seq", None, "mp")),
        check_vma=False,
    )
```

profile of v0, /device:TPU:0, one launch (start us, length us, event | category | flops | bytes accessed | tf_op | source)
XLA Modules:
  0.0 474.7 jit_solution(14382815806374926681)
XLA Ops:
  7.2 0.0 copy-start.3
  7.2 0.0 all-gather.8.cloned.1.call-start
  7.2 0.7 all-gather.8.cloned.1.call-update
  7.9 0.0 all-gather.4.cloned.1.call-start
  8.0 0.7 all-gather.4.cloned.1.call-update
  8.7 0.0 all-gather.6.cloned.1.call-start
  8.7 0.7 all-gather.6.cloned.1.call-update
  9.4 0.8 copy.46
  10.2 0.1 reshape.279
  10.2 1.5 copy.62
  11.8 0.3 convert_reduce_fusion
  12.1 0.0 copy-done.3
  12.1 0.1 iota_compare_fusion.2
  12.2 74.1 %all-gather.8.cloned.1.call-done = bf16[16,128,1024]{2,1,0:T(8,128)(2,1)} async-done(((bf16[2,128,1024]{2,1,0:T(8,128)(2,1)}), bf16[16,128,1024]{2,1,0:T(8,128)(2,1)}) %all-gather.8.cloned.1.call-update) | async-done | bytes 4194320 | tf_op jit(solution)/shard_map/all_gather | solution.py:51
  86.3 4.9 %gather_fusion.1 = bf16[16,128,1024]{2,1,0:T(8,128)(2,1)} fusion(bf16[16,128,1024]{2,1,0:T(8,128)(2,1)} %all-gather.8.cloned.1.call-done, s32[1024]{0:T(1024)S(1)} %pad_clamp_fusion), kind=kCustom, calls=%fused_computation.1.clone | custom fusion | bytes 8388672 | tf_op jit(solution)/shard_map/jit(_take)/gather | solution.py:54
  91.2 68.9 %all-gather.4.cloned.1.call-done = bf16[16,128,1024]{2,1,0:T(8,128)(2,1)} async-done(((bf16[2,128,1024]{2,1,0:T(8,128)(2,1)}), bf16[16,128,1024]{2,1,0:T(8,128)(2,1)}) %all-gather.4.cloned.1.call-update) | async-done | bytes 4194320 | tf_op jit(solution)/shard_map/all_gather | solution.py:50
  160.1 5.0 %gather_fusion = bf16[16,128,1024]{2,1,0:T(8,128)(2,1)} fusion(bf16[16,128,1024]{2,1,0:T(8,128)(2,1)} %all-gather.4.cloned.1.call-done, s32[1024]{0:T(1024)S(1)} %pad_clamp_fusion), kind=kCustom, calls=%fused_computation.clone | custom fusion | bytes 8388672 | tf_op jit(solution)/shard_map/jit(_take)/gather | solution.py:53
  165.1 7.4 %broadcast_select_fusion.1 = (bf16[16,128,1024]{2,1,0:T(8,128)(2,1)S(1)}, bf16[16,128,1024]{2,1,0:T(8,128)(2,1)}) fusion(bf16[16,128,1024]{2,1,0:T(8,128)(2,1)} %gather_fusion, pred[16]{0:T(512)(128)(4,1)S(1)} %get-tuple-element.6, bf16[16,128,1024]{2,1,0:T(8,128)(2,1)} %gather_fusion.1), kind=kLoop, calls=%fused_computation.17 | loop fusion | flops 4194304 | bytes 16777232 | tf_op jit(solution)/shard_map/jit(_take)/select_n | solution.py:53
  172.5 1.1 copy.61
  173.6 0.0 copy-start.1
  173.6 1.6 fusion.3
  175.2 0.3 copy-done.1
  175.5 3.5 bitcast_reduce_fusion
  179.0 39.2 %all-gather.6.cloned.1.call-done = bf16[512,8192]{1,0:T(8,128)(2,1)} async-done(((bf16[512,2048]{1,0:T(8,128)(2,1)}), bf16[512,8192]{1,0:T(8,128)(2,1)}) %all-gather.6.cloned.1.call-update) | async-done | bytes 8388624 | tf_op jit(solution)/shard_map/all_gather | solution.py:32
  218.2 0.0 copy-start.4
  218.2 15.0 %fusion.25 = bf16[64,8,8,128]{3,1,2,0:T(8,128)(2,1)S(1)} fusion(bf16[512,8192]{1,0:T(8,128)(2,1)} %all-gather.6.cloned.1.call-done, bf16[1024,8192]{1,0:T(8,128)(2,1)} %param.10), kind=kOutput, calls=%fused_computation.35 | convolution fusion | flops 8590458880 | bytes 26214400 | tf_op jit(solution)/shard_map/dot_general | solution.py:31
  233.2 0.3 copy.63
  233.5 0.0 copy-start.2
  233.5 0.0 copy-done.4
  233.5 3.1 convert_bitcast_fusion
  236.7 6.8 %copy.60 = bf16[8,256,8,128]{3,2,1,0:T(8,128)(2,1)} copy(bf16[8,256,8,128]{1,3,2,0:T(8,128)(2,1)} %convert_bitcast_fusion) | data formatting | bytes 8388608 | tf_op jit(solution)/shard_map/convert_element_type | solution.py:96
  243.4 7.3 %reshape.321 = bf16[16,128,1024]{2,1,0:T(8,128)(2,1)} reshape(bf16[8,256,8,128]{3,2,1,0:T(8,128)(2,1)} %copy.60) | data formatting | bytes 8388608 | tf_op jit(solution)/shard_map/reshape | solution.py:97
  250.7 2.5 broadcast.242.clone
  253.2 11.0 %scatter_fusion.1 = bf16[16,128,1024]{2,1,0:T(8,128)(2,1)} fusion(bf16[16,128,1024]{2,1,0:T(8,128)(2,1)} %broadcast.242.clone, s32[16]{0:T(128)S(1)} %fusion.39, bf16[16,128,1024]{2,1,0:T(8,128)(2,1)} %reshape.321), kind=kCustom, calls=%fused_computation.3 | custom fusion | bytes 12582976 | tf_op jit(solution)/shard_map/scatter | solution.py:108
  264.2 5.5 %all-to-all-start.1 = ((bf16[8,2,128,1024]{3,2,1,0:T(8,128)(2,1)}), bf16[8,2,128,1024]{3,2,1,0:T(8,128)(2,1)}, u32[]{:S(2)}, u32[]{:S(2)}) async-start(bf16[8,2,128,1024]{3,2,1,0:T(8,128)(2,1)} %bitcast.86), calls=%async_computation.1 | async-start | bytes 8388608 | tf_op jit(solution)/shard_map/all_to_all | solution.py:113
  269.7 0.0 copy-start.5
  269.7 3.5 copy.64
  273.1 0.0 copy-done.2
  273.2 0.0 copy-done.5
  273.2 1.7 fusion.14
  274.9 2.8 multiply_convert_fusion.1
  277.7 1.5 fusion.1
  279.2 4.8 %copy.58 = bf16[8,256,8,128]{3,2,1,0:T(8,128)(2,1)} copy(bf16[8,256,8,128]{3,1,2,0:T(8,128)(2,1)S(1)} %fusion.1) | data formatting | bytes 8388608 | tf_op jit(solution)/shard_map/convert_element_type | solution.py:91
  284.1 7.3 %reshape.313 = bf16[16,128,1024]{2,1,0:T(8,128)(2,1)} reshape(bf16[8,256,8,128]{3,2,1,0:T(8,128)(2,1)} %copy.58) | data formatting | bytes 8388608 | tf_op jit(solution)/shard_map/reshape | solution.py:92
  291.3 2.5 broadcast.242.clone.1
  293.8 11.0 %scatter_fusion = bf16[16,128,1024]{2,1,0:T(8,128)(2,1)} fusion(bf16[16,128,1024]{2,1,0:T(8,128)(2,1)} %broadcast.242.clone.1, s32[16]{0:T(128)S(1)} %fusion.39, bf16[16,128,1024]{2,1,0:T(8,128)(2,1)} %reshape.313), kind=kCustom, calls=%fused_computation.2 | custom fusion | bytes 12582976 | tf_op jit(solution)/shard_map/scatter | solution.py:102
  304.8 58.6 %all-to-all-done.1 = bf16[8,2,128,1024]{3,2,1,0:T(8,128)(2,1)} async-done(((bf16[8,2,128,1024]{3,2,1,0:T(8,128)(2,1)}), bf16[8,2,128,1024]{3,2,1,0:T(8,128)(2,1)}, u32[]{:S(2)}, u32[]{:S(2)}) %all-to-all-start.1) | async-done | bytes 4194336 | tf_op jit(solution)/shard_map/all_to_all | solution.py:113
  363.4 4.8 %all-to-all-start = ((bf16[8,2,128,1024]{3,2,1,0:T(8,128)(2,1)}), bf16[8,2,128,1024]{3,2,1,0:T(8,128)(2,1)}, u32[]{:S(2)}, u32[]{:S(2)}) async-start(bf16[8,2,128,1024]{3,2,1,0:T(8,128)(2,1)} %bitcast.85), calls=%async_computation | async-start | bytes 8388608 | tf_op jit(solution)/shard_map/all_to_all | solution.py:112
  368.2 0.1 fusion.34
  368.3 0.1 copy.56
  368.4 0.1 and.97
  368.5 0.2 select_reduce_fusion.1
  368.7 0.1 copy.55
  368.8 0.1 eq.62
  368.8 3.0 fusion.26
  371.8 0.7 copy.54
  372.5 1.2 copy.98
  373.8 6.4 %copy.68 = bf16[2,8,128,1024]{3,1,2,0:T(8,128)(2,1)} copy(bf16[2,8,128,1024]{3,2,1,0:T(8,128)(2,1)} %bitcast.37) | data formatting | bytes 8388608
  380.2 80.5 %all-to-all-done = bf16[8,2,128,1024]{3,2,1,0:T(8,128)(2,1)} async-done(((bf16[8,2,128,1024]{3,2,1,0:T(8,128)(2,1)}), bf16[8,2,128,1024]{3,2,1,0:T(8,128)(2,1)}, u32[]{:S(2)}, u32[]{:S(2)}) %all-to-all-start) | async-done | bytes 4194336 | tf_op jit(solution)/shard_map/all_to_all | solution.py:112
  460.7 4.7 copy.66
  465.4 0.0 copy-done
  465.4 0.8 convolution_convert_fusion
  466.2 0.8 convolution_convert_fusion.1
  466.9 1.3 copy_bitcast_fusion.1
  (8 shorter events, 0.1 us)
Async XLA Ops:
  7.2 5.0 %copy-start.3 = (s32[8]{0:T(128)S(1)}, s32[8]{0:T(128)}, u32[]{:S(2)}) copy-start(s32[8]{0:T(128)} %param.15) | copy-start | bytes 100
  7.2 79.1 %all-gather.8.cloned.1.call-start = ((), (), s32[]{:S(2)}) async-start(), calls=%async_computation.4 | async-start | bytes 4718592 | tf_op jit(solution)/shard_map/all_gather | solution.py:51
  7.9 152.2 %all-gather.4.cloned.1.call-start = ((), (), s32[]{:S(2)}) async-start(), calls=%async_computation.2 | async-start | bytes 4718592 | tf_op jit(solution)/shard_map/all_gather | solution.py:50
  8.7 209.6 %all-gather.6.cloned.1.call-start = ((), (), s32[]{:S(2)}) async-start(), calls=%async_computation.3 | async-start | bytes 10485760 | tf_op jit(solution)/shard_map/all_gather | solution.py:32
  173.6 1.9 copy-start.1
  218.2 15.3 %copy-start.4 = (f32[8,8,256,64]{2,3,1,0:T(8,128)S(1)}, f32[8,8,256,64]{2,3,1,0:T(8,128)}, u32[]{:S(2)}) copy-start(f32[8,8,256,64]{2,3,1,0:T(8,128)} %get-tuple-element.11) | copy-start | bytes 12582916
  233.5 39.6 %copy-start.2 = (bf16[64,8,8,128]{3,2,1,0:T(8,128)(2,1)}, bf16[64,8,8,128]{3,2,1,0:T(8,128)(2,1)S(1)}, u32[]{:S(2)}) copy-start(bf16[64,8,8,128]{3,2,1,0:T(8,128)(2,1)S(1)} %copy.63) | copy-start | bytes 3145732
  264.2 99.2 %all-to-all-start.1 = ((bf16[8,2,128,1024]{3,2,1,0:T(8,128)(2,1)}), bf16[8,2,128,1024]{3,2,1,0:T(8,128)(2,1)}, u32[]{:S(2)}, u32[]{:S(2)}) async-start(bf16[8,2,128,1024]{3,2,1,0:T(8,128)(2,1)} %bitcast.86), calls=%async_computation.1 | async-start | bytes 8388608 | tf_op jit(solution)/shard_map/all_to_all | solution.py:113
  269.7 3.5 copy-start.5
  363.4 97.4 %all-to-all-start = ((bf16[8,2,128,1024]{3,2,1,0:T(8,128)(2,1)}), bf16[8,2,128,1024]{3,2,1,0:T(8,128)(2,1)}, u32[]{:S(2)}, u32[]{:S(2)}) async-start(bf16[8,2,128,1024]{3,2,1,0:T(8,128)(2,1)} %bitcast.85), calls=%async_computation | async-start | bytes 8388608 | tf_op jit(solution)/shard_map/all_to_all | solution.py:112
  460.7 4.7 copy-start
Sparse Core Ops, SparseCore 0:
  10.1 76.0 all-gather.7
  88.4 71.6 all-gather.3
  161.7 56.5 all-gather.5
where the time goes:
time: 476 us; the launch traced here: 475 us
  waiting for transfers between devices  323 us (68%)
  local copies, waits for them, and re-layouts  85.2 us (18%)
  matrix products  30.2 us (6%)
  between operations  14 us (3%)
  other arithmetic  11.7 us (2%)
  starting transfers between devices  10.4 us (2%)
    all_to_all x1, waiting for transfers between devices, on_device(): lax.all_to_all(key_back, 'seq', split_axis=0, concat_axis=0, tiled=True)  80.5 us
    all_gather x1, waiting for transfers between devices, on_device(): lax.all_gather(values, 'seq', axis=0, tiled=True)  74.1 us
    all_gather x1, waiting for transfers between devices, on_device(): lax.all_gather(keys, 'seq', axis=0, tiled=True)  68.9 us
    all_to_all x1, waiting for transfers between devices, on_device(): lax.all_to_all(value_back, 'seq', split_axis=0, concat_axis=0, tiled=True)  58.6 us
    all_gather x1, waiting for transfers between devices, on_device(): lax.all_gather(out_grad, 'mp', axis=1, tiled=True)  39.2 us
    unnamed x20, local copies, waits for them, and re-layouts  19.8 us
    dot_general x1, matrix products, on_device(): lax.dot_general(lax.all_gather(out_grad, 'mp', axis=1, tiled=True), out_w...  15 us
    scatter x1, local copies, waits for them, and re-layouts, on_device(): value_back = jnp.zeros((seq_count * slot_cap, nbr_rows, head_cols), jnp.b...  11 us
  transfers between devices with their start and end apart: 5, of which 5 were waited for; matrix products, arithmetic and copies ran while one was open for 15% of the time, Pallas kernels for 0%

commit v1 on v0

v1 whole, which is shorter than its diff:
```python
import functools
import math

import jax
import jax.numpy as jnp
from jax import lax
from jax.experimental import pallas as pl
from jax.experimental.pallas import tpu as pltpu
from jax.sharding import PartitionSpec as P

HEAD = 128
BLOCK = 64
NEIGH = 2
LANES = 128
HEAD_CHUNKS = 2
F32 = jnp.float32
BF16 = jnp.bfloat16


def vmem_params(flops=0, moved=0):
    return dict(
        compiler_params=pltpu.CompilerParams(vmem_limit_bytes=48 * 1024 * 1024),
        cost_estimate=pl.CostEstimate(flops=flops, bytes_accessed=moved, transcendentals=0),
    )


def slot_of_place(lists_ref, base, place, entries_here, slot_cap):
    owner = lists_ref[base + place] // entries_here
    rank = 0
    for earlier in range(place):
        rank = rank + jnp.where(lists_ref[base + earlier] // entries_here == owner, 1, 0)
    return owner * slot_cap + rank


def place_rows(rows, lists_flat, my_index, n_seq, slot_cap, entries_here):
    tok_rows, cols = rows.shape
    places = tok_rows // BLOCK * NEIGH
    slots = n_seq * slot_cap

    def body(lists_ref, index_ref, rows_ref, out_ref, zero_ref, sems):
        base = index_ref[0] * places
        if slots > places:
            zero_ref[...] = jnp.zeros_like(zero_ref)
            for slot in range(slots):
                pltpu.make_async_copy(zero_ref, out_ref.at[slot], sems.at[slot]).start()
            for slot in range(slots):
                pltpu.make_async_copy(zero_ref, out_ref.at[slot], sems.at[slot]).wait()
        copies = []
        for place in range(places):
            slot = slot_of_place(lists_ref, base, place, entries_here, slot_cap)
            start = place // NEIGH * BLOCK
            copies.append(
                pltpu.make_async_copy(
                    rows_ref.at[pl.ds(start, BLOCK)], out_ref.at[slot], sems.at[place]
                )
            )
            copies[-1].start()
        for copy in copies:
            copy.wait()

    return pl.pallas_call(
        body,
        out_shape=jax.ShapeDtypeStruct((slots, BLOCK, cols), rows.dtype),
        in_specs=[
            pl.BlockSpec(memory_space=pltpu.SMEM),
            pl.BlockSpec(memory_space=pltpu.SMEM),
            pl.BlockSpec(memory_space=pl.ANY),
        ],
        out_specs=pl.BlockSpec(memory_space=pl.ANY),
        scratch_shapes=[
            pltpu.VMEM((BLOCK, cols), rows.dtype),
            pltpu.SemaphoreType.DMA((max(slots, places),)),
        ],
        name="place_rows",
        **vmem_params(moved=2 * slots * BLOCK * cols * 2),
    )(lists_flat, my_index, rows)


def join_places(back, lists_flat, my_index, n_seq, slot_cap, entries_here, blocks_here):
    slots, _, cols = back.shape
    places = blocks_here * NEIGH

    def body(lists_ref, index_ref, back_ref, out_ref):
        base = index_ref[0] * places
        for block in range(blocks_here):
            total = 0.0
            for neighbour in range(NEIGH):
                slot = slot_of_place(
                    lists_ref, base, block * NEIGH + neighbour, entries_here, slot_cap
                )
                total = total + back_ref[slot].astype(F32)
            out_ref[block * BLOCK : (block + 1) * BLOCK, :] = total.astype(out_ref.dtype)

    return pl.pallas_call(
        body,
        out_shape=jax.ShapeDtypeStruct((blocks_here * BLOCK, cols), back.dtype),
        in_specs=[
            pl.BlockSpec(memory_space=pltpu.SMEM),
            pl.BlockSpec(memory_space=pltpu.SMEM),
            pl.BlockSpec(memory_space=pltpu.VMEM),
        ],
        out_specs=pl.BlockSpec(memory_space=pltpu.VMEM),
        name="join_places",
        **vmem_params(moved=3 * slots * BLOCK * cols),
    )(lists_flat, my_index, back)


def lane_parts(total):
    width = 256 if total % 256 == 0 else LANES
    return [slice(at, at + width) for at in range(0, total, width)]


def pick_entry(stacked, entry):
    entries = stacked.shape[0] // LANES
    chosen = stacked[:LANES]
    for number in range(1, entries):
        chosen = jnp.where(
            entry == number, stacked[number * LANES : (number + 1) * LANES], chosen
        )
    return chosen


def spread_entry(chosen, entry, entries):
    return jnp.concatenate(
        [jnp.where(entry == number, chosen, 0.0) for number in range(entries)], axis=0
    ).astype(BF16)


NT = (((1,), (1,)), ((), ()))
NN = (((1,), (0,)), ((), ()))
TN = (((0,), (0,)), ((), ()))


def local_softmax(query_rows, keys, entry_lanes):
    rows, cols = query_rows.shape
    heads = cols // HEAD
    key_rows = keys.shape[0]
    scale = 1.0 / math.sqrt(HEAD)

    def body(query_ref, key_ref, entry_ref, weight_ref, lse_ref):
        head = pl.program_id(0)
        for part in lane_parts(rows):
            entry = entry_ref[:, part]
            scores = lax.dot_general(
                key_ref[...], query_ref[part, :], NT, preferred_element_type=F32
            )
            scores = pick_entry(scores, entry) * scale
            top = jnp.max(scores, axis=0, keepdims=True)
            raised = jnp.exp(scores - top)
            total = jnp.sum(raised, axis=0, keepdims=True)
            weight_ref[0, :, part] = raised / total
            lse_ref[pl.ds(head, 1), part] = top + jnp.log(total)

    return pl.pallas_call(
        body,
        grid=(heads,),
        out_shape=(
            jax.ShapeDtypeStruct((heads, LANES, rows), F32),
            jax.ShapeDtypeStruct((heads, rows), F32),
        ),
        in_specs=[
            pl.BlockSpec((rows, HEAD), lambda h: (0, h)),
            pl.BlockSpec((key_rows, HEAD), lambda h: (0, h)),
            pl.BlockSpec((1, rows), lambda h: (0, 0)),
        ],
        out_specs=(
            pl.BlockSpec((1, LANES, rows), lambda h: (h, 0, 0)),
            pl.BlockSpec((heads, rows), lambda h: (0, 0)),
        ),
        name="local_softmax",
        **vmem_params(2 * rows * key_rows * cols, 6 * heads * LANES * rows),
    )(query_rows, keys, entry_lanes)


def partner_lanes(partner_ref, all_ref, out_ref, slots):
    heads = out_ref.shape[0]
    lane = lax.broadcasted_iota(jnp.int32, (heads, LANES), 1)
    for group in range(slots // 2):
        halves = []
        for half in range(2):
            slot = group * 2 + half
            device, there = partner_ref[0, slot], partner_ref[1, slot]
            start = pl.multiple_of(there // 2 * LANES, LANES)
            tile = all_ref[device, :, pl.ds(start, LANES)]
            turned = pltpu.roll(tile, BLOCK, 1)
            halves.append(jnp.where(there % 2 == half, tile, turned))
        out_ref[:, group * LANES : (group + 1) * LANES] = jnp.where(
            lane < BLOCK, halves[0], halves[1]
        )


def weight_grads(
    chunk, weights, lse, all_lse, partner, live_lanes, grad_rows, values, entry_lanes
):
    heads, _, rows = weights.shape
    here = grad_rows.shape[1] // HEAD
    first = chunk * here
    value_rows = values.shape[0]
    slots = rows // BLOCK
    devices = all_lse.shape[0]

    def body(
        partner_ref,
        weight_ref,
        lse_ref,
        all_ref,
        live_ref,
        grad_ref,
        value_ref,
        entry_ref,
        slope_ref,
        share_ref,
        dot_ref,
        other_ref,
    ):
        head = pl.program_id(0)

        @pl.when(head == 0)
        def _():
            partner_lanes(partner_ref, all_ref, other_ref, slots)

        for part in lane_parts(rows):
            entry = entry_ref[:, part]
            own = lse_ref[pl.ds(first + head, 1), part]
            other = other_ref[pl.ds(first + head, 1), part]
            odds = jnp.where(live_ref[1:2, part] > 0.0, jnp.exp(other - own), 0.0)
            share = jnp.where(live_ref[0:1, part] > 0.0, 1.0 / (1.0 + odds), 0.0)
            slope = lax.dot_general(
                value_ref[...], grad_ref[part, :], NT, preferred_element_type=F32
            )
            slope = pick_entry(slope, entry)
            low = (weight_ref[0, :, part] * share).astype(BF16).astype(F32)
            slope_ref[0, :, part] = slope
            share_ref[pl.ds(head, 1), part] = share
            dot_ref[pl.ds(head, 1), part] = jnp.sum(low * slope, axis=0, keepdims=True)

    return pl.pallas_call(
        body,
        grid=(here,),
        out_shape=(
            jax.ShapeDtypeStruct((here, LANES, rows), F32),
            jax.ShapeDtypeStruct((here, rows), F32),
            jax.ShapeDtypeStruct((here, rows), F32),
        ),
        in_specs=[
            pl.BlockSpec(memory_space=pltpu.SMEM),
            pl.BlockSpec((1, LANES, rows), lambda h: (first + h, 0, 0)),
            pl.BlockSpec((heads, rows), lambda h: (0, 0)),
            pl.BlockSpec((devices, heads, rows), lambda h: (0, 0, 0)),
            pl.BlockSpec((2, rows), lambda h: (0, 0)),
            pl.BlockSpec((rows, HEAD), lambda h: (0, h)),
            pl.BlockSpec((value_rows, HEAD), lambda h: (0, first + h)),
            pl.BlockSpec((1, rows), lambda h: (0, 0)),
        ],
        out_specs=(
            pl.BlockSpec((1, LANES, rows), lambda h: (h, 0, 0)),
            pl.BlockSpec((here, rows), lambda h: (0, 0)),
            pl.BlockSpec((here, rows), lambda h: (0, 0)),
        ),
        scratch_shapes=[pltpu.VMEM((heads, rows), F32)],
        name="weight_grads",
        **vmem_params(2 * rows * value_rows * here * HEAD, 10 * here * LANES * rows),
    )(partner, weights, lse, all_lse, live_lanes, grad_rows, values, entry_lanes)


def score_grads(chunk, weights, share, slope, dots, all_dots, partner, keys, entry_lanes):
    _, _, rows = weights.shape
    here = slope.shape[0]
    first = chunk * here
    key_rows = keys.shape[0]
    slots = rows // BLOCK
    devices = all_dots.shape[0]
    scale = 1.0 / math.sqrt(HEAD)

    def body(
        partner_ref,
        weight_ref,
        share_ref,
        slope_ref,
        dot_ref,
        all_ref,
        key_ref,
        entry_ref,
        low_ref,
        query_ref,
        other_ref,
    ):
        head = pl.program_id(0)

        @pl.when(head == 0)
        def _():
            partner_lanes(partner_ref, all_ref, other_ref, slots)

        for part in lane_parts(rows):
            entry = entry_ref[:, part]
            dot = dot_ref[pl.ds(head, 1), part] + other_ref[pl.ds(head, 1), part]
            joint = weight_ref[0, :, part] * share_ref[pl.ds(head, 1), part]
            low = joint * (slope_ref[0, :, part] - dot)
            low_ref[0, :, part] = low.astype(BF16)
            wide = spread_entry(low, entry, key_rows // LANES)
            query = lax.dot_general(wide, key_ref[...], TN, preferred_element_type=F32)
            query_ref[part, :] = (query * scale).astype(BF16)

    return pl.pallas_call(
        body,
        grid=(here,),
        out_shape=(
            jax.ShapeDtypeStruct((here, LANES, rows), BF16),
            jax.ShapeDtypeStruct((rows, here * HEAD), BF16),
        ),
        in_specs=[
            pl.BlockSpec(memory_space=pltpu.SMEM),
            pl.BlockSpec((1, LANES, rows), lambda h: (first + h, 0, 0)),
            pl.BlockSpec((here, rows), lambda h: (0, 0)),
            pl.BlockSpec((1, LANES, rows), lambda h: (h, 0, 0)),
            pl.BlockSpec((here, rows), lambda h: (0, 0)),
            pl.BlockSpec((devices, here, rows), lambda h: (0, 0, 0)),
            pl.BlockSpec((key_rows, HEAD), lambda h: (0, first + h)),
            pl.BlockSpec((1, rows), lambda h: (0, 0)),
        ],
        out_specs=(
            pl.BlockSpec((1, LANES, rows), lambda h: (h, 0, 0)),
            pl.BlockSpec((rows, HEAD), lambda h: (0, h)),
        ),
        scratch_shapes=[pltpu.VMEM((here, rows), F32)],
        name="score_grads",
        **vmem_params(2 * rows * key_rows * here * HEAD, 12 * here * LANES * rows),
    )(partner, weights, share, slope, dots, all_dots, keys, entry_lanes)


def entry_grads(chunk, weights, share, low, query_rows, grad_rows, entry_lanes, entry_rows):
    _, _, rows = weights.shape
    here = low.shape[0]
    first = chunk * here
    scale = 1.0 / math.sqrt(HEAD)

    def body(weight_ref, share_ref, low_ref, query_ref, grad_ref, entry_ref, key_ref, value_ref):
        head = pl.program_id(0)
        key_sum = jnp.zeros((entry_rows, HEAD), F32)
        value_sum = jnp.zeros((entry_rows, HEAD), F32)
        for part in lane_parts(rows):
            entry = entry_ref[:, part]
            joint = weight_ref[0, :, part] * share_ref[pl.ds(head, 1), part]
            wide = spread_entry(joint, entry, entry_rows // LANES)
            value_sum += lax.dot_general(wide, grad_ref[part, :], NN, preferred_element_type=F32)
            wide = spread_entry(low_ref[0, :, part].astype(F32), entry, entry_rows // LANES)
            key_sum += lax.dot_general(wide, query_ref[part, :], NN, preferred_element_type=F32)
        key_ref[...] = (key_sum * scale).astype(BF16)
        value_ref[...] = value_sum.astype(BF16)

    return pl.pallas_call(
        body,
        grid=(here,),
        out_shape=(
            jax.ShapeDtypeStruct((entry_rows, here * HEAD), BF16),
            jax.ShapeDtypeStruct((entry_rows, here * HEAD), BF16),
        ),
        in_specs=[
            pl.BlockSpec((1, LANES, rows), lambda h: (first + h, 0, 0)),
            pl.BlockSpec((here, rows), lambda h: (0, 0)),
            pl.BlockSpec((1, LANES, rows), lambda h: (h, 0, 0)),
            pl.BlockSpec((rows, HEAD), lambda h: (0, first + h)),
            pl.BlockSpec((rows, HEAD), lambda h: (0, h)),
            pl.BlockSpec((1, rows), lambda h: (0, 0)),
        ],
        out_specs=(
            pl.BlockSpec((entry_rows, HEAD), lambda h: (0, h)),
            pl.BlockSpec((entry_rows, HEAD), lambda h: (0, h)),
        ),
        name="entry_grads",
        **vmem_params(4 * rows * entry_rows * here * HEAD, 8 * here * LANES * rows),
    )(weights, share, low, query_rows, grad_rows, entry_lanes)


def swap(value, axis, bits):
    size = lax.axis_size(axis)
    return lax.ppermute(value, axis, [(i, i ^ bits) for i in range(size)])


def cube_gather(value, axis):
    value, bits = value[None], 1
    while bits < lax.axis_size(axis):
        value = jnp.concatenate([value, swap(value, axis, bits)], axis=0)
        bits *= 2
    return value


def rank_slots(owners):
    slot_total = owners.shape[-1]
    earlier_mask = jnp.arange(slot_total)[None, :] < jnp.arange(slot_total)[:, None]
    same_owner = owners[..., :, None] == owners[..., None, :]
    return jnp.sum(same_owner & earlier_mask, axis=-1)


def owner_tables(all_lists, counts_all, my_index, entries_here, slot_cap):
    n_seq, places = all_lists.shape
    owners = all_lists // entries_here
    ranks = rank_slots(owners)
    chosen = (owners == my_index)[:, None, :] & (
        ranks[:, None, :] == jnp.arange(slot_cap)[None, :, None]
    )
    place = jnp.arange(places)

    def look(table):
        return jnp.sum(jnp.where(chosen, table[:, None, :], 0), axis=2).reshape(-1)

    def other(table):
        return table.reshape(n_seq, -1, NEIGH)[:, :, ::-1].reshape(n_seq, places)

    entry = look(all_lists % entries_here)
    device = look(other(owners) ^ my_index)
    there = look(other(ranks) + slot_cap * jnp.arange(n_seq)[:, None])
    per_place = jnp.repeat(counts_all.reshape(n_seq, -1), NEIGH, axis=1)
    own_live = look((place % NEIGH < per_place).astype(jnp.int32))
    other_live = look((NEIGH - 1 - place % NEIGH < per_place).astype(jnp.int32))
    live = jnp.stack([own_live, other_live]).astype(F32)
    lanes = functools.partial(jnp.repeat, repeats=BLOCK, axis=-1)
    return (
        lanes(entry[None]).astype(jnp.int32),
        jnp.stack([device, there]).astype(jnp.int32),
        lanes(live),
    )


def on_device(out_grad, out_weight, queries, keys, values, retrieval, counts):
    n_seq, n_mp = lax.axis_size("seq"), lax.axis_size("mp")
    my_index, my_mp = lax.axis_index("seq"), lax.axis_index("mp")
    tok_rows, head_cols = queries.shape
    entries_here, nbr_rows, _ = keys.shape
    blocks_here = tok_rows // BLOCK
    places = blocks_here * NEIGH
    slot_cap = (places + n_seq - 1) // n_seq
    rows = n_seq * slot_cap * BLOCK
    feats = out_grad.shape[1]
    chunk_cols = head_cols // HEAD_CHUNKS
    lists_flat = retrieval.reshape(-1).astype(jnp.int32)
    index_arr = my_index.astype(jnp.int32).reshape(1)
    key_rows = keys.reshape(entries_here * nbr_rows, head_cols)
    value_rows = values.reshape(entries_here * nbr_rows, head_cols)

    def exchange(slot_rows):
        cols = slot_rows.shape[-1]
        return lax.all_to_all(
            slot_rows.reshape(n_seq, slot_cap * BLOCK, cols), "seq", 0, 0, tiled=True
        ).reshape(rows, cols)

    def to_owners(token_rows):
        return exchange(
            place_rows(token_rows, lists_flat, index_arr, n_seq, slot_cap, entries_here)
        )

    query_slots = to_owners(queries)
    counts_all = lax.all_gather(counts, "seq", axis=0, tiled=True)
    entry_lanes, partner, live_lanes = owner_tables(
        retrieval.reshape(n_seq, places), counts_all, my_index, entries_here, slot_cap
    )

    def product(part, source, at):
        weight = lax.dynamic_slice_in_dim(
            out_weight, source * feats + at, part.shape[1], axis=1
        )
        return lax.dot_general(part, weight, NT, preferred_element_type=F32)

    steps = 2
    width = feats // steps
    arrived = []
    for bits in range(2, n_mp, 2):
        for step in range(steps):
            piece = swap(out_grad[:, step * width : (step + 1) * width], "mp", bits)
            arrived.append((piece, my_mp ^ bits, step * width))
            arrived.append((swap(piece, "mp", 1), my_mp ^ bits ^ 1, step * width))
    grad_sum = product(out_grad, my_mp, 0) + product(swap(out_grad, "mp", 1), my_mp ^ 1, 0)
    for piece, source, at in arrived:
        grad_sum = grad_sum + product(piece, source, at)
    grad_out = grad_sum.astype(BF16)

    weights, lse = local_softmax(query_slots, key_rows, entry_lanes)
    all_lse = cube_gather(lse, "seq")

    query_parts, key_parts, value_parts = [], [], []
    for chunk in range(HEAD_CHUNKS):
        grad_slots = to_owners(grad_out[:, chunk * chunk_cols : (chunk + 1) * chunk_cols])
        slope, share, dots = weight_grads(
            chunk, weights, lse, all_lse, partner, live_lanes, grad_slots, value_rows, entry_lanes
        )
        low, query_terms = score_grads(
            chunk,
            weights,
            share,
            slope,
            dots,
            cube_gather(dots, "seq"),
            partner,
            key_rows,
            entry_lanes,
        )
        back = exchange(query_terms).reshape(-1, BLOCK, chunk_cols)
        query_parts.append(
            join_places(
                back, lists_flat, index_arr, n_seq, slot_cap, entries_here, blocks_here
            )
        )
        key_part, value_part = entry_grads(
            chunk, weights, share, low, query_slots, grad_slots, entry_lanes, key_rows.shape[0]
        )
        key_parts.append(key_part)
        value_parts.append(value_part)
    query_grad = jnp.concatenate(query_parts, axis=1)
    key_grad = jnp.concatenate(key_parts, axis=1).reshape(keys.shape)
    value_grad = jnp.concatenate(value_parts, axis=1).reshape(values.shape)
    return (query_grad, key_grad, value_grad)


def solution(mesh):
    return jax.shard_map(
        on_device,
        mesh=mesh,
        in_specs=(
            P("seq", "mp"),
            P("mp", None),
            P("seq", "mp"),
            P("seq", None, "mp"),
            P("seq", None, "mp"),
            P(),
            P("seq"),
        ),
        out_specs=(P("seq", "mp"), P("seq", None, "mp"), P("seq", None, "mp")),
        check_vma=False,
    )
```

time: 476 us -> 235 us (0.49)
  waiting for transfers between devices: 323 us -> 77.5 us
  local copies, waits for them, and re-layouts: 85.2 us -> 19.7 us
  Pallas kernels: 0 us -> 41.2 us
  starting transfers between devices: 10.4 us -> 46.2 us
  blocking collectives: 0 us -> 25 us
  between operations: 14 us -> 1.76 us
  matrix products: 30.2 us -> 18.1 us
  other arithmetic: 11.7 us -> 4.59 us
    all_gather x3 -> x0, waiting for transfers between devices: 182 us -> none  [the longest x1 74.1 us: on_device(): lax.all_gather(values, 'seq', axis=0, tiled=True)]
    all_to_all x2 -> x5, waiting for transfers between devices: 139 us -> 11.2 us  [exchange(): lax.all_to_all(slot_rows.reshape(n_seq, slot_cap * BLOCK, cols), 'seq', 0...]
    ppermute x0 -> x14, waiting for transfers between devices: none -> 66.3 us  [swap(): return lax.ppermute(value, axis, [(i, i ^ bits) for i in range(size)])]
    pallas_call x0 -> x12, Pallas kernels: none -> 41.2 us  [the longest x3 9.97 us: place_rows(): pl.pallas_call(body, out_shape=jax.ShapeDtypeStruct((slots, BLOCK, cols),...]
    unnamed x0 -> x1, blocking collectives: none -> 25 us
    scatter x2 -> x0, local copies, waits for them, and re-layouts: 22 us -> none  [the longest x1 11 us: on_device(): value_back = jnp.zeros((seq_count * slot_cap, nbr_rows, head_cols), jnp.b...]
    ppermute x0 -> x14, starting transfers between devices: none -> 21.4 us  [swap(): return lax.ppermute(value, axis, [(i, i ^ bits) for i in range(size)])]
    reshape x4 -> x6, local copies, waits for them, and re-layouts: 15.9 us -> 0.52 us  [the longest x2 0.15 us: owner_tables(): per_place = jnp.repeat(counts_all.reshape(n_seq, -1), NEIGH, axis=1)]
  transfers between devices with their start and end apart: 5 -> 19, of which waited for: 5 -> 12; matrix products, arithmetic and copies ran while one was open for 15% -> 11% of each run, Pallas kernels for 0% -> 17%
where the time goes in v1:
time: 235 us; the launch traced here: 234 us
  waiting for transfers between devices  77.5 us (33%)
  starting transfers between devices  46.2 us (20%)
  Pallas kernels  41.2 us (18%)
  blocking collectives  25 us (11%)
  local copies, waits for them, and re-layouts  19.7 us (8%)
  matrix products  18.1 us (8%)
  other arithmetic  4.59 us (2%)
    ppermute x14, waiting for transfers between devices, swap(): return lax.ppermute(value, axis, [(i, i ^ bits) for i in range(size)])  66.3 us
    unnamed x1, blocking collectives  25 us
    all_to_all x5, starting transfers between devices, exchange(): lax.all_to_all(slot_rows.reshape(n_seq, slot_cap * BLOCK, cols), 'seq', 0...  24.8 us
    ppermute x14, starting transfers between devices, swap(): return lax.ppermute(value, axis, [(i, i ^ bits) for i in range(size)])  21.4 us
    dot_general x6, matrix products, product(): return lax.dot_general(part, weight, NT, preferred_element_type=F32)  18.1 us
    unnamed x48, local copies, waits for them, and re-layouts  13.7 us
    all_to_all x5, waiting for transfers between devices, exchange(): lax.all_to_all(slot_rows.reshape(n_seq, slot_cap * BLOCK, cols), 'seq', 0...  11.2 us
    pallas_call x3, Pallas kernels, place_rows(): pl.pallas_call(body, out_shape=jax.ShapeDtypeStruct((slots, BLOCK, cols),...  9.97 us
  transfers between devices with their start and end apart: 19, of which 12 were waited for; matrix products, arithmetic and copies ran while one was open for 11% of the time, Pallas kernels for 17%

profile of v1, /device:TPU:0, one launch (start us, length us, event | category | flops | bytes accessed | tf_op | source)
XLA Modules:
  0.0 234.0 jit_solution(7250626054423296447)
XLA Ops:
  0.7 3.1 %fusion.28 = (bf16[512,1024]{1,0:T(8,128)(2,1)}, bf16[512,1024]{1,0:T(8,128)(2,1)}) fusion(bf16[512,2048]{1,0:T(8,128)(2,1)} %param.7), kind=kLoop, calls=%fused_computation.66 | loop fusion | bytes 4194304 | tf_op jit(solution)/shard_map/slice | solution.py:469
  3.8 2.9 %collective-permute-start.4 = (bf16[512,1024]{1,0:T(8,128)(2,1)}, bf16[512,1024]{1,0:T(8,128)(2,1)}, u32[]{:S(2)}, u32[]{:S(2)}) collective-permute-start(bf16[512,1024]{1,0:T(8,128)(2,1)} %get-tuple-element.42), channel_id=1, source_target_pairs={{0,2},{1,3},{2,0},{3,1},{4,6},{5,7},{6,4},{7,5},{8,10},{9,11},{10,... | collective-permute-start | bytes 3145736 | tf_op jit(solution)/shard_map/ppermute | solution.py:377
  7.0 4.2 %place_rows.3 = bf16[16,64,1024]{2,1,0:T(8,128)(2,1)S(1)} custom-call(s32[128]{0:T(128)S(1)} %reshape.251.lists_ref, s32[1]{0:T(128)} %bitcast.index_ref, bf16[512,1024]{1,0:T(8,128)(2,1)S(1)} %copy-done.9), custom_call_target="tpu_custom_call" | custom-call | bytes 4194304 | tf_op jit(solution)/shard_map/place_rows/pallas_call | solution.py:61
  11.2 1.4 copy-done
  12.6 6.0 %all-to-all-start = ((bf16[8,128,1024]{2,1,0:T(8,128)(2,1)}), bf16[8,128,1024]{2,1,0:T(8,128)(2,1)S(1)}, u32[]{:S(2)}, u32[]{:S(2)}) async-start(bf16[8,128,1024]{2,1,0:T(8,128)(2,1)} %bitcast.38), calls=%async_computation | async-start | bytes 4194304 | tf_op jit(solution)/shard_map/all_to_all | solution.py:443
  18.6 0.6 collective-permute-start.6
  19.2 11.9 %collective-permute-done.4 = bf16[512,1024]{1,0:T(8,128)(2,1)} collective-permute-done((bf16[512,1024]{1,0:T(8,128)(2,1)}, bf16[512,1024]{1,0:T(8,128)(2,1)}, u32[]{:S(2)}, u32[]{:S(2)}) %collective-permute-start.4) | collective-permute-done | bytes 1048608 | tf_op jit(solution)/shard_map/ppermute | solution.py:377
  31.0 5.4 %fusion.2 = f32[1024,512]{0,1:T(8,128)S(1)} fusion(bf16[512,2048]{1,0:T(8,128)(2,1)} %param.7, bf16[1024,8192]{1,0:T(8,128)(2,1)} %param.8, s32[]{:T(128)S(6)} %select_n.90), kind=kOutput, calls=%fused_computation.2 | convolution fusion | flops 2147483648 | bytes 8388612 | tf_op jit(solution)/shard_map/dot_general | solution.py:462
  36.4 16.3 %collective-permute-done.6 = bf16[512,1024]{1,0:T(8,128)(2,1)} collective-permute-done((bf16[512,1024]{1,0:T(8,128)(2,1)S(1)}, bf16[512,1024]{1,0:T(8,128)(2,1)}, u32[]{:S(2)}, u32[]{:S(2)}) %collective-permute-start.6) | collective-permute-done | bytes 1048608 | tf_op jit(solution)/shard_map/ppermute | solution.py:377
  52.7 3.1 %fusion.6 = f32[1024,512]{0,1:T(8,128)S(1)} fusion(bf16[512,1024]{1,0:T(8,128)(2,1)} %collective-permute-done.6, bf16[1024,8192]{1,0:T(8,128)(2,1)} %param.8, s32[]{:T(128)S(6)} %select_n.94), kind=kOutput, calls=%fused_computation.7 | convolution fusion | flops 1073741824 | bytes 5242884 | tf_op jit(solution)/shard_map/dot_general | solution.py:462
  55.8 2.6 %fusion.10 = f32[1024,512]{0,1:T(8,128)S(1)} fusion(bf16[512,1024]{1,0:T(8,128)(2,1)} %collective-permute-done.4, bf16[1024,8192]{1,0:T(8,128)(2,1)S(1)} %copy-done.17, s32[]{:T(128)S(6)} %select_n.92), kind=kOutput, calls=%fused_computation.11 | convolution fusion | flops 1073741824 | bytes 5242884 | tf_op jit(solution)/shard_map/dot_general | solution.py:462
  58.4 1.3 fusion.8
  59.7 4.1 %fusion = f32[1024,512]{0,1:T(8,128)S(1)} fusion(bf16[512,2048]{1,0:T(8,128)(2,1)} %collective-permute-done.3, bf16[1024,8192]{1,0:T(8,128)(2,1)S(1)} %copy-done.17, s32[]{:T(128)S(6)} %select_n.91), kind=kOutput, calls=%fused_computation | convolution fusion | flops 2147483648 | bytes 8388612 | tf_op jit(solution)/shard_map/dot_general | solution.py:462
  63.8 1.6 fusion.14
  65.5 0.9 fusion.29
  66.3 2.9 %place_rows.5 = bf16[16,64,512]{2,1,0:T(8,128)(2,1)S(1)} custom-call(s32[128]{0:T(128)S(1)} %reshape.251.lists_ref, s32[1]{0:T(128)} %bitcast.index_ref, bf16[512,512]{1,0:T(8,128)(2,1)S(1)} %get-tuple-element.45.rows_ref), custom_call_target="tpu_custom_call" | custom-call | bytes 2097152 | tf_op jit(solution)/shard_map/place_rows/pallas_call | solution.py:61
  69.2 1.0 copy-done.5
  70.2 6.1 %all-to-all-start.3 = ((bf16[8,128,512]{2,1,0:T(8,128)(2,1)}), bf16[8,128,512]{2,1,0:T(8,128)(2,1)S(1)}, u32[]{:S(2)}, u32[]{:S(2)}) async-start(bf16[8,128,512]{2,1,0:T(8,128)(2,1)} %bitcast.43), calls=%async_computation.3 | async-start | bytes 2097152 | tf_op jit(solution)/shard_map/all_to_all | solution.py:443
  76.4 0.6 dynamic-slice
  77.9 25.0 %all-reduce = s32[64]{0:T(128)S(1)} all-reduce(s32[64]{0:T(128)S(1)} %dynamic-update-slice), channel_id=1, replica_groups=mesh['seq'=8,'mp'=4] {'seq'}, use_global_device_ids=true, to_apply=%add | all-reduce | flops 64 | bytes 512
  103.1 0.3 convert_reduce_fusion
  103.5 1.0 copy-done.8
  104.5 2.9 %place_rows.4 = bf16[16,64,512]{2,1,0:T(8,128)(2,1)S(1)} custom-call(s32[128]{0:T(128)S(1)} %reshape.251.lists_ref, s32[1]{0:T(128)} %bitcast.index_ref, bf16[512,512]{1,0:T(8,128)(2,1)S(1)} %copy-done.8), custom_call_target="tpu_custom_call" | custom-call | bytes 2097152 | tf_op jit(solution)/shard_map/place_rows/pallas_call | solution.py:61
  107.4 1.0 copy-done.4
  108.4 4.2 %all-to-all-start.1 = ((bf16[8,128,512]{2,1,0:T(8,128)(2,1)}), bf16[8,128,512]{2,1,0:T(8,128)(2,1)}, u32[]{:S(2)}, u32[]{:S(2)}) async-start(bf16[8,128,512]{2,1,0:T(8,128)(2,1)} %bitcast.42), calls=%async_computation.1 | async-start | bytes 2097152 | tf_op jit(solution)/shard_map/all_to_all | solution.py:443
  113.7 1.1 copy-done.1
  114.8 5.8 %local_softmax.1 = (f32[8,128,1024]{2,1,0:T(8,128)}, f32[8,1024]{1,0:T(8,128)S(1)}) custom-call(bf16[1024,1024]{1,0:T(8,128)(2,1)S(1)} %bitcast.33, bf16[256,1024]{1,0:T(8,128)(2,1)S(1)} %bitcast.39, s32[1,1024]{1,0:T(1,128)S(1)} %broadcast_in_dim.77.entry_ref), custom_call_target="tpu_custom_call" | custom-call | flops 536870912 | bytes 6291456 | tf_op jit(solution)/shard_map/local_softmax/pallas_call | solution.py:154
  120.6 1.9 collective-permute-start
  122.5 2.7 %collective-permute-done = f32[1,8,1024]{2,1,0:T(8,128)S(1)} collective-permute-done((f32[1,8,1024]{2,1,0:T(8,128)S(1)}, f32[1,8,1024]{2,1,0:T(8,128)S(1)}, u32[]{:S(2)}, u32[]{:S(2)}) %collective-permute-start) | collective-permute-done | bytes 32800 | tf_op jit(solution)/shard_map/ppermute | solution.py:377
  125.2 1.8 collective-permute-start.1
  127.3 3.5 %collective-permute-done.1 = f32[2,8,1024]{2,1,0:T(8,128)S(1)} collective-permute-done((f32[2,8,1024]{2,1,0:T(8,128)S(1)}, f32[2,8,1024]{2,1,0:T(8,128)S(1)}, u32[]{:S(2)}, u32[]{:S(2)}) %collective-permute-start.1) | collective-permute-done | bytes 65568 | tf_op jit(solution)/shard_map/ppermute | solution.py:377
  130.9 6.3 %collective-permute-start.2 = (f32[4,8,1024]{2,1,0:T(8,128)S(1)}, f32[4,8,1024]{2,1,0:T(8,128)}, u32[]{:S(2)}, u32[]{:S(2)}) collective-permute-start(f32[4,8,1024]{2,1,0:T(8,128)S(1)} %pad_maximum_fusion.4), channel_id=1, source_target_pairs={{0,16},{4,20},{8,24},{12,28},{16,0},{20,4},{24,8},{28,12},{1,17},{... | collective-permute-start | bytes 393224 | tf_op jit(solution)/shard_map/ppermute | solution.py:377
  137.7 6.3 %collective-permute-done.2 = f32[4,8,1024]{2,1,0:T(8,128)} collective-permute-done((f32[4,8,1024]{2,1,0:T(8,128)S(1)}, f32[4,8,1024]{2,1,0:T(8,128)}, u32[]{:S(2)}, u32[]{:S(2)}) %collective-permute-start.2) | collective-permute-done | bytes 131104 | tf_op jit(solution)/shard_map/ppermute | solution.py:377
  143.9 0.9 pad_maximum_fusion.3.all_ref
  144.9 1.0 copy-done.6
  145.9 3.5 %weight_grads.3 = (f32[4,128,1024]{2,1,0:T(8,128)S(1)}, f32[4,1024]{1,0:T(4,128)S(1)}, f32[4,1024]{1,0:T(4,128)S(1)}) custom-call(s32[2,16]{1,0:T(2,128)S(1)} %pad_add_fusion.partner_ref, f32[8,128,1024]{2,1,0:T(8,128)} %get-tuple-element.19.weight_ref, f32[8,1024]{1,0:T(8,128)S(1)} %get-tuple-element.20.lse_ref, ...), custom_call_target="tpu_custom_call" | custom-call | flops 268435456 | bytes 5242880 | tf_op jit(solution)/shard_map/weight_grads/pallas_call | solution.py:237
  149.4 1.4 collective-permute-start.11
  150.9 2.4 %collective-permute-done.11 = f32[1,4,1024]{2,1,0:T(4,128)S(1)} collective-permute-done((f32[1,4,1024]{2,1,0:T(4,128)S(1)}, f32[1,4,1024]{2,1,0:T(4,128)S(1)}, u32[]{:S(2)}, u32[]{:S(2)}) %collective-permute-start.11) | collective-permute-done | bytes 16416 | tf_op jit(solution)/shard_map/ppermute | solution.py:377
  153.3 3.9 %collective-permute-done.12 = f32[2,4,1024]{2,1,0:T(4,128)S(1)} collective-permute-done((f32[2,4,1024]{2,1,0:T(4,128)S(1)}, f32[2,4,1024]{2,1,0:T(4,128)S(1)}, u32[]{:S(2)}, u32[]{:S(2)}) %collective-permute-start.12) | collective-permute-done | bytes 32800 | tf_op jit(solution)/shard_map/ppermute | solution.py:377
  157.3 5.3 %collective-permute-done.13 = f32[4,4,1024]{2,1,0:T(4,128)S(1)} collective-permute-done((f32[4,4,1024]{2,1,0:T(4,128)S(1)}, f32[4,4,1024]{2,1,0:T(4,128)S(1)}, u32[]{:S(2)}, u32[]{:S(2)}) %collective-permute-start.13) | collective-permute-done | bytes 65568 | tf_op jit(solution)/shard_map/ppermute | solution.py:377
  162.7 3.7 %score_grads.3 = (bf16[4,128,1024]{2,1,0:T(8,128)(2,1)S(1)}, bf16[1024,512]{1,0:T(8,128)(2,1)S(1)}) custom-call(s32[2,16]{1,0:T(2,128)S(1)} %pad_add_fusion.partner_ref, f32[8,128,1024]{2,1,0:T(8,128)} %get-tuple-element.19.weight_ref, f32[4,1024]{1,0:T(4,128)S(1)} %get-tuple-element.25.share_ref, f32[4,128,1024]{2,1,0:T(8,128)S(1)} %get-tuple-element.26.slope_ref, ...), custom_call_target="tpu_custom_call" | custom-call | flops 268435456 | bytes 6291456 | tf_op jit(solution)/shard_map/score_grads/pallas_call | solution.py:304
  166.4 1.0 copy-done.10
  167.3 1.0 copy-done.12
  168.4 4.2 %all-to-all-start.4 = ((bf16[8,128,512]{2,1,0:T(8,128)(2,1)}), bf16[8,128,512]{2,1,0:T(8,128)(2,1)}, u32[]{:S(2)}, u32[]{:S(2)}) async-start(bf16[8,128,512]{2,1,0:T(8,128)(2,1)} %bitcast.46), calls=%async_computation.4 | async-start | bytes 2097152 | tf_op jit(solution)/shard_map/all_to_all | solution.py:443
  172.6 1.0 copy-done.7
  173.7 3.6 %weight_grads.2 = (f32[4,128,1024]{2,1,0:T(8,128)S(1)}, f32[4,1024]{1,0:T(4,128)S(1)}, f32[4,1024]{1,0:T(4,128)S(1)}) custom-call(s32[2,16]{1,0:T(2,128)S(1)} %pad_add_fusion.partner_ref, f32[8,128,1024]{2,1,0:T(8,128)} %get-tuple-element.19.weight_ref, f32[8,1024]{1,0:T(8,128)S(1)} %get-tuple-element.20.lse_ref, ...), custom_call_target="tpu_custom_call" | custom-call | flops 268435456 | bytes 5242880 | tf_op jit(solution)/shard_map/weight_grads/pallas_call | solution.py:237
  177.3 2.0 collective-permute-start.8
  179.2 3.7 %collective-permute-done.8 = f32[1,4,1024]{2,1,0:T(4,128)S(1)} collective-permute-done((f32[1,4,1024]{2,1,0:T(4,128)S(1)}, f32[1,4,1024]{2,1,0:T(4,128)S(1)}, u32[]{:S(2)}, u32[]{:S(2)}) %collective-permute-start.8) | collective-permute-done | bytes 16416 | tf_op jit(solution)/shard_map/ppermute | solution.py:377
  183.1 5.0 %collective-permute-done.9 = f32[2,4,1024]{2,1,0:T(4,128)S(1)} collective-permute-done((f32[2,4,1024]{2,1,0:T(4,128)S(1)}, f32[2,4,1024]{2,1,0:T(4,128)S(1)}, u32[]{:S(2)}, u32[]{:S(2)}) %collective-permute-start.9) | collective-permute-done | bytes 32800 | tf_op jit(solution)/shard_map/ppermute | solution.py:377
  188.1 4.1 %collective-permute-start.10 = (f32[4,4,1024]{2,1,0:T(4,128)S(1)}, f32[4,4,1024]{2,1,0:T(4,128)S(1)}, u32[]{:S(2)}, u32[]{:S(2)}) collective-permute-start(f32[4,4,1024]{2,1,0:T(4,128)S(1)} %pad_maximum_fusion.8), channel_id=1, source_target_pairs={{0,16},{4,20},{8,24},{12,28},{16,0},{20,4},{24,8},{28,12},{1,17},{... | collective-permute-start | bytes 196616 | tf_op jit(solution)/shard_map/ppermute | solution.py:377
  192.2 5.5 %collective-permute-done.10 = f32[4,4,1024]{2,1,0:T(4,128)S(1)} collective-permute-done((f32[4,4,1024]{2,1,0:T(4,128)S(1)}, f32[4,4,1024]{2,1,0:T(4,128)S(1)}, u32[]{:S(2)}, u32[]{:S(2)}) %collective-permute-start.10) | collective-permute-done | bytes 65568 | tf_op jit(solution)/shard_map/ppermute | solution.py:377
  197.7 3.7 %score_grads.2 = (bf16[4,128,1024]{2,1,0:T(8,128)(2,1)S(1)}, bf16[1024,512]{1,0:T(8,128)(2,1)S(1)}) custom-call(s32[2,16]{1,0:T(2,128)S(1)} %pad_add_fusion.partner_ref, f32[8,128,1024]{2,1,0:T(8,128)} %get-tuple-element.19.weight_ref, f32[4,1024]{1,0:T(4,128)S(1)} %get-tuple-element.21.share_ref, f32[4,128,1024]{2,1,0:T(8,128)S(1)} %get-tuple-element.22.slope_ref, ...), custom_call_target="tpu_custom_call" | custom-call | flops 268435456 | bytes 6291456 | tf_op jit(solution)/shard_map/score_grads/pallas_call | solution.py:304
  201.4 1.1 copy-done.11
  202.5 1.0 copy-done.14
  203.5 4.3 %all-to-all-start.2 = ((bf16[8,128,512]{2,1,0:T(8,128)(2,1)}), bf16[8,128,512]{2,1,0:T(8,128)(2,1)}, u32[]{:S(2)}, u32[]{:S(2)}) async-start(bf16[8,128,512]{2,1,0:T(8,128)(2,1)} %bitcast.47), calls=%async_computation.2 | async-start | bytes 2097152 | tf_op jit(solution)/shard_map/all_to_all | solution.py:443
  207.8 1.2 copy-done.13
  209.0 3.7 %entry_grads.3 = (bf16[256,512]{1,0:T(8,128)(2,1)S(1)}, bf16[256,512]{1,0:T(8,128)(2,1)S(1)}) custom-call(f32[8,128,1024]{2,1,0:T(8,128)} %get-tuple-element.19.weight_ref, f32[4,1024]{1,0:T(4,128)S(1)} %get-tuple-element.25.share_ref, bf16[4,128,1024]{2,1,0:T(8,128)(2,1)S(1)} %copy-done.13, bf16[1024,1024]{1,0:T(8,128)(2,1)S(1)} %bitcast.34, ...), custom_call_target="tpu_custom_call" | custom-call | flops 536870912 | bytes 4194304 | tf_op jit(solution)/shard_map/entry_grads/pallas_call | solution.py:351
  212.7 3.8 %entry_grads.2 = (bf16[256,512]{1,0:T(8,128)(2,1)S(1)}, bf16[256,512]{1,0:T(8,128)(2,1)S(1)}) custom-call(f32[8,128,1024]{2,1,0:T(8,128)} %get-tuple-element.19.weight_ref, f32[4,1024]{1,0:T(4,128)S(1)} %get-tuple-element.21.share_ref, bf16[4,128,1024]{2,1,0:T(8,128)(2,1)S(1)} %copy-done.15, bf16[1024,1024]{1,0:T(8,128)(2,1)S(1)} %bitcast.35, ...), custom_call_target="tpu_custom_call" | custom-call | flops 536870912 | bytes 4194304 | tf_op jit(solution)/shard_map/entry_grads/pallas_call | solution.py:351
  216.5 0.9 pad_maximum_fusion.1
  217.3 0.9 pad_maximum_fusion.2
  218.2 1.7 join_places.3
  219.9 11.2 %all-to-all-done.2 = bf16[8,128,512]{2,1,0:T(8,128)(2,1)} async-done(((bf16[8,128,512]{2,1,0:T(8,128)(2,1)}), bf16[8,128,512]{2,1,0:T(8,128)(2,1)}, u32[]{:S(2)}, u32[]{:S(2)}) %all-to-all-start.2) | async-done | bytes 1048608 | tf_op jit(solution)/shard_map/all_to_all | solution.py:443
  231.1 1.7 join_places.2
  232.8 1.1 pad_maximum_fusion
  (95 shorter events, 3.4 us)
Async XLA Ops:
  0.6 6.1 %copy-start.19 = (s32[64,2]{0,1:T(2,128)S(1)}, s32[64,2]{0,1:T(2,128)}, u32[]{:S(2)}) copy-start(s32[64,2]{0,1:T(2,128)} %param.12) | copy-start | bytes 1540
  0.6 6.3 %copy-start.9 = (bf16[512,1024]{1,0:T(8,128)(2,1)S(1)}, bf16[512,1024]{1,0:T(8,128)(2,1)}, u32[]{:S(2)}) copy-start(bf16[512,1024]{1,0:T(8,128)(2,1)} %rows_ref.1) | copy-start | bytes 3145732
  3.8 27.2 %collective-permute-start.4 = (bf16[512,1024]{1,0:T(8,128)(2,1)}, bf16[512,1024]{1,0:T(8,128)(2,1)}, u32[]{:S(2)}, u32[]{:S(2)}) collective-permute-start(bf16[512,1024]{1,0:T(8,128)(2,1)} %get-tuple-element.42), channel_id=1, source_target_pairs={{0,2},{1,3},{2,0},{3,1},{4,6},{5,7},{6,4},{7,5},{8,10},{9,11},{10,... | collective-permute-start | bytes 3145736 | tf_op jit(solution)/shard_map/ppermute | solution.py:377
  11.2 1.4 copy-start
  12.6 6.0 %copy-start.16 = (bf16[512,1024]{1,0:T(8,128)(2,1)S(1)}, bf16[512,1024]{1,0:T(8,128)(2,1)}, u32[]{:S(2)}) copy-start(bf16[512,1024]{1,0:T(8,128)(2,1)} %get-tuple-element.43) | copy-start | bytes 3145732
  12.6 57.6 %all-to-all-start = ((bf16[8,128,1024]{2,1,0:T(8,128)(2,1)}), bf16[8,128,1024]{2,1,0:T(8,128)(2,1)S(1)}, u32[]{:S(2)}, u32[]{:S(2)}) async-start(bf16[8,128,1024]{2,1,0:T(8,128)(2,1)} %bitcast.38), calls=%async_computation | async-start | bytes 4194304 | tf_op jit(solution)/shard_map/all_to_all | solution.py:443
  18.5 41.2 %collective-permute-start.3 = (bf16[512,2048]{1,0:T(8,128)(2,1)}, bf16[512,2048]{1,0:T(8,128)(2,1)}, u32[]{:S(2)}, u32[]{:S(2)}) collective-permute-start(bf16[512,2048]{1,0:T(8,128)(2,1)} %param.7), channel_id=1, source_target_pairs={{0,1},{1,0},{2,3},{3,2},{4,5},{5,4},{6,7},{7,6},{8,9},{9,8},{10,11... | collective-permute-start | bytes 6291464 | tf_op jit(solution)/shard_map/ppermute | solution.py:377
  18.6 34.1 %collective-permute-start.6 = (bf16[512,1024]{1,0:T(8,128)(2,1)S(1)}, bf16[512,1024]{1,0:T(8,128)(2,1)}, u32[]{:S(2)}, u32[]{:S(2)}) collective-permute-start(bf16[512,1024]{1,0:T(8,128)(2,1)S(1)} %copy-done.16), channel_id=1, source_target_pairs={{0,2},{1,3},{2,0},{3,1},{4,6},{5,7},{6,4},{7,5},{8,10},{9,11},{10,... | collective-permute-start | bytes 3145736 | tf_op jit(solution)/shard_map/ppermute | solution.py:377
  31.0 27.4 %collective-permute-start.5 = (bf16[512,1024]{1,0:T(8,128)(2,1)}, bf16[512,1024]{1,0:T(8,128)(2,1)S(1)}, u32[]{:S(2)}, u32[]{:S(2)}) collective-permute-start(bf16[512,1024]{1,0:T(8,128)(2,1)} %collective-permute-done.4), channel_id=1, source_target_pairs={{0,1},{1,0},{2,3},{3,2},{4,5},{5,4},{6,7},{7,6},{8,9},{9,8},{10,11... | collective-permute-start | bytes 3145736 | tf_op jit(solution)/shard_map/ppermute | solution.py:377
  31.0 24.8 %copy-start.17 = (bf16[1024,8192]{1,0:T(8,128)(2,1)S(1)}, bf16[1024,8192]{1,0:T(8,128)(2,1)}, u32[]{:S(2)}) copy-start(bf16[1024,8192]{1,0:T(8,128)(2,1)} %param.8) | copy-start | bytes 50331652
  52.7 11.2 %collective-permute-start.7 = (bf16[512,1024]{1,0:T(8,128)(2,1)}, bf16[512,1024]{1,0:T(8,128)(2,1)S(1)}, u32[]{:S(2)}, u32[]{:S(2)}) collective-permute-start(bf16[512,1024]{1,0:T(8,128)(2,1)} %collective-permute-done.6), channel_id=1, source_target_pairs={{0,1},{1,0},{2,3},{3,2},{4,5},{5,4},{6,7},{7,6},{8,9},{9,8},{10,11... | collective-permute-start | bytes 3145736 | tf_op jit(solution)/shard_map/ppermute | solution.py:377
  66.3 10.1 %copy-start.21 = (u32[32]{0:T(128)S(1)}, u32[32]{0:T(128)}, u32[]{:S(2)}) copy-start(u32[32]{0:T(128)} %constant.64) | copy-start | bytes 388
  66.3 11.4 %copy-start.20 = (s32[8]{0:T(128)S(1)}, s32[8]{0:T(128)}, u32[]{:S(2)}) copy-start(s32[8]{0:T(128)} %param.13) | copy-start | bytes 100
  69.2 1.0 copy-start.5
  70.2 38.2 %all-to-all-start.3 = ((bf16[8,128,512]{2,1,0:T(8,128)(2,1)}), bf16[8,128,512]{2,1,0:T(8,128)(2,1)S(1)}, u32[]{:S(2)}, u32[]{:S(2)}) async-start(bf16[8,128,512]{2,1,0:T(8,128)(2,1)} %bitcast.43), calls=%async_computation.3 | async-start | bytes 2097152 | tf_op jit(solution)/shard_map/all_to_all | solution.py:443
  103.5 1.0 copy-start.8
  107.4 1.0 copy-start.4
  108.4 59.9 %all-to-all-start.1 = ((bf16[8,128,512]{2,1,0:T(8,128)(2,1)}), bf16[8,128,512]{2,1,0:T(8,128)(2,1)}, u32[]{:S(2)}, u32[]{:S(2)}) async-start(bf16[8,128,512]{2,1,0:T(8,128)(2,1)} %bitcast.42), calls=%async_computation.1 | async-start | bytes 2097152 | tf_op jit(solution)/shard_map/all_to_all | solution.py:443
  113.7 1.1 copy-start.1
  120.6 4.6 %collective-permute-start = (f32[1,8,1024]{2,1,0:T(8,128)S(1)}, f32[1,8,1024]{2,1,0:T(8,128)S(1)}, u32[]{:S(2)}, u32[]{:S(2)}) collective-permute-start(f32[1,8,1024]{2,1,0:T(8,128)S(1)} %bitcast.48), channel_id=1, source_target_pairs={{0,4},{4,0},{8,12},{12,8},{16,20},{20,16},{24,28},{28,24},{1,5},{5... | collective-permute-start | bytes 98312 | tf_op jit(solution)/shard_map/ppermute | solution.py:377
  125.2 5.6 %collective-permute-start.1 = (f32[2,8,1024]{2,1,0:T(8,128)S(1)}, f32[2,8,1024]{2,1,0:T(8,128)S(1)}, u32[]{:S(2)}, u32[]{:S(2)}) collective-permute-start(f32[2,8,1024]{2,1,0:T(8,128)S(1)} %pad_maximum_fusion.7), channel_id=1, source_target_pairs={{0,8},{4,12},{8,0},{12,4},{16,24},{20,28},{24,16},{28,20},{1,9},{5... | collective-permute-start | bytes 196616 | tf_op jit(solution)/shard_map/ppermute | solution.py:377
  130.8 6.8 %copy-start.18 = (f32[2,8,1024]{2,1,0:T(8,128)}, f32[2,8,1024]{2,1,0:T(8,128)S(1)}, u32[]{:S(2)}) copy-start(f32[2,8,1024]{2,1,0:T(8,128)S(1)} %collective-permute-done.1) | copy-start | bytes 196612
  130.9 13.1 %collective-permute-start.2 = (f32[4,8,1024]{2,1,0:T(8,128)S(1)}, f32[4,8,1024]{2,1,0:T(8,128)}, u32[]{:S(2)}, u32[]{:S(2)}) collective-permute-start(f32[4,8,1024]{2,1,0:T(8,128)S(1)} %pad_maximum_fusion.4), channel_id=1, source_target_pairs={{0,16},{4,20},{8,24},{12,28},{16,0},{20,4},{24,8},{28,12},{1,17},{... | collective-permute-start | bytes 393224 | tf_op jit(solution)/shard_map/ppermute | solution.py:377
  144.9 1.0 copy-start.6
  145.9 16.7 %copy-start.2 = (bf16[2,128,1024]{2,1,0:T(8,128)(2,1)S(1)}, bf16[2,128,1024]{2,1,0:T(8,128)(2,1)}, u32[]{:S(2)}) copy-start(bf16[2,128,1024]{2,1,0:T(8,128)(2,1)} %param.10) | copy-start | bytes 1572868
  149.4 3.8 %collective-permute-start.11 = (f32[1,4,1024]{2,1,0:T(4,128)S(1)}, f32[1,4,1024]{2,1,0:T(4,128)S(1)}, u32[]{:S(2)}, u32[]{:S(2)}) collective-permute-start(f32[1,4,1024]{2,1,0:T(4,128)S(1)} %bitcast.56), channel_id=1, source_target_pairs={{0,4},{4,0},{8,12},{12,8},{16,20},{20,16},{24,28},{28,24},{1,5},{5... | collective-permute-start | bytes 49160 | tf_op jit(solution)/shard_map/ppermute | solution.py:377
  153.2 4.0 %collective-permute-start.12 = (f32[2,4,1024]{2,1,0:T(4,128)S(1)}, f32[2,4,1024]{2,1,0:T(4,128)S(1)}, u32[]{:S(2)}, u32[]{:S(2)}) collective-permute-start(f32[2,4,1024]{2,1,0:T(4,128)S(1)} %pad_maximum_fusion.11), channel_id=1, source_target_pairs={{0,8},{4,12},{8,0},{12,4},{16,24},{20,28},{24,16},{28,20},{1,9},{5... | collective-permute-start | bytes 98312 | tf_op jit(solution)/shard_map/ppermute | solution.py:377
  157.2 5.4 %collective-permute-start.13 = (f32[4,4,1024]{2,1,0:T(4,128)S(1)}, f32[4,4,1024]{2,1,0:T(4,128)S(1)}, u32[]{:S(2)}, u32[]{:S(2)}) collective-permute-start(f32[4,4,1024]{2,1,0:T(4,128)S(1)} %pad_maximum_fusion.9), channel_id=1, source_target_pairs={{0,16},{4,20},{8,24},{12,28},{16,0},{20,4},{24,8},{28,12},{1,17},{... | collective-permute-start | bytes 196616 | tf_op jit(solution)/shard_map/ppermute | solution.py:377
  166.4 1.0 copy-start.10
  167.3 1.0 copy-start.12
  168.4 35.1 %all-to-all-start.4 = ((bf16[8,128,512]{2,1,0:T(8,128)(2,1)}), bf16[8,128,512]{2,1,0:T(8,128)(2,1)}, u32[]{:S(2)}, u32[]{:S(2)}) async-start(bf16[8,128,512]{2,1,0:T(8,128)(2,1)} %bitcast.46), calls=%async_computation.4 | async-start | bytes 2097152 | tf_op jit(solution)/shard_map/all_to_all | solution.py:443
  172.6 1.0 copy-start.7
  173.7 24.1 %copy-start.3 = (bf16[2,128,1024]{2,1,0:T(8,128)(2,1)S(1)}, bf16[2,128,1024]{2,1,0:T(8,128)(2,1)}, u32[]{:S(2)}) copy-start(bf16[2,128,1024]{2,1,0:T(8,128)(2,1)} %param.10) | copy-start | bytes 1572868
  177.3 5.6 %collective-permute-start.8 = (f32[1,4,1024]{2,1,0:T(4,128)S(1)}, f32[1,4,1024]{2,1,0:T(4,128)S(1)}, u32[]{:S(2)}, u32[]{:S(2)}) collective-permute-start(f32[1,4,1024]{2,1,0:T(4,128)S(1)} %bitcast.52), channel_id=1, source_target_pairs={{0,4},{4,0},{8,12},{12,8},{16,20},{20,16},{24,28},{28,24},{1,5},{5... | collective-permute-start | bytes 49160 | tf_op jit(solution)/shard_map/ppermute | solution.py:377
  182.9 5.2 %collective-permute-start.9 = (f32[2,4,1024]{2,1,0:T(4,128)S(1)}, f32[2,4,1024]{2,1,0:T(4,128)S(1)}, u32[]{:S(2)}, u32[]{:S(2)}) collective-permute-start(f32[2,4,1024]{2,1,0:T(4,128)S(1)} %pad_maximum_fusion.10), channel_id=1, source_target_pairs={{0,8},{4,12},{8,0},{12,4},{16,24},{20,28},{24,16},{28,20},{1,9},{5... | collective-permute-start | bytes 98312 | tf_op jit(solution)/shard_map/ppermute | solution.py:377
  188.1 9.5 %collective-permute-start.10 = (f32[4,4,1024]{2,1,0:T(4,128)S(1)}, f32[4,4,1024]{2,1,0:T(4,128)S(1)}, u32[]{:S(2)}, u32[]{:S(2)}) collective-permute-start(f32[4,4,1024]{2,1,0:T(4,128)S(1)} %pad_maximum_fusion.8), channel_id=1, source_target_pairs={{0,16},{4,20},{8,24},{12,28},{16,0},{20,4},{24,8},{28,12},{1,17},{... | collective-permute-start | bytes 196616 | tf_op jit(solution)/shard_map/ppermute | solution.py:377
  201.4 1.1 copy-start.11
  202.5 1.0 copy-start.14
  203.5 27.6 %all-to-all-start.2 = ((bf16[8,128,512]{2,1,0:T(8,128)(2,1)}), bf16[8,128,512]{2,1,0:T(8,128)(2,1)}, u32[]{:S(2)}, u32[]{:S(2)}) async-start(bf16[8,128,512]{2,1,0:T(8,128)(2,1)} %bitcast.47), calls=%async_computation.2 | async-start | bytes 2097152 | tf_op jit(solution)/shard_map/all_to_all | solution.py:443
  207.7 1.2 copy-start.13
  209.0 3.7 %copy-start.15 = (bf16[4,128,1024]{2,1,0:T(8,128)(2,1)S(1)}, bf16[4,128,1024]{2,1,0:T(8,128)(2,1)}, u32[]{:S(2)}) copy-start(bf16[4,128,1024]{2,1,0:T(8,128)(2,1)} %copy-done.14) | copy-start | bytes 3145732

commit v2 on v1

v2 whole, which is shorter than its diff:
```python
import functools
import math

import jax
import jax.numpy as jnp
from jax import lax
from jax.experimental import pallas as pl
from jax.experimental.pallas import tpu as pltpu
from jax.sharding import PartitionSpec as P

HEAD = 128
BLOCK = 64
NEIGH = 2
LANES = 128
HEAD_CHUNKS = 1
F32 = jnp.float32
BF16 = jnp.bfloat16


def vmem_params(flops=0, moved=0, mib=48):
    return dict(
        compiler_params=pltpu.CompilerParams(vmem_limit_bytes=mib * 1024 * 1024),
        cost_estimate=pl.CostEstimate(flops=flops, bytes_accessed=moved, transcendentals=0),
    )


def slot_of_place(lists_ref, base, place, entries_here, slot_cap):
    owner = lists_ref[base + place] // entries_here
    rank = 0
    for earlier in range(place):
        rank = rank + jnp.where(lists_ref[base + earlier] // entries_here == owner, 1, 0)
    return owner * slot_cap + rank


def place_copies(lists_ref, base, rows_ref, out_refs, zero_ref, sems, places, entries_here, slot_cap):
    slots = out_refs[0].shape[0]
    width = out_refs[0].shape[2]
    if slots > places:
        zero_ref[...] = jnp.zeros_like(zero_ref)
        for chunk, out_ref in enumerate(out_refs):
            blanks = [
                pltpu.make_async_copy(zero_ref, out_ref.at[slot], sems.at[chunk, slot])
                for slot in range(slots)
            ]
            for blank in blanks:
                blank.start()
            for blank in blanks:
                blank.wait()
    slot_list = [
        slot_of_place(lists_ref, base, place, entries_here, slot_cap) for place in range(places)
    ]
    copies = []
    for chunk, out_ref in enumerate(out_refs):
        for place, slot in enumerate(slot_list):
            start = place // NEIGH * BLOCK
            copies.append(
                pltpu.make_async_copy(
                    rows_ref.at[pl.ds(start, BLOCK), pl.ds(chunk * width, width)],
                    out_ref.at[slot],
                    sems.at[chunk, place],
                )
            )
            copies[-1].start()
    for copy in copies:
        copy.wait()


def place_rows(rows, lists_flat, my_index, n_seq, slot_cap, entries_here):
    tok_rows, cols = rows.shape
    places = tok_rows // BLOCK * NEIGH
    slots = n_seq * slot_cap

    def body(lists_ref, index_ref, rows_ref, out_ref, zero_ref, sems):
        place_copies(
            lists_ref,
            index_ref[0] * places,
            rows_ref,
            [out_ref],
            zero_ref,
            sems,
            places,
            entries_here,
            slot_cap,
        )

    return pl.pallas_call(
        body,
        out_shape=jax.ShapeDtypeStruct((slots, BLOCK, cols), rows.dtype),
        in_specs=[
            pl.BlockSpec(memory_space=pltpu.SMEM),
            pl.BlockSpec(memory_space=pltpu.SMEM),
            pl.BlockSpec(memory_space=pltpu.VMEM),
        ],
        out_specs=pl.BlockSpec(memory_space=pl.ANY),
        scratch_shapes=[
            pltpu.VMEM((BLOCK, cols), rows.dtype),
            pltpu.SemaphoreType.DMA((1, max(slots, places))),
        ],
        name="place_rows",
        **vmem_params(moved=2 * slots * BLOCK * cols * 2, mib=60),
    )(lists_flat, my_index, rows)


def add_product(total, parts, weight, sources, placing=None):
    tok_rows, width = parts[0].shape
    feats = weight.shape[1] // lax.axis_size("mp")
    unit = math.gcd(width, feats)
    cuts = range(width // unit)
    first_units = [source * (feats // unit) + at // unit for source, at in sources]
    cols = weight.shape[0]
    step_cols = min(256, cols)
    steps = cols // step_cols
    places = tok_rows // BLOCK * NEIGH
    before = [] if total is None else [total]
    if placing is None:
        chunks = 1
    else:
        lists_flat, my_index, n_seq, slot_cap, entries_here, chunks = placing
        slots = n_seq * slot_cap

    def body(source_ref, *refs):
        refs = list(refs)
        place_refs = [refs.pop(0) for _ in range(2)] if placing is not None else None
        before_ref = refs.pop(0) if before else None
        part_refs = [refs.pop(0) for _ in parts]
        weight_refs = [[refs.pop(0) for _ in cuts] for _ in parts]
        out_refs = [refs.pop(0) for _ in range(chunks)]
        step = pl.program_id(0)
        result = before_ref[...] if before else 0.0
        for part_ref, weight_cuts in zip(part_refs, weight_refs):
            for cut, weight_ref in zip(cuts, weight_cuts):
                result = result + lax.dot_general(
                    part_ref[:, cut * unit : (cut + 1) * unit],
                    weight_ref[...],
                    NT,
                    preferred_element_type=F32,
                )
        if placing is None:
            out_refs[0][...] = result
            return
        low_ref, zero_ref, sems = refs
        low_ref[:, pl.ds(pl.multiple_of(step * step_cols, step_cols), step_cols)] = result.astype(
            BF16
        )

        @pl.when(step == steps - 1)
        def _():
            lists_ref, index_ref = place_refs
            place_copies(
                lists_ref,
                index_ref[0] * places,
                low_ref,
                out_refs,
                zero_ref,
                sems,
                places,
                entries_here,
                slot_cap,
            )

    block = pl.BlockSpec((tok_rows, step_cols), lambda k, s: (0, k))
    in_specs = [block] * len(before)
    in_specs += [pl.BlockSpec((tok_rows, width), lambda k, s: (0, 0))] * len(parts)
    for number in range(len(parts)):
        for cut in cuts:
            in_specs.append(
                pl.BlockSpec((step_cols, unit), lambda k, s, n=number, c=cut: (k, s[n] + c))
            )
    if placing is None:
        out_shape, out_specs = [jax.ShapeDtypeStruct((tok_rows, cols), F32)], [block]
        scratch, extra = [], []
    else:
        chunk_cols = cols // chunks
        out_shape = [jax.ShapeDtypeStruct((slots, BLOCK, chunk_cols), BF16)] * chunks
        out_specs = [pl.BlockSpec(memory_space=pl.ANY)] * chunks
        scratch = [
            pltpu.VMEM((tok_rows, cols), BF16),
            pltpu.VMEM((BLOCK, chunk_cols), BF16),
            pltpu.SemaphoreType.DMA((chunks, max(slots, places))),
        ]
        extra = [lists_flat, my_index]
        in_specs = [pl.BlockSpec(memory_space=pltpu.SMEM)] * 2 + in_specs
    return pl.pallas_call(
        body,
        grid_spec=pltpu.PrefetchScalarGridSpec(
            num_scalar_prefetch=1,
            grid=(steps,),
            in_specs=in_specs,
            out_specs=out_specs,
            scratch_shapes=scratch,
        ),
        out_shape=out_shape,
        name="add_product",
        **vmem_params(moved=1, mib=60),
    )(
        jnp.stack(first_units).astype(jnp.int32),
        *extra,
        *before,
        *parts,
        *[weight] * (len(parts) * len(cuts)),
    )


def join_places(
    chunk, chunks, back, before, lists_flat, my_index, n_seq, slot_cap, entries_here, blocks_here
):
    slots, _, cols = back.shape
    places = blocks_here * NEIGH
    kept = [] if before is None else [before]

    def body(lists_ref, index_ref, back_ref, *refs):
        out_ref = refs[-1]
        base = index_ref[0] * places
        for block in range(blocks_here):
            total = 0.0
            for neighbour in range(NEIGH):
                slot = slot_of_place(
                    lists_ref, base, block * NEIGH + neighbour, entries_here, slot_cap
                )
                total = total + back_ref[slot].astype(F32)
            out_ref[block * BLOCK : (block + 1) * BLOCK, :] = total.astype(out_ref.dtype)

    return pl.pallas_call(
        body,
        grid=(1,),
        out_shape=jax.ShapeDtypeStruct((blocks_here * BLOCK, chunks * cols), back.dtype),
        in_specs=[
            pl.BlockSpec(memory_space=pltpu.SMEM),
            pl.BlockSpec(memory_space=pltpu.SMEM),
            pl.BlockSpec((slots, BLOCK, cols), lambda i: (0, 0, 0)),
        ]
        + [pl.BlockSpec(memory_space=pl.ANY)] * len(kept),
        out_specs=pl.BlockSpec((blocks_here * BLOCK, cols), lambda i: (0, chunk)),
        input_output_aliases={3: 0} if kept else {},
        name="join_places",
        **vmem_params(moved=3 * slots * BLOCK * cols),
    )(lists_flat, my_index, back, *kept)


def lane_parts(total):
    width = 256 if total % 256 == 0 else LANES
    return [slice(at, at + width) for at in range(0, total, width)]


def pick_entry(stacked, entry):
    entries = stacked.shape[0] // LANES
    chosen = stacked[:LANES]
    for number in range(1, entries):
        chosen = jnp.where(
            entry == number, stacked[number * LANES : (number + 1) * LANES], chosen
        )
    return chosen


def spread_entry(chosen, entry, entries):
    return jnp.concatenate(
        [jnp.where(entry == number, chosen, 0.0) for number in range(entries)], axis=0
    ).astype(BF16)


NT = (((1,), (1,)), ((), ()))
NN = (((1,), (0,)), ((), ()))
TN = (((0,), (0,)), ((), ()))


def local_softmax(query_rows, keys, entry_lanes):
    rows, cols = query_rows.shape
    heads = cols // HEAD
    key_rows = keys.shape[0]
    scale = 1.0 / math.sqrt(HEAD)

    def body(query_ref, key_ref, entry_ref, weight_ref, lse_ref):
        head = pl.program_id(0)
        for part in lane_parts(rows):
            entry = entry_ref[:, part]
            scores = lax.dot_general(
                key_ref[...], query_ref[part, :], NT, preferred_element_type=F32
            )
            scores = pick_entry(scores, entry) * scale
            top = jnp.max(scores, axis=0, keepdims=True)
            raised = jnp.exp(scores - top)
            total = jnp.sum(raised, axis=0, keepdims=True)
            weight_ref[0, :, part] = raised / total
            lse_ref[pl.ds(head, 1), part] = top + jnp.log(total)

    return pl.pallas_call(
        body,
        grid=(heads,),
        out_shape=(
            jax.ShapeDtypeStruct((heads, LANES, rows), F32),
            jax.ShapeDtypeStruct((heads, rows), F32),
        ),
        in_specs=[
            pl.BlockSpec((rows, HEAD), lambda h: (0, h)),
            pl.BlockSpec((key_rows, HEAD), lambda h: (0, h)),
            pl.BlockSpec((1, rows), lambda h: (0, 0)),
        ],
        out_specs=(
            pl.BlockSpec((1, LANES, rows), lambda h: (h, 0, 0)),
            pl.BlockSpec((heads, rows), lambda h: (0, 0)),
        ),
        name="local_softmax",
        **vmem_params(moved=1, mib=60),
    )(query_rows, keys, entry_lanes)


def partner_lanes(partner_ref, all_ref, out_ref, slots):
    heads = out_ref.shape[0]
    lane = lax.broadcasted_iota(jnp.int32, (heads, LANES), 1)
    for group in range(slots // 2):
        halves = []
        for half in range(2):
            slot = group * 2 + half
            device, there = partner_ref[0, slot], partner_ref[1, slot]
            start = pl.multiple_of(there // 2 * LANES, LANES)
            tile = all_ref[device, :, pl.ds(start, LANES)]
            turned = pltpu.roll(tile, BLOCK, 1)
            halves.append(jnp.where(there % 2 == half, tile, turned))
        out_ref[:, group * LANES : (group + 1) * LANES] = jnp.where(
            lane < BLOCK, halves[0], halves[1]
        )


def live_lanes(partner_ref, all_ref, out_ref, slots, rows):
    lane = lax.broadcasted_iota(jnp.int32, (1, LANES), 1)
    for group in range(slots // 2):
        own, other = [], []
        for half in range(2):
            slot = group * 2 + half
            reader, place = partner_ref[2, slot], partner_ref[3, slot]
            counts = all_ref[reader, 0:1, rows:]
            count = jnp.sum(
                jnp.where(lane == place // NEIGH, counts, 0.0), axis=1, keepdims=True
            )
            at = (place % NEIGH).astype(F32)
            filled = partner_ref[4, slot] > 0
            own.append(jnp.where((at < count) & filled, 1.0, 0.0))
            other.append(jnp.where(NEIGH - 1 - at < count, 1.0, 0.0))
        part = slice(group * LANES, (group + 1) * LANES)
        out_ref[0:1, part] = jnp.where(lane < BLOCK, own[0], own[1])
        out_ref[1:2, part] = jnp.where(lane < BLOCK, other[0], other[1])


def weight_grads(n_seq, weights, lse, grad_rows, values, entry_lanes, count_lanes):
    heads, _, rows = weights.shape
    value_rows = values.shape[0]

    def body(
        weight_ref, lse_ref, grad_ref, value_ref, entry_ref, count_ref, slope_ref, all_ref, told_ref
    ):
        head = pl.program_id(0)

        @pl.when(head == 0)
        def _():
            told_ref[:heads, :rows] = lse_ref[...]
            told_ref[:, rows:] = jnp.broadcast_to(count_ref[...], (2 * heads, LANES))

        for part in lane_parts(rows):
            slope = lax.dot_general(
                value_ref[...], grad_ref[part, :], NT, preferred_element_type=F32
            )
            slope = pick_entry(slope, entry_ref[:, part])
            slope_ref[0, :, part] = slope
            told_ref[pl.ds(heads + head, 1), part] = jnp.sum(
                weight_ref[0, :, part] * slope, axis=0, keepdims=True
            )

        @pl.when(head == heads - 1)
        def _():
            for device in range(n_seq):
                all_ref[device] = told_ref[...]

    return pl.pallas_call(
        body,
        grid=(heads,),
        out_shape=(
            jax.ShapeDtypeStruct((heads, LANES, rows), F32),
            jax.ShapeDtypeStruct((n_seq, 2 * heads, rows + LANES), F32),
        ),
        in_specs=[
            pl.BlockSpec((1, LANES, rows), lambda h: (h, 0, 0)),
            pl.BlockSpec((heads, rows), lambda h: (0, 0)),
            pl.BlockSpec((rows, HEAD), lambda h: (0, h)),
            pl.BlockSpec((value_rows, HEAD), lambda h: (0, h)),
            pl.BlockSpec((1, rows), lambda h: (0, 0)),
            pl.BlockSpec((1, LANES), lambda h: (0, 0)),
        ],
        out_specs=(
            pl.BlockSpec((1, LANES, rows), lambda h: (h, 0, 0)),
            pl.BlockSpec((n_seq, 2 * heads, rows + LANES), lambda h: (0, 0, 0)),
        ),
        scratch_shapes=[pltpu.VMEM((2 * heads, rows + LANES), F32)],
        name="weight_grads",
        **vmem_params(moved=1, mib=60),
    )(weights, lse, grad_rows, values, entry_lanes, count_lanes)


def score_grads(weights, slope, all_told, my_index, partner, keys, entry_lanes):
    here, _, rows = weights.shape
    key_rows = keys.shape[0]
    slots = rows // BLOCK
    scale = 1.0 / math.sqrt(HEAD)

    def body(
        partner_ref,
        index_ref,
        weight_ref,
        slope_ref,
        all_ref,
        key_ref,
        entry_ref,
        share_ref,
        low_ref,
        query_ref,
        told_ref,
        other_ref,
        live_ref,
    ):
        head = pl.program_id(0)

        @pl.when(head == 0)
        def _():
            told_ref[...] = all_ref[index_ref[0], :, :rows]
            partner_lanes(partner_ref, all_ref, other_ref, slots)
            live_lanes(partner_ref, all_ref, live_ref, slots, rows)

        for part in lane_parts(rows):
            entry = entry_ref[:, part]
            apart = other_ref[pl.ds(head, 1), part] - told_ref[pl.ds(head, 1), part]
            odds = jnp.where(live_ref[1:2, part] > 0.0, jnp.exp(apart), 0.0)
            share = jnp.where(live_ref[0:1, part] > 0.0, 1.0 / (1.0 + odds), 0.0)
            rest = jnp.where(live_ref[1:2, part] > 0.0, 1.0 / (1.0 + jnp.exp(-apart)), 0.0)
            dot = (
                share * told_ref[pl.ds(here + head, 1), part]
                + rest * other_ref[pl.ds(here + head, 1), part]
            )
            share_ref[pl.ds(head, 1), part] = share
            joint = weight_ref[0, :, part] * share
            low = joint * (slope_ref[0, :, part] - dot)
            low_ref[0, :, part] = low.astype(BF16)
            wide = spread_entry(low, entry, key_rows // LANES)
            query = lax.dot_general(wide, key_ref[...], TN, preferred_element_type=F32)
            query_ref[part, :] = (query * scale).astype(BF16)

    return pl.pallas_call(
        body,
        grid=(here,),
        out_shape=(
            jax.ShapeDtypeStruct((here, rows), F32),
            jax.ShapeDtypeStruct((here, LANES, rows), BF16),
            jax.ShapeDtypeStruct((rows, here * HEAD), BF16),
        ),
        in_specs=[
            pl.BlockSpec(memory_space=pltpu.SMEM),
            pl.BlockSpec(memory_space=pltpu.SMEM),
            pl.BlockSpec((1, LANES, rows), lambda h: (h, 0, 0)),
            pl.BlockSpec((1, LANES, rows), lambda h: (h, 0, 0)),
            pl.BlockSpec(all_told.shape, lambda h: (0, 0, 0)),
            pl.BlockSpec((key_rows, HEAD), lambda h: (0, h)),
            pl.BlockSpec((1, rows), lambda h: (0, 0)),
        ],
        out_specs=(
            pl.BlockSpec((here, rows), lambda h: (0, 0)),
            pl.BlockSpec((1, LANES, rows), lambda h: (h, 0, 0)),
            pl.BlockSpec((rows, HEAD), lambda h: (0, h)),
        ),
        scratch_shapes=[
            pltpu.VMEM((2 * here, rows), F32),
            pltpu.VMEM((2 * here, rows), F32),
            pltpu.VMEM((2, rows), F32),
        ],
        name="score_grads",
        **vmem_params(moved=1, mib=60),
    )(partner, my_index, weights, slope, all_told, keys, entry_lanes)


def entry_grads(chunk, weights, share, low, query_rows, grad_rows, entry_lanes, entry_rows):
    _, _, rows = weights.shape
    here = low.shape[0]
    first = chunk * here
    scale = 1.0 / math.sqrt(HEAD)

    def body(weight_ref, share_ref, low_ref, query_ref, grad_ref, entry_ref, key_ref, value_ref):
        head = pl.program_id(0)
        key_sum = jnp.zeros((entry_rows, HEAD), F32)
        value_sum = jnp.zeros((entry_rows, HEAD), F32)
        for part in lane_parts(rows):
            entry = entry_ref[:, part]
            joint = weight_ref[0, :, part] * share_ref[pl.ds(head, 1), part]
            wide = spread_entry(joint, entry, entry_rows // LANES)
            value_sum += lax.dot_general(wide, grad_ref[part, :], NN, preferred_element_type=F32)
            wide = spread_entry(low_ref[0, :, part].astype(F32), entry, entry_rows // LANES)
            key_sum += lax.dot_general(wide, query_ref[part, :], NN, preferred_element_type=F32)
        key_ref[...] = (key_sum * scale).astype(BF16)
        value_ref[...] = value_sum.astype(BF16)

    return pl.pallas_call(
        body,
        grid=(here,),
        out_shape=(
            jax.ShapeDtypeStruct((entry_rows, here * HEAD), BF16),
            jax.ShapeDtypeStruct((entry_rows, here * HEAD), BF16),
        ),
        in_specs=[
            pl.BlockSpec((1, LANES, rows), lambda h: (first + h, 0, 0)),
            pl.BlockSpec((here, rows), lambda h: (0, 0)),
            pl.BlockSpec((1, LANES, rows), lambda h: (h, 0, 0)),
            pl.BlockSpec((rows, HEAD), lambda h: (0, first + h)),
            pl.BlockSpec((rows, HEAD), lambda h: (0, h)),
            pl.BlockSpec((1, rows), lambda h: (0, 0)),
        ],
        out_specs=(
            pl.BlockSpec((entry_rows, HEAD), lambda h: (0, h)),
            pl.BlockSpec((entry_rows, HEAD), lambda h: (0, h)),
        ),
        name="entry_grads",
        **vmem_params(moved=1, mib=60),
    )(weights, share, low, query_rows, grad_rows, entry_lanes)


def swap(value, axis, bits):
    size = lax.axis_size(axis)
    return lax.ppermute(value, axis, [(i, i ^ bits) for i in range(size)])


def rank_slots(owners):
    slot_total = owners.shape[-1]
    earlier_mask = jnp.arange(slot_total)[None, :] < jnp.arange(slot_total)[:, None]
    same_owner = owners[..., :, None] == owners[..., None, :]
    return jnp.sum(same_owner & earlier_mask, axis=-1)


def owner_tables(all_lists, my_index, entries_here, slot_cap):
    n_seq, places = all_lists.shape
    owners = all_lists // entries_here
    ranks = rank_slots(owners)
    chosen = (owners == my_index)[:, None, :] & (
        ranks[:, None, :] == jnp.arange(slot_cap)[None, :, None]
    )

    def look(table):
        return jnp.sum(jnp.where(chosen, table[:, None, :], 0), axis=2).reshape(-1)

    def other(table):
        return table.reshape(n_seq, -1, NEIGH)[:, :, ::-1].reshape(n_seq, places)

    reader = jnp.arange(n_seq)[:, None]
    partner = [
        look(other(owners)),
        look(other(ranks) + slot_cap * reader),
        look(reader + jnp.zeros_like(owners)),
        look(jnp.arange(places) + jnp.zeros_like(owners)),
        look(jnp.ones_like(owners)),
    ]
    entry = look(all_lists % entries_here)
    return (
        jnp.repeat(entry[None], BLOCK, axis=1).astype(jnp.int32),
        jnp.stack(partner).astype(jnp.int32),
    )


def on_device(out_grad, out_weight, queries, keys, values, retrieval, counts):
    n_seq, n_mp = lax.axis_size("seq"), lax.axis_size("mp")
    my_index, my_mp = lax.axis_index("seq"), lax.axis_index("mp")
    tok_rows, head_cols = queries.shape
    entries_here, nbr_rows, _ = keys.shape
    blocks_here = tok_rows // BLOCK
    places = blocks_here * NEIGH
    slot_cap = (places + n_seq - 1) // n_seq
    rows = n_seq * slot_cap * BLOCK
    feats = out_grad.shape[1]
    lists_flat = retrieval.reshape(-1).astype(jnp.int32)
    index_arr = my_index.astype(jnp.int32).reshape(1)
    key_rows = keys.reshape(entries_here * nbr_rows, head_cols)
    value_rows = values.reshape(entries_here * nbr_rows, head_cols)

    def exchange(slot_rows):
        cols = slot_rows.shape[-1]
        return lax.all_to_all(
            slot_rows.reshape(n_seq, slot_cap * BLOCK, cols), "seq", 0, 0, tiled=True
        ).reshape(rows, cols)

    far_bits = list(range(2, n_mp, 2))
    cut = feats * 3 // 4
    tie = lax.optimization_barrier

    def sources(at):
        return [(my_mp ^ bits ^ side, at) for bits in far_bits for side in (0, 1)]

    def both_cores(pieces):
        return [x for piece in pieces for x in (piece, swap(piece, "mp", 1))]

    near = swap(out_grad, "mp", 1)
    first = [swap(out_grad[:, :cut], "mp", bits) for bits in far_bits]
    near, outgoing = tie((near, queries))
    query_places = place_rows(outgoing, lists_flat, index_arr, n_seq, slot_cap, entries_here)
    query_slots = exchange(query_places)
    entry_lanes, partner = owner_tables(
        retrieval.reshape(n_seq, places), my_index, entries_here, slot_cap
    )

    placing = (lists_flat, index_arr, n_seq, slot_cap, entries_here, HEAD_CHUNKS)
    (grad_sum,) = add_product(None, [out_grad, near], out_weight, [(my_mp, 0), (my_mp ^ 1, 0)])
    second, first, grad_sum = tie((out_grad[:, cut:], first, grad_sum))
    second = [swap(second, "mp", bits) for bits in far_bits]
    (grad_sum,) = add_product(grad_sum, both_cores(first), out_weight, sources(0))
    second, grad_sum = tie((second, grad_sum))
    grad_sum = add_product(grad_sum, both_cores(second), out_weight, sources(cut), placing)
    grad_places = grad_sum

    count_lanes = jnp.pad(counts.astype(F32), (0, LANES - blocks_here))[None]
    weights, lse = local_softmax(query_slots, key_rows, entry_lanes)

    grad_slots = exchange(grad_places[0])
    slope, told = weight_grads(
        n_seq, weights, lse, grad_slots, value_rows, entry_lanes, count_lanes
    )
    all_told = lax.all_to_all(told, "seq", 0, 0, tiled=True)
    share, low, query_terms = score_grads(
        weights, slope, all_told, index_arr, partner, key_rows, entry_lanes
    )
    back = exchange(query_terms).reshape(-1, BLOCK, head_cols)
    query_grad = join_places(
        0, 1, back, None, lists_flat, index_arr, n_seq, slot_cap, entries_here, blocks_here
    )
    key_grad, value_grad = entry_grads(
        0, weights, share, low, query_slots, grad_slots, entry_lanes, key_rows.shape[0]
    )
    key_grad = key_grad.reshape(keys.shape)
    value_grad = value_grad.reshape(values.shape)
    return (query_grad, key_grad, value_grad)


def solution(mesh):
    return jax.shard_map(
        on_device,
        mesh=mesh,
        in_specs=(
            P("seq", "mp"),
            P("mp", None),
            P("seq", "mp"),
            P("seq", None, "mp"),
            P("seq", None, "mp"),
            P(),
            P("seq"),
        ),
        out_specs=(P("seq", "mp"), P("seq", None, "mp"), P("seq", None, "mp")),
        check_vma=False,
    )
```

time: 235 us -> 216 us (0.919)
  waiting for transfers between devices: 77.5 us -> 110 us
  blocking collectives: 25 us -> 0 us
  Pallas kernels: 41.2 us -> 65.1 us
  starting transfers between devices: 46.2 us -> 24 us
  matrix products: 18.1 us -> 0 us
  local copies, waits for them, and re-layouts: 19.7 us -> 12.1 us
    all_to_all x5 -> x3, waiting for transfers between devices: 11.2 us -> 78.3 us  [exchange(): lax.all_to_all(slot_rows.reshape(n_seq, slot_cap * BLOCK, cols), 'seq', 0...]
    ppermute x14 -> x5, waiting for transfers between devices: 66.3 us -> 17.2 us  [swap(): return lax.ppermute(value, axis, [(i, i ^ bits) for i in range(size)])]
    pallas_call x4 -> x5, Pallas kernels: 10.5 us -> 36.4 us  [the longest x3 26.1 us: add_product(): pl.pallas_call(body, grid_spec=pltpu.PrefetchScalarGridSpec(num_scalar_pr...]
    unnamed x1 -> x0, blocking collectives: 25 us -> none
    dot_general x6 -> x0, matrix products: 18.1 us -> none  [product(): return lax.dot_general(part, weight, NT, preferred_element_type=F32)]
    ppermute x14 -> x5, starting transfers between devices: 21.4 us -> 4.77 us  [swap(): return lax.ppermute(value, axis, [(i, i ^ bits) for i in range(size)])]
    all_to_all x0 -> x1, waiting for transfers between devices: none -> 14.6 us  [on_device(): all_told = lax.all_to_all(told, 'seq', 0, 0, tiled=True)]
    unnamed x48 -> x19, local copies, waits for them, and re-layouts: 13.7 us -> 4.39 us
  transfers between devices with their start and end apart: 19 -> 9, of which waited for: 12 -> 7; matrix products, arithmetic and copies ran while one was open for 11% -> 5% of each run, Pallas kernels for 17% -> 21%
where the time goes in v2:
time: 216 us; the launch traced here: 215 us
  waiting for transfers between devices  110 us (51%)
  Pallas kernels  65.1 us (30%)
  starting transfers between devices  24 us (11%)
  local copies, waits for them, and re-layouts  12.1 us (6%)
  other arithmetic  2.54 us (1%)
    all_to_all x3, waiting for transfers between devices, exchange(): lax.all_to_all(slot_rows.reshape(n_seq, slot_cap * BLOCK, cols), 'seq', 0...  78.3 us
    pallas_call x3, Pallas kernels, add_product(): pl.pallas_call(body, grid_spec=pltpu.PrefetchScalarGridSpec(num_scalar_pr...  26.1 us
    ppermute x5, waiting for transfers between devices, swap(): return lax.ppermute(value, axis, [(i, i ^ bits) for i in range(size)])  17.2 us
    all_to_all x3, starting transfers between devices, exchange(): lax.all_to_all(slot_rows.reshape(n_seq, slot_cap * BLOCK, cols), 'seq', 0...  15.6 us
    all_to_all x1, waiting for transfers between devices, on_device(): all_told = lax.all_to_all(told, 'seq', 0, 0, tiled=True)  14.6 us
    pallas_call x1, Pallas kernels, score_grads(): pl.pallas_call(body, grid=(here,), out_shape=(jax.ShapeDtypeStruct((here,...  9.14 us
    pallas_call x1, Pallas kernels, entry_grads(): pl.pallas_call(body, grid=(here,), out_shape=(jax.ShapeDtypeStruct((entry...  8.53 us
    pallas_call x1, Pallas kernels, weight_grads(): pl.pallas_call(body, grid=(heads,), out_shape=(jax.ShapeDtypeStruct((head...  8.33 us
  transfers between devices with their start and end apart: 9, of which 7 were waited for; matrix products, arithmetic and copies ran while one was open for 5% of the time, Pallas kernels for 21%

profile of v2, /device:TPU:0, one launch (start us, length us, event | category | flops | bytes accessed | tf_op | source)
XLA Modules:
  0.0 214.7 jit_solution(1563586943959101220)
XLA Ops:
  0.6 0.0 copy-start.7
  0.6 0.5 collective-permute-start
  1.2 2.6 %slice.7 = bf16[512,1536]{1,0:T(8,128)(2,1)} slice(bf16[512,2048]{1,0:T(8,128)(2,1)} %refs_0_.1), slice={[0:512], [0:1536]} | slice | bytes 3145728 | tf_op jit(solution)/shard_map/slice | solution.py:594
  3.8 2.5 %collective-permute-start.1 = (bf16[512,1536]{1,0:T(8,128)(2,1)}, bf16[512,1536]{1,0:T(8,128)(2,1)}, u32[]{:S(2)}, u32[]{:S(2)}) collective-permute-start(bf16[512,1536]{1,0:T(8,128)(2,1)} %slice.7), channel_id=1, source_target_pairs={{0,2},{1,3},{2,0},{3,1},{4,6},{5,7},{6,4},{7,5},{8,10},{9,11},{10,... | collective-permute-start | bytes 4718600 | tf_op jit(solution)/shard_map/ppermute | solution.py:523
  6.3 0.1 copy.22
  6.4 0.7 reshape.180.lists_ref.refs_0_
  7.1 0.0 collective-permute-done.refs_1_
  7.1 3.5 %place_rows.1 = bf16[16,64,1024]{2,1,0:T(8,128)(2,1)} custom-call(s32[128]{0:T(128)} %reshape.180.lists_ref.refs_0_, s32[1]{0:T(128)} %bitcast.index_ref.refs_1_, bf16[512,1024]{1,0:T(8,128)(2,1)} %rows_ref), custom_call_target="tpu_custom_call" | custom-call | bytes 4194304 | tf_op jit(solution)/shard_map/place_rows/pallas_call | solution.py:86
  10.6 5.8 %all-to-all-start = ((bf16[8,128,1024]{2,1,0:T(8,128)(2,1)}), bf16[8,128,1024]{2,1,0:T(8,128)(2,1)S(1)}, u32[]{:S(2)}, u32[]{:S(2)}) async-start(bf16[8,128,1024]{2,1,0:T(8,128)(2,1)} %bitcast.30), calls=%async_computation | async-start | bytes 4194304 | tf_op jit(solution)/shard_map/all_to_all | solution.py:579
  16.4 1.1 slice.6
  17.5 0.6 pad_add_fusion.1.source_ref
  18.1 10.2 %add_product.3.refs_0_ = f32[512,1024]{1,0:T(8,128)} custom-call(s32[2]{0:T(128)} %pad_add_fusion.1.source_ref, bf16[512,2048]{1,0:T(8,128)(2,1)} %refs_0_.1, bf16[512,2048]{1,0:T(8,128)(2,1)} %copy-done.4, bf16[1024,8192]{1,0:T(8,128)(2,1)} %refs_6_.3, bf16[1024,8192]{1,0:T(8,128)(2,1)} %refs_6_.3), custom_call_target="tpu_custom_call" | custom-call | bytes 1 | tf_op jit(solution)/shard_map/add_product/pallas_call | solution.py:183
  28.3 13.4 %collective-permute-done.1.refs_1_ = bf16[512,1536]{1,0:T(8,128)(2,1)} collective-permute-done((bf16[512,1536]{1,0:T(8,128)(2,1)}, bf16[512,1536]{1,0:T(8,128)(2,1)}, u32[]{:S(2)}, u32[]{:S(2)}) %collective-permute-start.1) | collective-permute-done | bytes 1572896 | tf_op jit(solution)/shard_map/ppermute | solution.py:523
  41.7 0.0 collective-permute-start.3
  41.7 1.7 collective-permute-start.2
  43.4 0.6 pad_add_fusion.2.source_ref
  44.0 1.4 collective-permute-done.3.refs_2_
  45.4 9.4 %add_product.4.refs_2_ = f32[512,1024]{1,0:T(8,128)} custom-call(s32[2]{0:T(128)} %pad_add_fusion.2.source_ref, f32[512,1024]{1,0:T(8,128)} %add_product.3.refs_0_, bf16[512,1536]{1,0:T(8,128)(2,1)} %collective-permute-done.1.refs_1_, bf16[512,1536]{1,0:T(8,128)(2,1)} %collective-permute-done.3.refs_2_, bf16[1024,8192]{1,0:T(8,128)(2,1)} %refs_6_.3, ...), custom_call_target="tpu_custom_call" | custom-call | bytes 1 | tf_op jit(solution)/shard_map/add_product/pallas_call | solution.py:183
  54.8 1.2 collective-permute-done.2.refs_3_
  56.0 0.0 collective-permute-start.4
  56.0 0.7 pad_add_fusion.source_ref
  56.8 1.2 collective-permute-done.4.refs_4_
  57.9 0.8 copy-done.6
  58.7 6.5 %add_product.5 = bf16[16,64,1024]{2,1,0:T(8,128)(2,1)} custom-call(s32[2]{0:T(128)} %pad_add_fusion.source_ref, s32[128]{0:T(128)} %reshape.180.lists_ref.refs_0_, s32[1]{0:T(128)} %bitcast.index_ref.refs_1_, f32[512,1024]{1,0:T(8,128)} %add_product.4.refs_2_, bf16[512,512]{1,0:T(8,128)(2,1)} %copy-done.5, bf16[512,512]{1,0:T(8,128)(2,1)} %copy-done.6, ...), custom_call_target="tpu_custom_call" | custom-call | bytes 1 | tf_op jit(solution)/shard_map/add_product/pallas_call | solution.py:183
  65.3 0.0 all-to-all-done
  65.3 0.0 copy-start.8
  65.3 1.3 copy-done.2
  66.6 6.1 %all-to-all-start.1 = ((bf16[8,128,1024]{2,1,0:T(8,128)(2,1)}), bf16[8,128,1024]{2,1,0:T(8,128)(2,1)S(1)}, u32[]{:S(2)}, u32[]{:S(2)}) async-start(bf16[8,128,1024]{2,1,0:T(8,128)(2,1)} %bitcast.29), calls=%async_computation.1 | async-start | bytes 4194304 | tf_op jit(solution)/shard_map/all_to_all | solution.py:579
  72.7 0.1 reshape.183
  72.8 0.1 reshape.182
  72.9 0.1 copy.24
  73.0 0.1 copy.25
  73.1 0.3 convert_reduce_fusion
  73.4 0.1 copy.27
  73.5 0.1 copy.28
  73.6 0.3 select_reduce_fusion
  73.9 0.1 copy.33
  74.0 0.1 broadcast_in_dim_reshape.4
  74.0 0.1 broadcast_in_dim.74
  74.1 0.7 broadcast_in_dim.75.entry_ref
  74.8 0.5 pad_bitcast_fusion.count_ref
  75.3 7.6 %local_softmax.1 = (f32[8,128,1024]{2,1,0:T(8,128)}, f32[8,1024]{1,0:T(8,128)}) custom-call(bf16[1024,1024]{1,0:T(8,128)(2,1)} %bitcast.27, bf16[256,1024]{1,0:T(8,128)(2,1)} %bitcast.31, s32[1,1024]{1,0:T(1,128)} %broadcast_in_dim.75.entry_ref), custom_call_target="tpu_custom_call" | custom-call | bytes 1 | tf_op jit(solution)/shard_map/local_softmax/pallas_call | solution.py:286
  82.9 38.4 %all-to-all-done.1 = bf16[8,128,1024]{2,1,0:T(8,128)(2,1)S(1)} async-done(((bf16[8,128,1024]{2,1,0:T(8,128)(2,1)}), bf16[8,128,1024]{2,1,0:T(8,128)(2,1)S(1)}, u32[]{:S(2)}, u32[]{:S(2)}) %all-to-all-start.1) | async-done | bytes 2097184 | tf_op jit(solution)/shard_map/all_to_all | solution.py:579
  121.2 1.3 copy-done.1
  122.6 8.3 %weight_grads.1 = (f32[8,128,1024]{2,1,0:T(8,128)}, f32[8,16,1152]{2,1,0:T(8,128)}) custom-call(f32[8,128,1024]{2,1,0:T(8,128)} %get-tuple-element.20.weight_ref, f32[8,1024]{1,0:T(8,128)} %get-tuple-element.21.lse_ref, bf16[1024,1024]{1,0:T(8,128)(2,1)} %bitcast.25, bf16[256,1024]{1,0:T(8,128)(2,1)} %bitcast.34, s32[1,1024]{1,0:T(1,128)} %broadcast_in_dim.75.entry_ref, ...), custom_call_target="tpu_custom_call" | custom-call | bytes 1 | tf_op jit(solution)/shard_map/weight_grads/pallas_call | solution.py:373
  130.9 3.6 %all-to-all-start.2 = ((f32[8,16,1152]{2,1,0:T(8,128)}), f32[8,16,1152]{2,1,0:T(8,128)S(1)}, u32[]{:S(2)}, u32[]{:S(2)}) async-start(f32[8,16,1152]{2,1,0:T(8,128)} %get-tuple-element.29), calls=%async_computation.2 | async-start | bytes 1179648 | tf_op jit(solution)/shard_map/all_to_all | solution.py:618
  134.5 0.1 copy.32
  134.6 0.1 stack_reshape.19
  134.7 0.1 copy.31
  134.8 0.1 stack_reshape.18
  134.9 0.1 copy.30
  135.0 0.1 stack_reshape.17
  135.0 0.1 copy.29
  135.1 0.1 stack_reshape.16
  135.2 0.1 copy.26
  135.3 0.1 stack_reshape.15
  135.4 0.6 stack.30.partner_ref
  136.0 14.6 %all-to-all-done.2.all_ref = f32[8,16,1152]{2,1,0:T(8,128)S(1)} async-done(((f32[8,16,1152]{2,1,0:T(8,128)}), f32[8,16,1152]{2,1,0:T(8,128)S(1)}, u32[]{:S(2)}, u32[]{:S(2)}) %all-to-all-start.2) | async-done | bytes 589856 | tf_op jit(solution)/shard_map/all_to_all | solution.py:618
  150.6 0.8 copy-done.3
  151.4 9.1 %score_grads.1 = (f32[8,1024]{1,0:T(8,128)}, bf16[8,128,1024]{2,1,0:T(8,128)(2,1)}, bf16[1024,1024]{1,0:T(8,128)(2,1)}) custom-call(s32[5,16]{1,0:T(8,128)} %stack.30.partner_ref, s32[1]{0:T(128)} %bitcast.index_ref.refs_1_, f32[8,128,1024]{2,1,0:T(8,128)} %get-tuple-element.20.weight_ref, f32[8,128,1024]{2,1,0:T(8,128)} %get-tuple-element.28.slope_ref, ...), custom_call_target="tpu_custom_call" | custom-call | bytes 1 | tf_op jit(solution)/shard_map/score_grads/pallas_call | solution.py:445
  160.6 3.6 %all-to-all-start.3 = ((bf16[8,128,1024]{2,1,0:T(8,128)(2,1)}), bf16[8,128,1024]{2,1,0:T(8,128)(2,1)S(1)}, u32[]{:S(2)}, u32[]{:S(2)}) async-start(bf16[8,128,1024]{2,1,0:T(8,128)(2,1)} %bitcast.33), calls=%async_computation.3 | async-start | bytes 4194304 | tf_op jit(solution)/shard_map/all_to_all | solution.py:579
  164.2 8.5 %entry_grads.1 = (bf16[256,1024]{1,0:T(8,128)(2,1)}, bf16[256,1024]{1,0:T(8,128)(2,1)}) custom-call(f32[8,128,1024]{2,1,0:T(8,128)} %get-tuple-element.20.weight_ref, f32[8,1024]{1,0:T(8,128)} %get-tuple-element.31.share_ref, bf16[8,128,1024]{2,1,0:T(8,128)(2,1)} %get-tuple-element.32.low_ref, bf16[1024,1024]{1,0:T(8,128)(2,1)} %bitcast.28, ...), custom_call_target="tpu_custom_call" | custom-call | bytes 1 | tf_op jit(solution)/shard_map/entry_grads/pallas_call | solution.py:497
  172.7 39.9 %all-to-all-done.3 = bf16[8,128,1024]{2,1,0:T(8,128)(2,1)S(1)} async-done(((bf16[8,128,1024]{2,1,0:T(8,128)(2,1)}), bf16[8,128,1024]{2,1,0:T(8,128)(2,1)S(1)}, u32[]{:S(2)}, u32[]{:S(2)}) %all-to-all-start.3) | async-done | bytes 2097184 | tf_op jit(solution)/shard_map/all_to_all | solution.py:579
  212.6 2.0 join_places.1
  (21 shorter events, 0.1 us)
Async XLA Ops:
  0.6 5.7 %copy-start.7 = (s32[64,2]{0,1:T(2,128)S(1)}, s32[64,2]{0,1:T(2,128)}, u32[]{:S(2)}) copy-start(s32[64,2]{0,1:T(2,128)} %param.12) | copy-start | bytes 1540
  0.6 6.4 %collective-permute-start = (bf16[512,2048]{1,0:T(8,128)(2,1)}, bf16[512,2048]{1,0:T(8,128)(2,1)S(1)}, u32[]{:S(2)}, u32[]{:S(2)}) collective-permute-start(bf16[512,2048]{1,0:T(8,128)(2,1)} %refs_0_.1), channel_id=1, source_target_pairs={{0,1},{1,0},{2,3},{3,2},{4,5},{5,4},{6,7},{7,6},{8,9},{9,8},{10,11... | collective-permute-start | bytes 6291464 | tf_op jit(solution)/shard_map/ppermute | solution.py:523
  3.8 37.9 %collective-permute-start.1 = (bf16[512,1536]{1,0:T(8,128)(2,1)}, bf16[512,1536]{1,0:T(8,128)(2,1)}, u32[]{:S(2)}, u32[]{:S(2)}) collective-permute-start(bf16[512,1536]{1,0:T(8,128)(2,1)} %slice.7), channel_id=1, source_target_pairs={{0,2},{1,3},{2,0},{3,1},{4,6},{5,7},{6,4},{7,5},{8,10},{9,11},{10,... | collective-permute-start | bytes 4718600 | tf_op jit(solution)/shard_map/ppermute | solution.py:523
  7.1 3.5 %copy-start.4 = (bf16[512,2048]{1,0:T(8,128)(2,1)}, bf16[512,2048]{1,0:T(8,128)(2,1)S(1)}, u32[]{:S(2)}) copy-start(bf16[512,2048]{1,0:T(8,128)(2,1)S(1)} %collective-permute-done.refs_1_) | copy-start | bytes 6291460
  10.6 54.7 %all-to-all-start = ((bf16[8,128,1024]{2,1,0:T(8,128)(2,1)}), bf16[8,128,1024]{2,1,0:T(8,128)(2,1)S(1)}, u32[]{:S(2)}, u32[]{:S(2)}) async-start(bf16[8,128,1024]{2,1,0:T(8,128)(2,1)} %bitcast.30), calls=%async_computation | async-start | bytes 4194304 | tf_op jit(solution)/shard_map/all_to_all | solution.py:579
  41.7 3.8 %collective-permute-start.3 = (bf16[512,1536]{1,0:T(8,128)(2,1)}, bf16[512,1536]{1,0:T(8,128)(2,1)}, u32[]{:S(2)}, u32[]{:S(2)}) collective-permute-start(bf16[512,1536]{1,0:T(8,128)(2,1)} %collective-permute-done.1.refs_1_), channel_id=1, source_target_pairs={{0,1},{1,0},{2,3},{3,2},{4,5},{5,4},{6,7},{7,6},{8,9},{9,8},{10,11... | collective-permute-start | bytes 4718600 | tf_op jit(solution)/shard_map/ppermute | solution.py:523
  41.7 14.3 %collective-permute-start.2 = (bf16[512,512]{1,0:T(8,128)(2,1)S(1)}, bf16[512,512]{1,0:T(8,128)(2,1)S(1)}, u32[]{:S(2)}, u32[]{:S(2)}) collective-permute-start(bf16[512,512]{1,0:T(8,128)(2,1)S(1)} %slice.6), channel_id=1, source_target_pairs={{0,2},{1,3},{2,0},{3,1},{4,6},{5,7},{6,4},{7,5},{8,10},{9,11},{10,... | collective-permute-start | bytes 1572872 | tf_op jit(solution)/shard_map/ppermute | solution.py:523
  56.0 1.9 copy-start.5
  56.0 1.9 collective-permute-start.4
  57.9 0.8 copy-start.6
  65.3 1.4 copy-start.2
  65.3 7.6 %copy-start.8 = (s32[8]{0:T(128)S(1)}, s32[8]{0:T(128)}, u32[]{:S(2)}) copy-start(s32[8]{0:T(128)} %param.13) | copy-start | bytes 100
  66.6 54.6 %all-to-all-start.1 = ((bf16[8,128,1024]{2,1,0:T(8,128)(2,1)}), bf16[8,128,1024]{2,1,0:T(8,128)(2,1)S(1)}, u32[]{:S(2)}, u32[]{:S(2)}) async-start(bf16[8,128,1024]{2,1,0:T(8,128)(2,1)} %bitcast.29), calls=%async_computation.1 | async-start | bytes 4194304 | tf_op jit(solution)/shard_map/all_to_all | solution.py:579
  121.2 1.3 copy-start.1
  130.9 19.7 %all-to-all-start.2 = ((f32[8,16,1152]{2,1,0:T(8,128)}), f32[8,16,1152]{2,1,0:T(8,128)S(1)}, u32[]{:S(2)}, u32[]{:S(2)}) async-start(f32[8,16,1152]{2,1,0:T(8,128)} %get-tuple-element.29), calls=%async_computation.2 | async-start | bytes 1179648 | tf_op jit(solution)/shard_map/all_to_all | solution.py:618
  150.6 0.8 copy-start.3
  160.6 52.1 %all-to-all-start.3 = ((bf16[8,128,1024]{2,1,0:T(8,128)(2,1)}), bf16[8,128,1024]{2,1,0:T(8,128)(2,1)S(1)}, u32[]{:S(2)}, u32[]{:S(2)}) async-start(bf16[8,128,1024]{2,1,0:T(8,128)(2,1)} %bitcast.33), calls=%async_computation.3 | async-start | bytes 4194304 | tf_op jit(solution)/shard_map/all_to_all | solution.py:579
  164.2 48.4 %copy-start = (s32[128]{0:T(128)S(1)}, s32[128]{0:T(128)}, u32[]{:S(2)}) copy-start(s32[128]{0:T(128)} %reshape.180.lists_ref.refs_0_) | copy-start | bytes 1540

commit v3 on v2

--- a/solution.py
+++ b/solution.py
@@ -13,6 +13,7 @@
 NEIGH = 2
 LANES = 128
 HEAD_CHUNKS = 1
+STEPS = 2
 F32 = jnp.float32
 BF16 = jnp.bfloat16
 
@@ -25,10 +26,11 @@
 
 
 def slot_of_place(lists_ref, base, place, entries_here, slot_cap):
-    owner = lists_ref[base + place] // entries_here
+    owner = lists_ref[base + place // NEIGH, place % NEIGH] // entries_here
     rank = 0
     for earlier in range(place):
-        rank = rank + jnp.where(lists_ref[base + earlier] // entries_here == owner, 1, 0)
+        named = lists_ref[base + earlier // NEIGH, earlier % NEIGH]
+        rank = rank + jnp.where(named // entries_here == owner, 1, 0)
     return owner * slot_cap + rank
 
 
@@ -65,7 +67,7 @@
         copy.wait()
 
 
-def place_rows(rows, lists_flat, my_index, n_seq, slot_cap, entries_here):
+def place_rows(rows, lists, my_index, n_seq, slot_cap, entries_here):
     tok_rows, cols = rows.shape
     places = tok_rows // BLOCK * NEIGH
     slots = n_seq * slot_cap
@@ -73,7 +75,7 @@
     def body(lists_ref, index_ref, rows_ref, out_ref, zero_ref, sems):
         place_copies(
             lists_ref,
-            index_ref[0] * places,
+            index_ref[0] * (places // NEIGH),
             rows_ref,
             [out_ref],
             zero_ref,
@@ -98,7 +100,7 @@
         ],
         name="place_rows",
         **vmem_params(moved=2 * slots * BLOCK * cols * 2, mib=60),
-    )(lists_flat, my_index, rows)
+    )(lists, my_index, rows)
 
 
 def add_product(total, parts, weight, sources, placing=None):
@@ -108,14 +110,14 @@
     cuts = range(width // unit)
     first_units = [source * (feats // unit) + at // unit for source, at in sources]
     cols = weight.shape[0]
-    step_cols = min(256, cols)
+    step_cols = cols // (2 * len(parts)) if len(parts) < 3 else min(256, cols)
     steps = cols // step_cols
     places = tok_rows // BLOCK * NEIGH
     before = [] if total is None else [total]
     if placing is None:
         chunks = 1
     else:
-        lists_flat, my_index, n_seq, slot_cap, entries_here, chunks = placing
+        lists, my_index, n_seq, slot_cap, entries_here, chunks = placing
         slots = n_seq * slot_cap
 
     def body(source_ref, *refs):
@@ -148,7 +150,7 @@
             lists_ref, index_ref = place_refs
             place_copies(
                 lists_ref,
-                index_ref[0] * places,
+                index_ref[0] * (places // NEIGH),
                 low_ref,
                 out_refs,
                 zero_ref,
@@ -178,7 +180,7 @@
             pltpu.VMEM((BLOCK, chunk_cols), BF16),
             pltpu.SemaphoreType.DMA((chunks, max(slots, places))),
         ]
-        extra = [lists_flat, my_index]
+        extra = [lists, my_index]
         in_specs = [pl.BlockSpec(memory_space=pltpu.SMEM)] * 2 + in_specs
     return pl.pallas_call(
         body,
@@ -202,7 +204,7 @@
 
 
 def join_places(
-    chunk, chunks, back, before, lists_flat, my_index, n_seq, slot_cap, entries_here, blocks_here
+    chunk, chunks, back, before, lists, my_index, n_seq, slot_cap, entries_here, blocks_here
 ):
     slots, _, cols = back.shape
     places = blocks_here * NEIGH
@@ -210,7 +212,7 @@
 
     def body(lists_ref, index_ref, back_ref, *refs):
         out_ref = refs[-1]
-        base = index_ref[0] * places
+        base = index_ref[0] * (places // NEIGH)
         for block in range(blocks_here):
             total = 0.0
             for neighbour in range(NEIGH):
@@ -234,7 +236,7 @@
         input_output_aliases={3: 0} if kept else {},
         name="join_places",
         **vmem_params(moved=3 * slots * BLOCK * cols),
-    )(lists_flat, my_index, back, *kept)
+    )(lists, my_index, back, *kept)
 
 
 def lane_parts(total):
@@ -263,13 +265,13 @@
 TN = (((0,), (0,)), ((), ()))
 
 
-def local_softmax(query_rows, keys, entry_lanes):
+def local_softmax(query_rows, keys, values, entry_lanes):
     rows, cols = query_rows.shape
     heads = cols // HEAD
     key_rows = keys.shape[0]
     scale = 1.0 / math.sqrt(HEAD)
 
-    def body(query_ref, key_ref, entry_ref, weight_ref, lse_ref):
+    def body(query_ref, key_ref, value_ref, entry_ref, weight_ref, lse_ref, seen_ref, mean_ref):
         head = pl.program_id(0)
         for part in lane_parts(rows):
             entry = entry_ref[:, part]
@@ -280,28 +282,43 @@
             top = jnp.max(scores, axis=0, keepdims=True)
             raised = jnp.exp(scores - top)
             total = jnp.sum(raised, axis=0, keepdims=True)
-            weight_ref[0, :, part] = raised / total
+            weights = raised / total
+            weight_ref[0, :, part] = weights
             lse_ref[pl.ds(head, 1), part] = top + jnp.log(total)
-
+            wide = spread_entry(weights, entry, key_rows // LANES)
+            seen_ref[part, :] = lax.dot_general(
+                wide, value_ref[...], TN, preferred_element_type=F32
+            )
+            mean_ref[part, :] = lax.dot_general(
+                wide, key_ref[...], TN, preferred_element_type=F32
+            ).astype(BF16)
+
+    column = pl.BlockSpec((rows, HEAD), lambda h: (0, h))
+    entry_column = pl.BlockSpec((key_rows, HEAD), lambda h: (0, h))
     return pl.pallas_call(
         body,
         grid=(heads,),
         out_shape=(
             jax.ShapeDtypeStruct((heads, LANES, rows), F32),
             jax.ShapeDtypeStruct((heads, rows), F32),
+            jax.ShapeDtypeStruct((rows, cols), F32),
+            jax.ShapeDtypeStruct((rows, cols), BF16),
         ),
         in_specs=[
             pl.BlockSpec((rows, HEAD), lambda h: (0, h)),
-            pl.BlockSpec((key_rows, HEAD), lambda h: (0, h)),
+            entry_column,
+            entry_column,
             pl.BlockSpec((1, rows), lambda h: (0, 0)),
         ],
         out_specs=(
             pl.BlockSpec((1, LANES, rows), lambda h: (h, 0, 0)),
             pl.BlockSpec((heads, rows), lambda h: (0, 0)),
+            column,
+            column,
         ),
         name="local_softmax",
         **vmem_params(moved=1, mib=60),
-    )(query_rows, keys, entry_lanes)
+    )(query_rows, keys, values, entry_lanes)
 
 
 def partner_lanes(partner_ref, all_ref, out_ref, slots):
@@ -323,14 +340,15 @@
 
 def live_lanes(partner_ref, all_ref, out_ref, slots, rows):
     lane = lax.broadcasted_iota(jnp.int32, (1, LANES), 1)
+    row = lax.broadcasted_iota(jnp.int32, (all_ref.shape[1], LANES), 0)
     for group in range(slots // 2):
         own, other = [], []
         for half in range(2):
             slot = group * 2 + half
             reader, place = partner_ref[2, slot], partner_ref[3, slot]
-            counts = all_ref[reader, 0:1, rows:]
+            counts = all_ref[reader, :, rows:]
             count = jnp.sum(
-                jnp.where(lane == place // NEIGH, counts, 0.0), axis=1, keepdims=True
+                jnp.where(row == place // NEIGH, counts, 0.0), axis=0, keepdims=True
             )
             at = (place % NEIGH).astype(F32)
             filled = partner_ref[4, slot] > 0
@@ -341,181 +359,204 @@
         out_ref[1:2, part] = jnp.where(lane < BLOCK, other[0], other[1])
 
 
-def weight_grads(n_seq, weights, lse, grad_rows, values, entry_lanes, count_lanes):
-    heads, _, rows = weights.shape
-    value_rows = values.shape[0]
-
-    def body(
-        weight_ref, lse_ref, grad_ref, value_ref, entry_ref, count_ref, slope_ref, all_ref, told_ref
-    ):
-        head = pl.program_id(0)
-
-        @pl.when(head == 0)
+def head_columns(heads, cols):
+    row = lax.broadcasted_iota(jnp.int32, (heads, cols), 0)
+    column = lax.broadcasted_iota(jnp.int32, (heads, cols), 1)
+    return jnp.where(row == column // HEAD, 1.0, 0.0).astype(BF16)
+
+
+def row_dots(n_seq, lse, seen, grad_rows, count_lanes):
+    heads, rows = lse.shape
+    cols = seen.shape[1]
+    step_rows = rows // STEPS
+    steps = rows // step_rows
+
+    def body(lse_ref, seen_ref, grad_ref, count_ref, all_ref, told_ref):
+        step = pl.program_id(0)
+
+        @pl.when(step == 0)
         def _():
             told_ref[:heads, :rows] = lse_ref[...]
-            told_ref[:, rows:] = jnp.broadcast_to(count_ref[...], (2 * heads, LANES))
-
-        for part in lane_parts(rows):
-            slope = lax.dot_general(
-                value_ref[...], grad_ref[part, :], NT, preferred_element_type=F32
-            )
-            slope = pick_entry(slope, entry_ref[:, part])
-            slope_ref[0, :, part] = slope
-            told_ref[pl.ds(heads + head, 1), part] = jnp.sum(
-                weight_ref[0, :, part] * slope, axis=0, keepdims=True
-            )
-
-        @pl.when(head == heads - 1)
+            told_ref[:, rows:] = count_ref[...]
+
+        terms = grad_ref[...].astype(F32) * seen_ref[...]
+        high = terms.astype(BF16)
+        low = (terms - high.astype(F32)).astype(BF16)
+        of_head = head_columns(heads, cols)
+        at = pl.ds(pl.multiple_of(step * step_rows, step_rows), step_rows)
+        told_ref[heads:, at] = sum(
+            lax.dot_general(of_head, part, NT, preferred_element_type=F32) for part in (high, low)
+        )
+
+        @pl.when(step == steps - 1)
         def _():
             for device in range(n_seq):
                 all_ref[device] = told_ref[...]
 
     return pl.pallas_call(
         body,
+        grid=(steps,),
+        out_shape=jax.ShapeDtypeStruct((n_seq, 2 * heads, rows + LANES), F32),
+        in_specs=[
+            pl.BlockSpec((heads, rows), lambda i: (0, 0)),
+            pl.BlockSpec((step_rows, cols), lambda i: (i, 0)),
+            pl.BlockSpec((step_rows, cols), lambda i: (i, 0)),
+            pl.BlockSpec((2 * heads, LANES), lambda i: (0, 0)),
+        ],
+        out_specs=pl.BlockSpec((n_seq, 2 * heads, rows + LANES), lambda i: (0, 0, 0)),
+        scratch_shapes=[pltpu.VMEM((2 * heads, rows + LANES), F32)],
+        name="row_dots",
+        **vmem_params(moved=1, mib=60),
+    )(lse, seen, grad_rows, count_lanes)
+
+
+def slope_terms(weights, told, grad_rows, keys, values, entry_lanes):
+    heads, _, rows = weights.shape
+    cols = heads * HEAD
+    key_rows = keys.shape[0]
+
+    def body(weight_ref, told_ref, grad_ref, key_ref, value_ref, entry_ref, out_ref):
+        head = pl.program_id(0)
+        for part in lane_parts(rows):
+            entry = entry_ref[:, part]
+            slope = lax.dot_general(
+                value_ref[...], grad_ref[part, :], NT, preferred_element_type=F32
+            )
+            dot = told_ref[0, pl.ds(heads + head, 1), part]
+            terms = weight_ref[0, :, part] * (pick_entry(slope, entry) - dot)
+            wide = spread_entry(terms, entry, key_rows // LANES)
+            out_ref[part, :] = lax.dot_general(
+                wide, key_ref[...], TN, preferred_element_type=F32
+            ).astype(BF16)
+
+    column = pl.BlockSpec((rows, HEAD), lambda h: (0, h))
+    entry_column = pl.BlockSpec((key_rows, HEAD), lambda h: (0, h))
+    return pl.pallas_call(
+        body,
         grid=(heads,),
-        out_shape=(
-            jax.ShapeDtypeStruct((heads, LANES, rows), F32),
-            jax.ShapeDtypeStruct((n_seq, 2 * heads, rows + LANES), F32),
-        ),
+        out_shape=jax.ShapeDtypeStruct((rows, cols), BF16),
         in_specs=[
             pl.BlockSpec((1, LANES, rows), lambda h: (h, 0, 0)),
-            pl.BlockSpec((heads, rows), lambda h: (0, 0)),
+            pl.BlockSpec((1,) + told.shape[1:], lambda h: (0, 0, 0)),
             pl.BlockSpec((rows, HEAD), lambda h: (0, h)),
-            pl.BlockSpec((value_rows, HEAD), lambda h: (0, h)),
+            entry_column,
+            entry_column,
             pl.BlockSpec((1, rows), lambda h: (0, 0)),
-            pl.BlockSpec((1, LANES), lambda h: (0, 0)),
-        ],
-        out_specs=(
-            pl.BlockSpec((1, LANES, rows), lambda h: (h, 0, 0)),
-            pl.BlockSpec((n_seq, 2 * heads, rows + LANES), lambda h: (0, 0, 0)),
-        ),
-        scratch_shapes=[pltpu.VMEM((2 * heads, rows + LANES), F32)],
-        name="weight_grads",
+        ],
+        out_specs=column,
+        name="slope_terms",
         **vmem_params(moved=1, mib=60),
-    )(weights, lse, grad_rows, values, entry_lanes, count_lanes)
-
-
-def score_grads(weights, slope, all_told, my_index, partner, keys, entry_lanes):
-    here, _, rows = weights.shape
-    key_rows = keys.shape[0]
+    )(weights, told, grad_rows, keys, values, entry_lanes)
+
+
+def query_terms_of(terms, mean, all_told, my_index, partner):
+    rows, cols = terms.shape
+    heads = cols // HEAD
     slots = rows // BLOCK
+    step_rows = rows // STEPS
     scale = 1.0 / math.sqrt(HEAD)
 
     def body(
-        partner_ref,
-        index_ref,
-        weight_ref,
-        slope_ref,
-        all_ref,
-        key_ref,
-        entry_ref,
-        share_ref,
-        low_ref,
-        query_ref,
-        told_ref,
-        other_ref,
-        live_ref,
+        partner_ref, index_ref, all_ref, term_ref, mean_ref, stat_ref, out_ref, other_ref, live_ref, more_ref
     ):
-        head = pl.program_id(0)
-
-        @pl.when(head == 0)
+        step = pl.program_id(0)
+
+        @pl.when(step == 0)
         def _():
-            told_ref[...] = all_ref[index_ref[0], :, :rows]
             partner_lanes(partner_ref, all_ref, other_ref, slots)
             live_lanes(partner_ref, all_ref, live_ref, slots, rows)
-
-        for part in lane_parts(rows):
-            entry = entry_ref[:, part]
-            apart = other_ref[pl.ds(head, 1), part] - told_ref[pl.ds(head, 1), part]
-            odds = jnp.where(live_ref[1:2, part] > 0.0, jnp.exp(apart), 0.0)
-            share = jnp.where(live_ref[0:1, part] > 0.0, 1.0 / (1.0 + odds), 0.0)
-            rest = jnp.where(live_ref[1:2, part] > 0.0, 1.0 / (1.0 + jnp.exp(-apart)), 0.0)
-            dot = (
-                share * told_ref[pl.ds(here + head, 1), part]
-                + rest * other_ref[pl.ds(here + head, 1), part]
-            )
-            share_ref[pl.ds(head, 1), part] = share
-            joint = weight_ref[0, :, part] * share
-            low = joint * (slope_ref[0, :, part] - dot)
-            low_ref[0, :, part] = low.astype(BF16)
-            wide = spread_entry(low, entry, key_rows // LANES)
-            query = lax.dot_general(wide, key_ref[...], TN, preferred_element_type=F32)
-            query_ref[part, :] = (query * scale).astype(BF16)
-
-    return pl.pallas_call(
-        body,
-        grid=(here,),
+            own = all_ref[index_ref[0], :, :rows]
+            apart = other_ref[:heads, :] - own[:heads, :]
+            own_live, other_live = live_ref[0:1, :] > 0.0, live_ref[1:2, :] > 0.0
+            odds = jnp.where(other_live, jnp.exp(apart), 0.0)
+            share = jnp.where(own_live, 1.0 / (1.0 + odds), 0.0)
+            rest = jnp.where(other_live, 1.0 / (1.0 + jnp.exp(-apart)), 0.0)
+            more = rest * (other_ref[heads:, :] - own[heads:, :])
+            stat_ref[:heads, :] = share
+            stat_ref[heads:, :] = own[heads:, :] + more
+            more_ref[...] = more
+
+        at = pl.ds(pl.multiple_of(step * step_rows, step_rows), step_rows)
+        of_head = head_columns(heads, cols)
+
+        def spread(rows_of_heads):
+            high = rows_of_heads.astype(BF16)
+            low = (rows_of_heads - high.astype(F32)).astype(BF16)
+            return sum(
+                lax.dot_general(part, of_head, TN, preferred_element_type=F32)
+                for part in (high, low)
+            )
+
+        share, more = spread(stat_ref[:heads, at]), spread(more_ref[:, at])
+        query = share * (term_ref[...].astype(F32) - more * mean_ref[...].astype(F32))
+        out_ref[...] = (query * scale).astype(BF16)
+
+    block = pl.BlockSpec((step_rows, cols), lambda i: (i, 0))
+    return pl.pallas_call(
+        body,
+        grid=(rows // step_rows,),
         out_shape=(
-            jax.ShapeDtypeStruct((here, rows), F32),
-            jax.ShapeDtypeStruct((here, LANES, rows), BF16),
-            jax.ShapeDtypeStruct((rows, here * HEAD), BF16),
+            jax.ShapeDtypeStruct((2 * heads, rows), F32),
+            jax.ShapeDtypeStruct((rows, cols), BF16),
         ),
         in_specs=[
             pl.BlockSpec(memory_space=pltpu.SMEM),
             pl.BlockSpec(memory_space=pltpu.SMEM),
-            pl.BlockSpec((1, LANES, rows), lambda h: (h, 0, 0)),
-            pl.BlockSpec((1, LANES, rows), lambda h: (h, 0, 0)),
-            pl.BlockSpec(all_told.shape, lambda h: (0, 0, 0)),
-            pl.BlockSpec((key_rows, HEAD), lambda h: (0, h)),
-            pl.BlockSpec((1, rows), lambda h: (0, 0)),
-        ],
-        out_specs=(
-            pl.BlockSpec((here, rows), lambda h: (0, 0)),
-            pl.BlockSpec((1, LANES, rows), lambda h: (h, 0, 0)),
-            pl.BlockSpec((rows, HEAD), lambda h: (0, h)),
-        ),
+            pl.BlockSpec(all_told.shape, lambda i: (0, 0, 0)),
+            pl.BlockSpec((step_rows, cols), lambda i: (i, 0)),
+            pl.BlockSpec((step_rows, cols), lambda i: (i, 0)),
+        ],
+        out_specs=(pl.BlockSpec((2 * heads, rows), lambda i: (0, 0)), block),
         scratch_shapes=[
-            pltpu.VMEM((2 * here, rows), F32),
-            pltpu.VMEM((2 * here, rows), F32),
+            pltpu.VMEM((2 * heads, rows), F32),
             pltpu.VMEM((2, rows), F32),
-        ],
-        name="score_grads",
+            pltpu.VMEM((heads, rows), F32),
+        ],
+        name="query_terms",
         **vmem_params(moved=1, mib=60),
-    )(partner, my_index, weights, slope, all_told, keys, entry_lanes)
-
-
-def entry_grads(chunk, weights, share, low, query_rows, grad_rows, entry_lanes, entry_rows):
-    _, _, rows = weights.shape
-    here = low.shape[0]
-    first = chunk * here
+    )(partner, my_index, all_told, terms, mean)
+
+
+def entry_grads(weights, stat, query_rows, grad_rows, values, entry_lanes):
+    heads, _, rows = weights.shape
+    cols = heads * HEAD
+    entry_rows = values.shape[0]
     scale = 1.0 / math.sqrt(HEAD)
 
-    def body(weight_ref, share_ref, low_ref, query_ref, grad_ref, entry_ref, key_ref, value_ref):
+    def body(weight_ref, stat_ref, query_ref, grad_ref, value_ref, entry_ref, key_out, value_out):
         head = pl.program_id(0)
         key_sum = jnp.zeros((entry_rows, HEAD), F32)
         value_sum = jnp.zeros((entry_rows, HEAD), F32)
         for part in lane_parts(rows):
             entry = entry_ref[:, part]
-            joint = weight_ref[0, :, part] * share_ref[pl.ds(head, 1), part]
+            grad = grad_ref[part, :]
+            joint = weight_ref[0, :, part] * stat_ref[pl.ds(head, 1), part]
+            slope = lax.dot_general(value_ref[...], grad, NT, preferred_element_type=F32)
+            low = joint * (pick_entry(slope, entry) - stat_ref[pl.ds(heads + head, 1), part])
             wide = spread_entry(joint, entry, entry_rows // LANES)
-            value_sum += lax.dot_general(wide, grad_ref[part, :], NN, preferred_element_type=F32)
-            wide = spread_entry(low_ref[0, :, part].astype(F32), entry, entry_rows // LANES)
+            value_sum += lax.dot_general(wide, grad, NN, preferred_element_type=F32)
+            wide = spread_entry(low, entry, entry_rows // LANES)
             key_sum += lax.dot_general(wide, query_ref[part, :], NN, preferred_element_type=F32)
-        key_ref[...] = (key_sum * scale).astype(BF16)
-        value_ref[...] = value_sum.astype(BF16)
-
-    return pl.pallas_call(
-        body,
-        grid=(here,),
-        out_shape=(
-            jax.ShapeDtypeStruct((entry_rows, here * HEAD), BF16),
-            jax.ShapeDtypeStruct((entry_rows, here * HEAD), BF16),
-        ),
+        key_out[...] = (key_sum * scale).astype(BF16)
+        value_out[...] = value_sum.astype(BF16)
+
+    entry_column = pl.BlockSpec((entry_rows, HEAD), lambda h: (0, h))
+    return pl.pallas_call(
+        body,
+        grid=(heads,),
+        out_shape=[jax.ShapeDtypeStruct((entry_rows, cols), BF16)] * 2,
         in_specs=[
-            pl.BlockSpec((1, LANES, rows), lambda h: (first + h, 0, 0)),
-            pl.BlockSpec((here, rows), lambda h: (0, 0)),
             pl.BlockSpec((1, LANES, rows), lambda h: (h, 0, 0)),
-            pl.BlockSpec((rows, HEAD), lambda h: (0, first + h)),
+            pl.BlockSpec((2 * heads, rows), lambda h: (0, 0)),
             pl.BlockSpec((rows, HEAD), lambda h: (0, h)),
+            pl.BlockSpec((rows, HEAD), lambda h: (0, h)),
+            pl.BlockSpec((entry_rows, HEAD), lambda h: (0, h)),
             pl.BlockSpec((1, rows), lambda h: (0, 0)),
         ],
-        out_specs=(
-            pl.BlockSpec((entry_rows, HEAD), lambda h: (0, h)),
-            pl.BlockSpec((entry_rows, HEAD), lambda h: (0, h)),
-        ),
+        out_specs=[entry_column] * 2,
         name="entry_grads",
         **vmem_params(moved=1, mib=60),
-    )(weights, share, low, query_rows, grad_rows, entry_lanes)
+    )(weights, stat, query_rows, grad_rows, values, entry_lanes)
 
 
 def swap(value, axis, bits):
@@ -569,7 +610,7 @@
     slot_cap = (places + n_seq - 1) // n_seq
     rows = n_seq * slot_cap * BLOCK
     feats = out_grad.shape[1]
-    lists_flat = retrieval.reshape(-1).astype(jnp.int32)
+    lists = retrieval
     index_arr = my_index.astype(jnp.int32).reshape(1)
     key_rows = keys.reshape(entries_here * nbr_rows, head_cols)
     value_rows = values.reshape(entries_here * nbr_rows, head_cols)
@@ -581,50 +622,42 @@
         ).reshape(rows, cols)
 
     far_bits = list(range(2, n_mp, 2))
-    cut = feats * 3 // 4
     tie = lax.optimization_barrier
-
-    def sources(at):
-        return [(my_mp ^ bits ^ side, at) for bits in far_bits for side in (0, 1)]
-
-    def both_cores(pieces):
-        return [x for piece in pieces for x in (piece, swap(piece, "mp", 1))]
-
+    far = [swap(out_grad, "mp", bits) for bits in far_bits]
     near = swap(out_grad, "mp", 1)
-    first = [swap(out_grad[:, :cut], "mp", bits) for bits in far_bits]
-    near, outgoing = tie((near, queries))
-    query_places = place_rows(outgoing, lists_flat, index_arr, n_seq, slot_cap, entries_here)
+    query_places = place_rows(queries, lists, index_arr, n_seq, slot_cap, entries_here)
     query_slots = exchange(query_places)
     entry_lanes, partner = owner_tables(
         retrieval.reshape(n_seq, places), my_index, entries_here, slot_cap
     )
 
-    placing = (lists_flat, index_arr, n_seq, slot_cap, entries_here, HEAD_CHUNKS)
+    placing = (lists, index_arr, n_seq, slot_cap, entries_here, HEAD_CHUNKS)
     (grad_sum,) = add_product(None, [out_grad, near], out_weight, [(my_mp, 0), (my_mp ^ 1, 0)])
-    second, first, grad_sum = tie((out_grad[:, cut:], first, grad_sum))
-    second = [swap(second, "mp", bits) for bits in far_bits]
-    (grad_sum,) = add_product(grad_sum, both_cores(first), out_weight, sources(0))
-    second, grad_sum = tie((second, grad_sum))
-    grad_sum = add_product(grad_sum, both_cores(second), out_weight, sources(cut), placing)
+    far, grad_sum = tie((far, grad_sum))
+    beside = [swap(part, "mp", 1) for part in far]
+    (grad_sum,) = add_product(grad_sum, far, out_weight, [(my_mp ^ bits, 0) for bits in far_bits])
+    beside, grad_sum = tie((beside, grad_sum))
+    grad_sum = add_product(
+        grad_sum, beside, out_weight, [(my_mp ^ bits ^ 1, 0) for bits in far_bits], placing
+    )
     grad_places = grad_sum
 
-    count_lanes = jnp.pad(counts.astype(F32), (0, LANES - blocks_here))[None]
-    weights, lse = local_softmax(query_slots, key_rows, entry_lanes)
-
+    count_lanes = jnp.pad(counts.astype(F32), (0, max(0, 2 * head_cols // HEAD - blocks_here)))
+    count_lanes = jnp.broadcast_to(count_lanes[:, None], (count_lanes.shape[0], LANES))
+    weights, lse, seen, mean = local_softmax(query_slots, key_rows, value_rows, entry_lanes)
     grad_slots = exchange(grad_places[0])
-    slope, told = weight_grads(
-        n_seq, weights, lse, grad_slots, value_rows, entry_lanes, count_lanes
-    )
+    weights, lse, seen, mean, grad_slots = tie((weights, lse, seen, mean, grad_slots))
+    told = row_dots(n_seq, lse, seen, grad_slots, count_lanes)
     all_told = lax.all_to_all(told, "seq", 0, 0, tiled=True)
-    share, low, query_terms = score_grads(
-        weights, slope, all_told, index_arr, partner, key_rows, entry_lanes
-    )
+    terms = slope_terms(weights, told, grad_slots, key_rows, value_rows, entry_lanes)
+    all_told, terms = tie((all_told, terms))
+    stat, query_terms = query_terms_of(terms, mean, all_told, index_arr, partner)
     back = exchange(query_terms).reshape(-1, BLOCK, head_cols)
     query_grad = join_places(
-        0, 1, back, None, lists_flat, index_arr, n_seq, slot_cap, entries_here, blocks_here
+        0, 1, back, None, lists, index_arr, n_seq, slot_cap, entries_here, blocks_here
     )
     key_grad, value_grad = entry_grads(
-        0, weights, share, low, query_slots, grad_slots, entry_lanes, key_rows.shape[0]
+        weights, stat, query_slots, grad_slots, value_rows, entry_lanes
     )
     key_grad = key_grad.reshape(keys.shape)
     value_grad = value_grad.reshape(values.shape)

time: 216 us -> 207 us (0.958)
  waiting for transfers between devices: 110 us -> 102 us
  Pallas kernels: 65.1 us -> 72 us
  local copies, waits for them, and re-layouts: 12.1 us -> 7.68 us
    all_to_all x1, waiting for transfers between devices: 14.6 us -> 4.36 us  [on_device(): all_told = lax.all_to_all(told, 'seq', 0, 0, tiled=True)]
    ppermute x5 -> x3, waiting for transfers between devices: 17.2 us -> 25.8 us  [swap(): return lax.ppermute(value, axis, [(i, i ^ bits) for i in range(size)])]
    all_to_all x3, waiting for transfers between devices: 78.3 us -> 72.3 us  [exchange(): lax.all_to_all(slot_rows.reshape(n_seq, slot_cap * BLOCK, cols), 'seq', 0...]
    pallas_call x1, Pallas kernels: 7.56 us -> 13.4 us  [local_softmax(): pl.pallas_call(body, grid=(heads,), out_shape=(jax.ShapeDtypeStruct((head...]
    pallas_call x3 -> x4, Pallas kernels: 26 us -> 30.3 us  [the longest x1 10.3 us: slope_terms(): pl.pallas_call(body, grid=(heads,), out_shape=jax.ShapeDtypeStruct((rows,...]
    slice x2 -> x0, local copies, waits for them, and re-layouts: 3.72 us -> none  [the longest x1 2.65 us: on_device(): first = [swap(out_grad[:, :cut], 'mp', bits) for bits in far_bits]]
    pallas_call x3, Pallas kernels: 26.1 us -> 23 us  [add_product(): pl.pallas_call(body, grid_spec=pltpu.PrefetchScalarGridSpec(num_scalar_pr...]
    ppermute x5 -> x3, starting transfers between devices: 4.77 us -> 3.09 us  [swap(): return lax.ppermute(value, axis, [(i, i ^ bits) for i in range(size)])]
  transfers between devices with their start and end apart: 9 -> 7, of which waited for: 7 -> 4; matrix products, arithmetic and copies ran while one was open for 5% -> 3% of each run, Pallas kernels for 21% -> 29%
where the time goes in v3:
time: 207 us; the launch traced here: 206 us
  waiting for transfers between devices  102 us (49%)
  Pallas kernels  72 us (35%)
  starting transfers between devices  22.4 us (11%)
  local copies, waits for them, and re-layouts  7.68 us (4%)
    all_to_all x3, waiting for transfers between devices, exchange(): lax.all_to_all(slot_rows.reshape(n_seq, slot_cap * BLOCK, cols), 'seq', 0...  72.3 us
    ppermute x3, waiting for transfers between devices, swap(): return lax.ppermute(value, axis, [(i, i ^ bits) for i in range(size)])  25.8 us
    pallas_call x3, Pallas kernels, add_product(): pl.pallas_call(body, grid_spec=pltpu.PrefetchScalarGridSpec(num_scalar_pr...  23 us
    all_to_all x3, starting transfers between devices, exchange(): lax.all_to_all(slot_rows.reshape(n_seq, slot_cap * BLOCK, cols), 'seq', 0...  15.6 us
    pallas_call x1, Pallas kernels, local_softmax(): pl.pallas_call(body, grid=(heads,), out_shape=(jax.ShapeDtypeStruct((head...  13.4 us
    pallas_call x1, Pallas kernels, slope_terms(): pl.pallas_call(body, grid=(heads,), out_shape=jax.ShapeDtypeStruct((rows,...  10.3 us
    pallas_call x1, Pallas kernels, entry_grads(): pl.pallas_call(body, grid=(heads,), out_shape=[jax.ShapeDtypeStruct((entr...  9.53 us
    pallas_call x1, Pallas kernels, query_terms_of(): pl.pallas_call(body, grid=(rows // step_rows,), out_shape=(jax.ShapeDtype...  6.11 us
  transfers between devices with their start and end apart: 7, of which 4 were waited for; matrix products, arithmetic and copies ran while one was open for 3% of the time, Pallas kernels for 29%

profile of v3, /device:TPU:0, one launch (start us, length us, event | category | flops | bytes accessed | tf_op | source)
XLA Modules:
  0.0 206.5 jit_solution(10930578328493626511)
XLA Ops:
  0.6 0.5 collective-permute-start.1
  1.1 2.6 %collective-permute-start = (bf16[512,2048]{1,0:T(8,128)(2,1)}, bf16[512,2048]{1,0:T(8,128)(2,1)}, u32[]{:S(2)}, u32[]{:S(2)}) collective-permute-start(bf16[512,2048]{1,0:T(8,128)(2,1)} %refs_0_.2), channel_id=1, source_target_pairs={{0,2},{1,3},{2,0},{3,1},{4,6},{5,7},{6,4},{7,5},{8,10},{9,11},{10,... | collective-permute-start | bytes 6291464 | tf_op jit(solution)/shard_map/ppermute | solution.py:564
  3.7 1.4 copy.39.lists_ref.refs_0_
  5.1 2.7 %place_rows.1 = bf16[16,64,1024]{2,1,0:T(8,128)(2,1)} custom-call(s32[64,2]{1,0:T(8,128)} %copy.39.lists_ref.refs_0_, s32[1]{0:T(128)} %bitcast.index_ref.refs_1_, bf16[512,1024]{1,0:T(8,128)(2,1)} %rows_ref.1), custom_call_target="tpu_custom_call" | custom-call | bytes 4194304 | tf_op jit(solution)/shard_map/place_rows/pallas_call | solution.py:88
  7.8 5.9 %all-to-all-start = ((bf16[8,128,1024]{2,1,0:T(8,128)(2,1)}), bf16[8,128,1024]{2,1,0:T(8,128)(2,1)S(1)}, u32[]{:S(2)}, u32[]{:S(2)}) async-start(bf16[8,128,1024]{2,1,0:T(8,128)(2,1)} %bitcast.27), calls=%async_computation | async-start | bytes 4194304 | tf_op jit(solution)/shard_map/all_to_all | solution.py:620
  13.7 0.6 pad_add_fusion.source_ref
  14.3 0.0 collective-permute-done.1.refs_1_
  14.3 10.2 %add_product.3.refs_0_ = f32[512,1024]{1,0:T(8,128)} custom-call(s32[2]{0:T(128)} %pad_add_fusion.source_ref, bf16[512,2048]{1,0:T(8,128)(2,1)} %refs_0_.2, bf16[512,2048]{1,0:T(8,128)(2,1)} %collective-permute-done.1.refs_1_, bf16[1024,8192]{1,0:T(8,128)(2,1)} %refs_4_.1, bf16[1024,8192]{1,0:T(8,128)(2,1)} %refs_4_.1), custom_call_target="tpu_custom_call" | custom-call | bytes 1 | tf_op jit(solution)/shard_map/add_product/pallas_call | solution.py:185
  24.5 25.8 %collective-permute-done.refs_1_ = bf16[512,2048]{1,0:T(8,128)(2,1)} collective-permute-done((bf16[512,2048]{1,0:T(8,128)(2,1)}, bf16[512,2048]{1,0:T(8,128)(2,1)}, u32[]{:S(2)}, u32[]{:S(2)}) %collective-permute-start) | collective-permute-done | bytes 2097184 | tf_op jit(solution)/shard_map/ppermute | solution.py:564
  50.3 0.0 collective-permute-start.2
  50.3 6.2 %add_product.4.refs_2_ = f32[512,1024]{1,0:T(8,128)} custom-call(s32[1]{0:T(128)} %bitcast.11.source_ref, f32[512,1024]{1,0:T(8,128)} %add_product.3.refs_0_, bf16[512,2048]{1,0:T(8,128)(2,1)} %collective-permute-done.refs_1_, bf16[1024,8192]{1,0:T(8,128)(2,1)} %refs_4_.1), custom_call_target="tpu_custom_call" | custom-call | bytes 1 | tf_op jit(solution)/shard_map/add_product/pallas_call | solution.py:185
  56.4 0.0 collective-permute-done.2.refs_3_
  56.4 6.7 %add_product.5 = bf16[16,64,1024]{2,1,0:T(8,128)(2,1)} custom-call(s32[1]{0:T(128)} %bitcast.8.source_ref, s32[64,2]{1,0:T(8,128)} %copy.39.lists_ref.refs_0_, s32[1]{0:T(128)} %bitcast.index_ref.refs_1_, f32[512,1024]{1,0:T(8,128)} %add_product.4.refs_2_, bf16[512,2048]{1,0:T(8,128)(2,1)} %collective-permute-done.2.refs_3_, bf16[1024,8192]{1,0:T(8,128)(2,1)} %refs_4_.1), custom_call_target="tpu_custom_call" | custom-call | bytes 1 | tf_op jit(solution)/shard_map/add_product/pallas_call | solution.py:185
  63.1 0.0 all-to-all-done
  63.1 0.0 copy-start.2
  63.1 0.0 copy-start.4
  63.1 0.0 copy-start
  63.1 0.0 copy-start.5
  63.1 1.3 copy-done.2
  64.5 6.1 %all-to-all-start.1 = ((bf16[8,128,1024]{2,1,0:T(8,128)(2,1)}), bf16[8,128,1024]{2,1,0:T(8,128)(2,1)S(1)}, u32[]{:S(2)}, u32[]{:S(2)}) async-start(bf16[8,128,1024]{2,1,0:T(8,128)(2,1)} %bitcast.26), calls=%async_computation.1 | async-start | bytes 4194304 | tf_op jit(solution)/shard_map/all_to_all | solution.py:620
  70.6 0.0 copy-done.4
  70.6 0.1 reshape.180
  70.7 0.0 copy-done
  70.7 0.1 reshape.179
  70.7 0.0 copy-done.5
  70.8 0.1 copy.27
  70.9 0.1 copy.28
  71.0 0.3 convert_reduce_fusion
  71.2 0.1 copy.30
  71.4 0.1 copy.31
  71.5 0.3 select_reduce_fusion
  71.8 0.1 copy.37
  71.8 0.1 broadcast_in_dim_reshape.4
  71.9 0.1 broadcast_in_dim.77
  72.0 0.7 broadcast_in_dim.78.entry_ref
  72.7 13.4 %local_softmax.1 = (f32[8,128,1024]{2,1,0:T(8,128)}, f32[8,1024]{1,0:T(8,128)}, f32[1024,1024]{1,0:T(8,128)}, bf16[1024,1024]{1,0:T(8,128)(2,1)}) custom-call(bf16[1024,1024]{1,0:T(8,128)(2,1)} %bitcast.24, bf16[256,1024]{1,0:T(8,128)(2,1)} %bitcast.32, bf16[256,1024]{1,0:T(8,128)(2,1)} %bitcast.28, s32[1,1024]{1,0:T(1,128)} %broadcast_in_dim.78.entry_ref), custom_call_target="tpu_custom_call" | custom-call | bytes 1 | tf_op jit(solution)/shard_map/local_softmax/pallas_call | solution.py:298
  86.0 33.4 %all-to-all-done.1 = bf16[8,128,1024]{2,1,0:T(8,128)(2,1)S(1)} async-done(((bf16[8,128,1024]{2,1,0:T(8,128)(2,1)}), bf16[8,128,1024]{2,1,0:T(8,128)(2,1)S(1)}, u32[]{:S(2)}, u32[]{:S(2)}) %all-to-all-start.1) | async-done | bytes 2097184 | tf_op jit(solution)/shard_map/all_to_all | solution.py:620
  119.5 0.0 copy-start.1
  119.5 0.8 broadcast_in_dim.79.count_ref
  120.3 0.5 copy-done.1
  120.8 4.4 %row_dots.1.told_ref = f32[8,16,1152]{2,1,0:T(8,128)} custom-call(f32[8,1024]{1,0:T(8,128)} %get-tuple-element.30.lse_ref, f32[1024,1024]{1,0:T(8,128)} %get-tuple-element.31.seen_ref, bf16[1024,1024]{1,0:T(8,128)(2,1)} %bitcast.21, f32[16,128]{1,0:T(8,128)} %broadcast_in_dim.79.count_ref), custom_call_target="tpu_custom_call" | custom-call | bytes 1 | tf_op jit(solution)/shard_map/row_dots/pallas_call | solution.py:396
  125.2 3.6 %all-to-all-start.2 = ((f32[8,16,1152]{2,1,0:T(8,128)}), f32[8,16,1152]{2,1,0:T(8,128)S(1)}, u32[]{:S(2)}, u32[]{:S(2)}) async-start(f32[8,16,1152]{2,1,0:T(8,128)} %row_dots.1.told_ref), calls=%async_computation.2 | async-start | bytes 1179648 | tf_op jit(solution)/shard_map/all_to_all | solution.py:651
  128.8 0.1 copy.35
  128.9 0.1 stack_reshape.19
  129.0 0.1 copy.34
  129.1 0.1 stack_reshape.18
  129.2 0.1 copy.33
  129.3 0.1 stack_reshape.17
  129.3 0.1 copy.32
  129.4 0.1 stack_reshape.16
  129.5 0.1 copy.29
  129.6 0.1 stack_reshape.15
  129.7 0.6 stack.18.partner_ref
  130.3 10.3 %slope_terms.1.term_ref = bf16[1024,1024]{1,0:T(8,128)(2,1)} custom-call(f32[8,128,1024]{2,1,0:T(8,128)} %get-tuple-element.33.weight_ref, f32[8,16,1152]{2,1,0:T(8,128)} %row_dots.1.told_ref, bf16[1024,1024]{1,0:T(8,128)(2,1)} %bitcast.22, bf16[256,1024]{1,0:T(8,128)(2,1)} %bitcast.33, bf16[256,1024]{1,0:T(8,128)(2,1)} %bitcast.29, ...), custom_call_target="tpu_custom_call" | custom-call | bytes 1 | tf_op jit(solution)/shard_map/slope_terms/pallas_call | solution.py:434
  140.6 4.4 %all-to-all-done.2.all_ref = f32[8,16,1152]{2,1,0:T(8,128)S(1)} async-done(((f32[8,16,1152]{2,1,0:T(8,128)}), f32[8,16,1152]{2,1,0:T(8,128)S(1)}, u32[]{:S(2)}, u32[]{:S(2)}) %all-to-all-start.2) | async-done | bytes 589856 | tf_op jit(solution)/shard_map/all_to_all | solution.py:651
  144.9 0.0 copy-start.3
  144.9 0.8 copy-done.3
  145.8 6.1 %query_terms.1 = (f32[16,1024]{1,0:T(8,128)}, bf16[1024,1024]{1,0:T(8,128)(2,1)}) custom-call(s32[5,16]{1,0:T(8,128)} %stack.18.partner_ref, s32[1]{0:T(128)} %bitcast.index_ref.refs_1_, f32[8,16,1152]{2,1,0:T(8,128)} %copy-done.3, bf16[1024,1024]{1,0:T(8,128)(2,1)} %slope_terms.1.term_ref, bf16[1024,1024]{1,0:T(8,128)(2,1)} %get-tuple-element.36.mean_ref), custom_call_target="tpu_custom_call" | custom-call | bytes 1 | tf_op jit(solution)/shard_map/query_terms/pallas_call | solution.py:495
  151.9 3.6 %all-to-all-start.3 = ((bf16[8,128,1024]{2,1,0:T(8,128)(2,1)}), bf16[8,128,1024]{2,1,0:T(8,128)(2,1)S(1)}, u32[]{:S(2)}, u32[]{:S(2)}) async-start(bf16[8,128,1024]{2,1,0:T(8,128)(2,1)} %bitcast.31), calls=%async_computation.3 | async-start | bytes 4194304 | tf_op jit(solution)/shard_map/all_to_all | solution.py:620
  155.5 9.5 %entry_grads.1 = (bf16[256,1024]{1,0:T(8,128)(2,1)}, bf16[256,1024]{1,0:T(8,128)(2,1)}) custom-call(f32[8,128,1024]{2,1,0:T(8,128)} %get-tuple-element.33.weight_ref, f32[16,1024]{1,0:T(8,128)} %get-tuple-element.38.stat_ref, bf16[1024,1024]{1,0:T(8,128)(2,1)} %bitcast.25, bf16[1024,1024]{1,0:T(8,128)(2,1)} %bitcast.23, bf16[256,1024]{1,0:T(8,128)(2,1)} %bitcast.30, ...), custom_call_target="tpu_custom_call" | custom-call | bytes 1 | tf_op jit(solution)/shard_map/entry_grads/pallas_call | solution.py:544
  165.0 38.9 %all-to-all-done.3 = bf16[8,128,1024]{2,1,0:T(8,128)(2,1)S(1)} async-done(((bf16[8,128,1024]{2,1,0:T(8,128)(2,1)}), bf16[8,128,1024]{2,1,0:T(8,128)(2,1)S(1)}, u32[]{:S(2)}, u32[]{:S(2)}) %all-to-all-start.3) | async-done | bytes 2097184 | tf_op jit(solution)/shard_map/all_to_all | solution.py:620
  203.9 2.6 %join_places.1 = bf16[512,1024]{1,0:T(8,128)(2,1)} custom-call(s32[64,2]{1,0:T(8,128)S(1)} %copy-done, s32[1]{0:T(128)} %bitcast.index_ref.refs_1_, bf16[16,64,1024]{2,1,0:T(8,128)(2,1)S(1)} %bitcast.20), custom_call_target="tpu_custom_call" | custom-call | bytes 3145728 | tf_op jit(solution)/shard_map/join_places/pallas_call | solution.py:225
  (10 shorter events, 0.1 us)
Async XLA Ops:
  0.6 13.7 %collective-permute-start.1 = (bf16[512,2048]{1,0:T(8,128)(2,1)}, bf16[512,2048]{1,0:T(8,128)(2,1)}, u32[]{:S(2)}, u32[]{:S(2)}) collective-permute-start(bf16[512,2048]{1,0:T(8,128)(2,1)} %refs_0_.2), channel_id=1, source_target_pairs={{0,1},{1,0},{2,3},{3,2},{4,5},{5,4},{6,7},{7,6},{8,9},{9,8},{10,11... | collective-permute-start | bytes 6291464 | tf_op jit(solution)/shard_map/ppermute | solution.py:564
  1.1 49.1 %collective-permute-start = (bf16[512,2048]{1,0:T(8,128)(2,1)}, bf16[512,2048]{1,0:T(8,128)(2,1)}, u32[]{:S(2)}, u32[]{:S(2)}) collective-permute-start(bf16[512,2048]{1,0:T(8,128)(2,1)} %refs_0_.2), channel_id=1, source_target_pairs={{0,2},{1,3},{2,0},{3,1},{4,6},{5,7},{6,4},{7,5},{8,10},{9,11},{10,... | collective-permute-start | bytes 6291464 | tf_op jit(solution)/shard_map/ppermute | solution.py:564
  7.8 55.3 %all-to-all-start = ((bf16[8,128,1024]{2,1,0:T(8,128)(2,1)}), bf16[8,128,1024]{2,1,0:T(8,128)(2,1)S(1)}, u32[]{:S(2)}, u32[]{:S(2)}) async-start(bf16[8,128,1024]{2,1,0:T(8,128)(2,1)} %bitcast.27), calls=%async_computation | async-start | bytes 4194304 | tf_op jit(solution)/shard_map/all_to_all | solution.py:620
  50.3 6.2 %collective-permute-start.2 = (bf16[512,2048]{1,0:T(8,128)(2,1)}, bf16[512,2048]{1,0:T(8,128)(2,1)}, u32[]{:S(2)}, u32[]{:S(2)}) collective-permute-start(bf16[512,2048]{1,0:T(8,128)(2,1)} %collective-permute-done.refs_1_), channel_id=1, source_target_pairs={{0,1},{1,0},{2,3},{3,2},{4,5},{5,4},{6,7},{7,6},{8,9},{9,8},{10,11... | collective-permute-start | bytes 6291464 | tf_op jit(solution)/shard_map/ppermute | solution.py:564
  63.1 1.4 copy-start.2
  63.1 7.5 %copy-start.4 = (s32[64,2]{0,1:T(2,128)S(1)}, s32[64,2]{0,1:T(2,128)}, u32[]{:S(2)}) copy-start(s32[64,2]{0,1:T(2,128)} %param.12) | copy-start | bytes 1540
  63.1 7.6 %copy-start = (s32[64,2]{1,0:T(8,128)S(1)}, s32[64,2]{1,0:T(8,128)}, u32[]{:S(2)}) copy-start(s32[64,2]{1,0:T(8,128)} %copy.39.lists_ref.refs_0_) | copy-start | bytes 1540
  63.1 7.6 %copy-start.5 = (s32[8]{0:T(128)S(1)}, s32[8]{0:T(128)}, u32[]{:S(2)}) copy-start(s32[8]{0:T(128)} %param.13) | copy-start | bytes 100
  64.5 55.0 %all-to-all-start.1 = ((bf16[8,128,1024]{2,1,0:T(8,128)(2,1)}), bf16[8,128,1024]{2,1,0:T(8,128)(2,1)S(1)}, u32[]{:S(2)}, u32[]{:S(2)}) async-start(bf16[8,128,1024]{2,1,0:T(8,128)(2,1)} %bitcast.26), calls=%async_computation.1 | async-start | bytes 4194304 | tf_op jit(solution)/shard_map/all_to_all | solution.py:620
  119.5 1.3 copy-start.1
  125.2 19.7 %all-to-all-start.2 = ((f32[8,16,1152]{2,1,0:T(8,128)}), f32[8,16,1152]{2,1,0:T(8,128)S(1)}, u32[]{:S(2)}, u32[]{:S(2)}) async-start(f32[8,16,1152]{2,1,0:T(8,128)} %row_dots.1.told_ref), calls=%async_computation.2 | async-start | bytes 1179648 | tf_op jit(solution)/shard_map/all_to_all | solution.py:651
  144.9 0.8 copy-start.3
  151.9 52.1 %all-to-all-start.3 = ((bf16[8,128,1024]{2,1,0:T(8,128)(2,1)}), bf16[8,128,1024]{2,1,0:T(8,128)(2,1)S(1)}, u32[]{:S(2)}, u32[]{:S(2)}) async-start(bf16[8,128,1024]{2,1,0:T(8,128)(2,1)} %bitcast.31), calls=%async_computation.3 | async-start | bytes 4194304 | tf_op jit(solution)/shard_map/all_to_all | solution.py:620

commit v4 on v3

--- a/solution.py
+++ b/solution.py
@@ -240,7 +240,7 @@
 
 
 def lane_parts(total):
-    width = 256 if total % 256 == 0 else LANES
+    width = math.gcd(total, 512)
     return [slice(at, at + width) for at in range(0, total, width)]
 
 
@@ -321,14 +321,14 @@
     )(query_rows, keys, values, entry_lanes)
 
 
-def partner_lanes(partner_ref, all_ref, out_ref, slots):
+def partner_lanes(partner_ref, device_row, all_ref, out_ref, slots):
     heads = out_ref.shape[0]
     lane = lax.broadcasted_iota(jnp.int32, (heads, LANES), 1)
     for group in range(slots // 2):
         halves = []
         for half in range(2):
             slot = group * 2 + half
-            device, there = partner_ref[0, slot], partner_ref[1, slot]
+            device, there = partner_ref[device_row, slot], partner_ref[1, slot]
             start = pl.multiple_of(there // 2 * LANES, LANES)
             tile = all_ref[device, :, pl.ds(start, LANES)]
             turned = pltpu.roll(tile, BLOCK, 1)
@@ -340,15 +340,14 @@
 
 def live_lanes(partner_ref, all_ref, out_ref, slots, rows):
     lane = lax.broadcasted_iota(jnp.int32, (1, LANES), 1)
-    row = lax.broadcasted_iota(jnp.int32, (all_ref.shape[1], LANES), 0)
     for group in range(slots // 2):
         own, other = [], []
         for half in range(2):
             slot = group * 2 + half
             reader, place = partner_ref[2, slot], partner_ref[3, slot]
-            counts = all_ref[reader, :, rows:]
+            counts = all_ref[reader, 0:1, rows:]
             count = jnp.sum(
-                jnp.where(row == place // NEIGH, counts, 0.0), axis=0, keepdims=True
+                jnp.where(lane == place // NEIGH, counts, 0.0), axis=1, keepdims=True
             )
             at = (place % NEIGH).astype(F32)
             filled = partner_ref[4, slot] > 0
@@ -365,26 +364,20 @@
     return jnp.where(row == column // HEAD, 1.0, 0.0).astype(BF16)
 
 
-def row_dots(n_seq, lse, seen, grad_rows, count_lanes):
-    heads, rows = lse.shape
-    cols = seen.shape[1]
+def row_dots(n_seq, seen, grad_rows):
+    rows, cols = seen.shape
+    heads = cols // HEAD
     step_rows = rows // STEPS
     steps = rows // step_rows
 
-    def body(lse_ref, seen_ref, grad_ref, count_ref, all_ref, told_ref):
+    def body(seen_ref, grad_ref, all_ref, told_ref):
         step = pl.program_id(0)
-
-        @pl.when(step == 0)
-        def _():
-            told_ref[:heads, :rows] = lse_ref[...]
-            told_ref[:, rows:] = count_ref[...]
-
         terms = grad_ref[...].astype(F32) * seen_ref[...]
         high = terms.astype(BF16)
         low = (terms - high.astype(F32)).astype(BF16)
         of_head = head_columns(heads, cols)
         at = pl.ds(pl.multiple_of(step * step_rows, step_rows), step_rows)
-        told_ref[heads:, at] = sum(
+        told_ref[:, at] = sum(
             lax.dot_general(of_head, part, NT, preferred_element_type=F32) for part in (high, low)
         )
 
@@ -396,18 +389,16 @@
     return pl.pallas_call(
         body,
         grid=(steps,),
-        out_shape=jax.ShapeDtypeStruct((n_seq, 2 * heads, rows + LANES), F32),
+        out_shape=jax.ShapeDtypeStruct((n_seq, heads, rows), F32),
         in_specs=[
-            pl.BlockSpec((heads, rows), lambda i: (0, 0)),
             pl.BlockSpec((step_rows, cols), lambda i: (i, 0)),
             pl.BlockSpec((step_rows, cols), lambda i: (i, 0)),
-            pl.BlockSpec((2 * heads, LANES), lambda i: (0, 0)),
-        ],
-        out_specs=pl.BlockSpec((n_seq, 2 * heads, rows + LANES), lambda i: (0, 0, 0)),
-        scratch_shapes=[pltpu.VMEM((2 * heads, rows + LANES), F32)],
+        ],
+        out_specs=pl.BlockSpec((n_seq, heads, rows), lambda i: (0, 0, 0)),
+        scratch_shapes=[pltpu.VMEM((heads, rows), F32)],
         name="row_dots",
         **vmem_params(moved=1, mib=60),
-    )(lse, seen, grad_rows, count_lanes)
+    )(seen, grad_rows)
 
 
 def slope_terms(weights, told, grad_rows, keys, values, entry_lanes):
@@ -422,7 +413,7 @@
             slope = lax.dot_general(
                 value_ref[...], grad_ref[part, :], NT, preferred_element_type=F32
             )
-            dot = told_ref[0, pl.ds(heads + head, 1), part]
+            dot = told_ref[0, pl.ds(head, 1), part]
             terms = weight_ref[0, :, part] * (pick_entry(slope, entry) - dot)
             wide = spread_entry(terms, entry, key_rows // LANES)
             out_ref[part, :] = lax.dot_general(
@@ -449,42 +440,41 @@
     )(weights, told, grad_rows, keys, values, entry_lanes)
 
 
-def query_terms_of(terms, mean, all_told, my_index, partner):
+def query_terms_of(terms, mean, lse, dots, all_lse, all_dots, partner):
     rows, cols = terms.shape
     heads = cols // HEAD
     slots = rows // BLOCK
     step_rows = rows // STEPS
     scale = 1.0 / math.sqrt(HEAD)
 
-    def body(
-        partner_ref, index_ref, all_ref, term_ref, mean_ref, stat_ref, out_ref, other_ref, live_ref, more_ref
-    ):
+    def body(partner_ref, lse_ref, dot_ref, all_lse_ref, all_dot_ref, term_ref, mean_ref, *refs):
+        stat_ref, out_ref, other_ref, apart_ref, live_ref, more_ref = refs
         step = pl.program_id(0)
 
         @pl.when(step == 0)
         def _():
-            partner_lanes(partner_ref, all_ref, other_ref, slots)
-            live_lanes(partner_ref, all_ref, live_ref, slots, rows)
-            own = all_ref[index_ref[0], :, :rows]
-            apart = other_ref[:heads, :] - own[:heads, :]
+            partner_lanes(partner_ref, 5, all_lse_ref, apart_ref, slots)
+            partner_lanes(partner_ref, 0, all_dot_ref, other_ref, slots)
+            live_lanes(partner_ref, all_lse_ref, live_ref, slots, rows)
+            own = dot_ref[0]
+            apart = apart_ref[...] - lse_ref[...]
             own_live, other_live = live_ref[0:1, :] > 0.0, live_ref[1:2, :] > 0.0
             odds = jnp.where(other_live, jnp.exp(apart), 0.0)
             share = jnp.where(own_live, 1.0 / (1.0 + odds), 0.0)
             rest = jnp.where(other_live, 1.0 / (1.0 + jnp.exp(-apart)), 0.0)
-            more = rest * (other_ref[heads:, :] - own[heads:, :])
+            more = rest * (other_ref[...] - own)
             stat_ref[:heads, :] = share
-            stat_ref[heads:, :] = own[heads:, :] + more
+            stat_ref[heads:, :] = own + more
             more_ref[...] = more
 
         at = pl.ds(pl.multiple_of(step * step_rows, step_rows), step_rows)
-        of_head = head_columns(heads, cols)
+        of_head = jnp.concatenate([head_columns(heads, cols)] * 2, axis=0)
 
         def spread(rows_of_heads):
             high = rows_of_heads.astype(BF16)
             low = (rows_of_heads - high.astype(F32)).astype(BF16)
-            return sum(
-                lax.dot_general(part, of_head, TN, preferred_element_type=F32)
-                for part in (high, low)
+            return lax.dot_general(
+                jnp.concatenate([high, low], axis=0), of_head, TN, preferred_element_type=F32
             )
 
         share, more = spread(stat_ref[:heads, at]), spread(more_ref[:, at])
@@ -501,20 +491,23 @@
         ),
         in_specs=[
             pl.BlockSpec(memory_space=pltpu.SMEM),
-            pl.BlockSpec(memory_space=pltpu.SMEM),
-            pl.BlockSpec(all_told.shape, lambda i: (0, 0, 0)),
+            pl.BlockSpec((heads, rows), lambda i: (0, 0)),
+            pl.BlockSpec((1, heads, rows), lambda i: (0, 0, 0)),
+            pl.BlockSpec(all_lse.shape, lambda i: (0, 0, 0)),
+            pl.BlockSpec(all_dots.shape, lambda i: (0, 0, 0)),
             pl.BlockSpec((step_rows, cols), lambda i: (i, 0)),
             pl.BlockSpec((step_rows, cols), lambda i: (i, 0)),
         ],
         out_specs=(pl.BlockSpec((2 * heads, rows), lambda i: (0, 0)), block),
         scratch_shapes=[
-            pltpu.VMEM((2 * heads, rows), F32),
+            pltpu.VMEM((heads, rows), F32),
+            pltpu.VMEM((heads, rows), F32),
             pltpu.VMEM((2, rows), F32),
             pltpu.VMEM((heads, rows), F32),
         ],
         name="query_terms",
         **vmem_params(moved=1, mib=60),
-    )(partner, my_index, all_told, terms, mean)
+    )(partner, lse, dots, all_lse, all_dots, terms, mean)
 
 
 def entry_grads(weights, stat, query_rows, grad_rows, values, entry_lanes):
@@ -564,6 +557,13 @@
     return lax.ppermute(value, axis, [(i, i ^ bits) for i in range(size)])
 
 
+def cube_gather(value, axis, steps):
+    for step in steps:
+        bits = lax.axis_size(axis) >> (step + 1)
+        value = jnp.concatenate([value, swap(value, axis, bits)], axis=0)
+    return value
+
+
 def rank_slots(owners):
     slot_total = owners.shape[-1]
     earlier_mask = jnp.arange(slot_total)[None, :] < jnp.arange(slot_total)[:, None]
@@ -586,12 +586,20 @@
         return table.reshape(n_seq, -1, NEIGH)[:, :, ::-1].reshape(n_seq, places)
 
     reader = jnp.arange(n_seq)[:, None]
+
+    def turned(device):
+        apart, position, bits = device ^ my_index, 0, n_seq >> 1
+        for step in range(n_seq.bit_length() - 1):
+            position = position + (apart >> step) % 2 * (bits >> step)
+        return position
+
     partner = [
         look(other(owners)),
         look(other(ranks) + slot_cap * reader),
-        look(reader + jnp.zeros_like(owners)),
+        look(turned(reader) + jnp.zeros_like(owners)),
         look(jnp.arange(places) + jnp.zeros_like(owners)),
         look(jnp.ones_like(owners)),
+        look(turned(other(owners))),
     ]
     entry = look(all_lists % entries_here)
     return (
@@ -642,16 +650,20 @@
     )
     grad_places = grad_sum
 
-    count_lanes = jnp.pad(counts.astype(F32), (0, max(0, 2 * head_cols // HEAD - blocks_here)))
-    count_lanes = jnp.broadcast_to(count_lanes[:, None], (count_lanes.shape[0], LANES))
     weights, lse, seen, mean = local_softmax(query_slots, key_rows, value_rows, entry_lanes)
     grad_slots = exchange(grad_places[0])
-    weights, lse, seen, mean, grad_slots = tie((weights, lse, seen, mean, grad_slots))
-    told = row_dots(n_seq, lse, seen, grad_slots, count_lanes)
+    count_lanes = jnp.pad(counts.astype(F32), (0, LANES - blocks_here))
+    count_lanes = jnp.broadcast_to(count_lanes[None], (lse.shape[0], LANES))
+    all_lse = cube_gather(jnp.concatenate([lse, count_lanes], axis=1)[None], "seq", range(1))
+    weights, lse, seen, mean, all_lse, grad_slots = tie(
+        (weights, lse, seen, mean, all_lse, grad_slots)
+    )
+    told = row_dots(n_seq, seen, grad_slots)
     all_told = lax.all_to_all(told, "seq", 0, 0, tiled=True)
+    all_lse = cube_gather(all_lse, "seq", range(1, n_seq.bit_length() - 1))
     terms = slope_terms(weights, told, grad_slots, key_rows, value_rows, entry_lanes)
-    all_told, terms = tie((all_told, terms))
-    stat, query_terms = query_terms_of(terms, mean, all_told, index_arr, partner)
+    all_told, all_lse, terms = tie((all_told, all_lse, terms))
+    stat, query_terms = query_terms_of(terms, mean, lse, told, all_lse, all_told, partner)
     back = exchange(query_terms).reshape(-1, BLOCK, head_cols)
     query_grad = join_places(
         0, 1, back, None, lists, index_arr, n_seq, slot_cap, entries_here, blocks_here

time: 207 us -> 205 us (level)
  starting transfers between devices: 22.4 us -> 28.3 us
  Pallas kernels: 72 us -> 67 us
  waiting for transfers between devices: 102 us -> 97.7 us
    all_to_all x3, waiting for transfers between devices: 72.3 us -> 38.6 us  [exchange(): lax.all_to_all(slot_rows.reshape(n_seq, slot_cap * BLOCK, cols), 'seq', 0...]
    ppermute x3 -> x6, waiting for transfers between devices: 25.8 us -> 59.1 us  [swap(): return lax.ppermute(value, axis, [(i, i ^ bits) for i in range(size)])]
    ppermute x3 -> x6, starting transfers between devices: 3.09 us -> 8.14 us  [swap(): return lax.ppermute(value, axis, [(i, i ^ bits) for i in range(size)])]
    all_to_all x1, waiting for transfers between devices: 4.36 us -> 0.01 us  [on_device(): all_told = lax.all_to_all(told, 'seq', 0, 0, tiled=True)]
  transfers between devices with their start and end apart: 7 -> 10, of which waited for: 4 -> 3; matrix products, arithmetic and copies ran while one was open for 3% -> 4% of each run, Pallas kernels for 29% -> 29%
where the time goes in v4:
time: 205 us; the launch traced here: 204 us
  waiting for transfers between devices  97.7 us (48%)
  Pallas kernels  67 us (33%)
  starting transfers between devices  28.3 us (14%)
  local copies, waits for them, and re-layouts  7.65 us (4%)
  other arithmetic  2.82 us (1%)
    ppermute x6, waiting for transfers between devices, swap(): return lax.ppermute(value, axis, [(i, i ^ bits) for i in range(size)])  59.1 us
    all_to_all x3, waiting for transfers between devices, exchange(): lax.all_to_all(slot_rows.reshape(n_seq, slot_cap * BLOCK, cols), 'seq', 0...  38.6 us
    pallas_call x3, Pallas kernels, add_product(): pl.pallas_call(body, grid_spec=pltpu.PrefetchScalarGridSpec(num_scalar_pr...  23 us
    all_to_all x3, starting transfers between devices, exchange(): lax.all_to_all(slot_rows.reshape(n_seq, slot_cap * BLOCK, cols), 'seq', 0...  16.5 us
    pallas_call x1, Pallas kernels, local_softmax(): pl.pallas_call(body, grid=(heads,), out_shape=(jax.ShapeDtypeStruct((head...  11.3 us
    pallas_call x1, Pallas kernels, slope_terms(): pl.pallas_call(body, grid=(heads,), out_shape=jax.ShapeDtypeStruct((rows,...  9.08 us
    pallas_call x1, Pallas kernels, entry_grads(): pl.pallas_call(body, grid=(heads,), out_shape=[jax.ShapeDtypeStruct((entr...  9.06 us
    ppermute x6, starting transfers between devices, swap(): return lax.ppermute(value, axis, [(i, i ^ bits) for i in range(size)])  8.14 us
  transfers between devices with their start and end apart: 10, of which 3 were waited for; matrix products, arithmetic and copies ran while one was open for 4% of the time, Pallas kernels for 29%

profile of v4, /device:TPU:0, one launch (start us, length us, event | category | flops | bytes accessed | tf_op | source)
XLA Modules:
  0.0 204.3 jit_solution(12867613249004343251)
XLA Ops:
  0.6 0.5 collective-permute-start.2
  1.1 2.6 %collective-permute-start.1 = (bf16[512,2048]{1,0:T(8,128)(2,1)}, bf16[512,2048]{1,0:T(8,128)(2,1)}, u32[]{:S(2)}, u32[]{:S(2)}) collective-permute-start(bf16[512,2048]{1,0:T(8,128)(2,1)} %refs_0_.2), channel_id=1, source_target_pairs={{0,2},{1,3},{2,0},{3,1},{4,6},{5,7},{6,4},{7,5},{8,10},{9,11},{10,... | collective-permute-start | bytes 6291464 | tf_op jit(solution)/shard_map/ppermute | solution.py:557
  3.7 1.4 copy.43.lists_ref.refs_0_
  5.1 2.7 %place_rows.1 = bf16[16,64,1024]{2,1,0:T(8,128)(2,1)} custom-call(s32[64,2]{1,0:T(8,128)} %copy.43.lists_ref.refs_0_, s32[1]{0:T(128)} %bitcast.index_ref.refs_1_, bf16[512,1024]{1,0:T(8,128)(2,1)} %rows_ref.1), custom_call_target="tpu_custom_call" | custom-call | bytes 4194304 | tf_op jit(solution)/shard_map/place_rows/pallas_call | solution.py:88
  7.8 5.8 %all-to-all-start = ((bf16[8,128,1024]{2,1,0:T(8,128)(2,1)}), bf16[8,128,1024]{2,1,0:T(8,128)(2,1)S(1)}, u32[]{:S(2)}, u32[]{:S(2)}) async-start(bf16[8,128,1024]{2,1,0:T(8,128)(2,1)} %bitcast.29), calls=%async_computation | async-start | bytes 4194304 | tf_op jit(solution)/shard_map/all_to_all | solution.py:628
  13.7 0.6 pad_add_fusion.source_ref
  14.3 0.0 collective-permute-done.2.refs_1_
  14.3 10.2 %add_product.3.refs_0_ = f32[512,1024]{1,0:T(8,128)} custom-call(s32[2]{0:T(128)} %pad_add_fusion.source_ref, bf16[512,2048]{1,0:T(8,128)(2,1)} %refs_0_.2, bf16[512,2048]{1,0:T(8,128)(2,1)} %collective-permute-done.2.refs_1_, bf16[1024,8192]{1,0:T(8,128)(2,1)} %refs_4_.1, bf16[1024,8192]{1,0:T(8,128)(2,1)} %refs_4_.1), custom_call_target="tpu_custom_call" | custom-call | bytes 1 | tf_op jit(solution)/shard_map/add_product/pallas_call | solution.py:185
  24.5 25.8 %collective-permute-done.1.refs_1_ = bf16[512,2048]{1,0:T(8,128)(2,1)} collective-permute-done((bf16[512,2048]{1,0:T(8,128)(2,1)}, bf16[512,2048]{1,0:T(8,128)(2,1)}, u32[]{:S(2)}, u32[]{:S(2)}) %collective-permute-start.1) | collective-permute-done | bytes 2097184 | tf_op jit(solution)/shard_map/ppermute | solution.py:557
  50.3 0.0 collective-permute-start.3
  50.3 6.2 %add_product.4.refs_2_ = f32[512,1024]{1,0:T(8,128)} custom-call(s32[1]{0:T(128)} %bitcast.12.source_ref, f32[512,1024]{1,0:T(8,128)} %add_product.3.refs_0_, bf16[512,2048]{1,0:T(8,128)(2,1)} %collective-permute-done.1.refs_1_, bf16[1024,8192]{1,0:T(8,128)(2,1)} %refs_4_.1), custom_call_target="tpu_custom_call" | custom-call | bytes 1 | tf_op jit(solution)/shard_map/add_product/pallas_call | solution.py:185
  56.4 0.0 collective-permute-done.3.refs_3_
  56.4 6.6 %add_product.5 = bf16[16,64,1024]{2,1,0:T(8,128)(2,1)} custom-call(s32[1]{0:T(128)} %bitcast.9.source_ref, s32[64,2]{1,0:T(8,128)} %copy.43.lists_ref.refs_0_, s32[1]{0:T(128)} %bitcast.index_ref.refs_1_, f32[512,1024]{1,0:T(8,128)} %add_product.4.refs_2_, bf16[512,2048]{1,0:T(8,128)(2,1)} %collective-permute-done.3.refs_3_, bf16[1024,8192]{1,0:T(8,128)(2,1)} %refs_4_.1), custom_call_target="tpu_custom_call" | custom-call | bytes 1 | tf_op jit(solution)/shard_map/add_product/pallas_call | solution.py:185
  63.1 0.0 all-to-all-done
  63.1 0.0 copy-start.4
  63.1 0.0 copy-start
  63.1 0.0 copy-start.5
  63.1 1.3 copy-done.2
  64.4 6.1 %all-to-all-start.1 = ((bf16[8,128,1024]{2,1,0:T(8,128)(2,1)}), bf16[8,128,1024]{2,1,0:T(8,128)(2,1)S(1)}, u32[]{:S(2)}, u32[]{:S(2)}) async-start(bf16[8,128,1024]{2,1,0:T(8,128)(2,1)} %bitcast.28), calls=%async_computation.1 | async-start | bytes 4194304 | tf_op jit(solution)/shard_map/all_to_all | solution.py:628
  70.6 0.1 reshape.297
  70.7 0.1 reshape.296
  70.8 0.1 copy.29
  70.9 0.1 copy.30
  71.0 0.3 convert_reduce_fusion
  71.3 0.1 copy.32
  71.4 0.1 copy.33
  71.5 0.3 select_reduce_fusion
  71.9 0.1 copy.41
  71.9 0.1 broadcast_in_dim_reshape.4
  72.0 0.1 broadcast_in_dim.88
  72.1 0.7 broadcast_in_dim.89.entry_ref
  72.8 11.3 %local_softmax.1 = (f32[8,128,1024]{2,1,0:T(8,128)}, f32[8,1024]{1,0:T(8,128)}, f32[1024,1024]{1,0:T(8,128)}, bf16[1024,1024]{1,0:T(8,128)(2,1)}) custom-call(bf16[1024,1024]{1,0:T(8,128)(2,1)} %bitcast.26, bf16[256,1024]{1,0:T(8,128)(2,1)} %bitcast.34, bf16[256,1024]{1,0:T(8,128)(2,1)} %bitcast.30, s32[1,1024]{1,0:T(1,128)} %broadcast_in_dim.89.entry_ref), custom_call_target="tpu_custom_call" | custom-call | bytes 1 | tf_op jit(solution)/shard_map/local_softmax/pallas_call | solution.py:298
  84.1 0.8 maximum_bitcast_fusion
  84.9 2.9 %collective-permute-start = (f32[1,8,1152]{2,1,0:T(8,128)S(1)}, f32[1,8,1152]{2,1,0:T(8,128)S(1)}, u32[]{:S(2)}, u32[]{:S(2)}) collective-permute-start(f32[1,8,1152]{2,1,0:T(8,128)S(1)} %maximum_bitcast_fusion), channel_id=1, source_target_pairs={{0,16},{4,20},{8,24},{12,28},{16,0},{20,4},{24,8},{28,12},{1,17},{... | collective-permute-start | bytes 110600 | tf_op jit(solution)/shard_map/ppermute | solution.py:557
  87.8 33.3 %collective-permute-done = f32[1,8,1152]{2,1,0:T(8,128)S(1)} collective-permute-done((f32[1,8,1152]{2,1,0:T(8,128)S(1)}, f32[1,8,1152]{2,1,0:T(8,128)S(1)}, u32[]{:S(2)}, u32[]{:S(2)}) %collective-permute-start) | collective-permute-done | bytes 36896 | tf_op jit(solution)/shard_map/ppermute | solution.py:557
  121.1 0.0 all-to-all-done.1
  121.1 0.1 collective-permute-start.4
  121.2 1.2 copy-done.1
  122.4 4.2 %row_dots.1.told_ref.dot_ref = f32[8,8,1024]{2,1,0:T(8,128)} custom-call(f32[1024,1024]{1,0:T(8,128)} %get-tuple-element.33.seen_ref, bf16[1024,1024]{1,0:T(8,128)(2,1)} %bitcast.23), custom_call_target="tpu_custom_call" | custom-call | bytes 1 | tf_op jit(solution)/shard_map/row_dots/pallas_call | solution.py:389
  126.7 3.6 %all-to-all-start.2 = ((f32[8,8,1024]{2,1,0:T(8,128)}), f32[8,8,1024]{2,1,0:T(8,128)S(1)}, u32[]{:S(2)}, u32[]{:S(2)}) async-start(f32[8,8,1024]{2,1,0:T(8,128)} %row_dots.1.told_ref.dot_ref), calls=%async_computation.2 | async-start | bytes 524288 | tf_op jit(solution)/shard_map/all_to_all | solution.py:662
  130.3 0.0 collective-permute-done.4
  130.3 2.1 %collective-permute-start.5 = (f32[4,8,1152]{2,1,0:T(8,128)S(1)}, f32[4,8,1152]{2,1,0:T(8,128)S(1)}, u32[]{:S(2)}, u32[]{:S(2)}) collective-permute-start(f32[4,8,1152]{2,1,0:T(8,128)S(1)} %pad_maximum_fusion.1), channel_id=1, source_target_pairs={{0,4},{4,0},{8,12},{12,8},{16,20},{20,16},{24,28},{28,24},{1,5},{5... | collective-permute-start | bytes 442376 | tf_op jit(solution)/shard_map/ppermute | solution.py:557
  132.4 0.1 copy.39
  132.5 0.1 stack_reshape.23
  132.6 0.1 copy.37
  132.6 0.1 stack_reshape.22
  132.7 0.1 copy.36
  132.8 0.1 stack_reshape.21
  132.9 0.1 copy.35
  133.0 0.1 stack_reshape.20
  133.0 0.1 copy.34
  133.1 0.1 stack_reshape.19
  133.2 0.1 copy.31
  133.3 0.1 stack_reshape.18
  133.4 0.6 stack.18.partner_ref
  134.0 9.1 %slope_terms.1.term_ref = bf16[1024,1024]{1,0:T(8,128)(2,1)} custom-call(f32[8,128,1024]{2,1,0:T(8,128)} %get-tuple-element.36.weight_ref, f32[8,8,1024]{2,1,0:T(8,128)} %row_dots.1.told_ref.dot_ref, bf16[1024,1024]{1,0:T(8,128)(2,1)} %bitcast.24, bf16[256,1024]{1,0:T(8,128)(2,1)} %bitcast.35, bf16[256,1024]{1,0:T(8,128)(2,1)} %bitcast.31, ...), custom_call_target="tpu_custom_call" | custom-call | bytes 1 | tf_op jit(solution)/shard_map/slope_terms/pallas_call | solution.py:425
  143.1 0.7 pad_maximum_fusion.all_lse_ref
  143.8 0.0 all-to-all-done.2.all_dot_ref
  143.8 0.7 copy-done.3
  144.5 5.0 %query_terms.1 = (f32[16,1024]{1,0:T(8,128)}, bf16[1024,1024]{1,0:T(8,128)(2,1)}) custom-call(s32[6,16]{1,0:T(8,128)} %stack.18.partner_ref, f32[8,1024]{1,0:T(8,128)} %get-tuple-element.32.lse_ref, f32[8,8,1024]{2,1,0:T(8,128)} %row_dots.1.told_ref.dot_ref, f32[8,8,1152]{2,1,0:T(8,128)} %pad_maximum_fusion.all_lse_ref, f32[8,8,1024]{2,1,0:T(8,128)} %copy-done.3, ...), custom_call_target="tpu_custom_call" | custom-call | bytes 1 | tf_op jit(solution)/shard_map/query_terms/pallas_call | solution.py:485
  149.6 4.5 %all-to-all-start.3 = ((bf16[8,128,1024]{2,1,0:T(8,128)(2,1)}), bf16[8,128,1024]{2,1,0:T(8,128)(2,1)S(1)}, u32[]{:S(2)}, u32[]{:S(2)}) async-start(bf16[8,128,1024]{2,1,0:T(8,128)(2,1)} %bitcast.33), calls=%async_computation.3 | async-start | bytes 4194304 | tf_op jit(solution)/shard_map/all_to_all | solution.py:628
  154.1 9.1 %entry_grads.1 = (bf16[256,1024]{1,0:T(8,128)(2,1)}, bf16[256,1024]{1,0:T(8,128)(2,1)}) custom-call(f32[8,128,1024]{2,1,0:T(8,128)} %get-tuple-element.36.weight_ref, f32[16,1024]{1,0:T(8,128)} %get-tuple-element.42.stat_ref, bf16[1024,1024]{1,0:T(8,128)(2,1)} %bitcast.27, bf16[1024,1024]{1,0:T(8,128)(2,1)} %bitcast.25, bf16[256,1024]{1,0:T(8,128)(2,1)} %bitcast.32, ...), custom_call_target="tpu_custom_call" | custom-call | bytes 1 | tf_op jit(solution)/shard_map/entry_grads/pallas_call | solution.py:537
  163.2 38.6 %all-to-all-done.3 = bf16[8,128,1024]{2,1,0:T(8,128)(2,1)S(1)} async-done(((bf16[8,128,1024]{2,1,0:T(8,128)(2,1)}), bf16[8,128,1024]{2,1,0:T(8,128)(2,1)S(1)}, u32[]{:S(2)}, u32[]{:S(2)}) %all-to-all-start.3) | async-done | bytes 2097184 | tf_op jit(solution)/shard_map/all_to_all | solution.py:628
  201.7 2.6 %join_places.1 = bf16[512,1024]{1,0:T(8,128)(2,1)} custom-call(s32[64,2]{1,0:T(8,128)S(1)} %copy-done, s32[1]{0:T(128)} %bitcast.index_ref.refs_1_, bf16[16,64,1024]{2,1,0:T(8,128)(2,1)S(1)} %bitcast.22), custom_call_target="tpu_custom_call" | custom-call | bytes 3145728 | tf_op jit(solution)/shard_map/join_places/pallas_call | solution.py:225
  (21 shorter events, 0.2 us)
Async XLA Ops:
  0.6 13.6 %collective-permute-start.2 = (bf16[512,2048]{1,0:T(8,128)(2,1)}, bf16[512,2048]{1,0:T(8,128)(2,1)}, u32[]{:S(2)}, u32[]{:S(2)}) collective-permute-start(bf16[512,2048]{1,0:T(8,128)(2,1)} %refs_0_.2), channel_id=1, source_target_pairs={{0,1},{1,0},{2,3},{3,2},{4,5},{5,4},{6,7},{7,6},{8,9},{9,8},{10,11... | collective-permute-start | bytes 6291464 | tf_op jit(solution)/shard_map/ppermute | solution.py:557
  1.1 49.1 %collective-permute-start.1 = (bf16[512,2048]{1,0:T(8,128)(2,1)}, bf16[512,2048]{1,0:T(8,128)(2,1)}, u32[]{:S(2)}, u32[]{:S(2)}) collective-permute-start(bf16[512,2048]{1,0:T(8,128)(2,1)} %refs_0_.2), channel_id=1, source_target_pairs={{0,2},{1,3},{2,0},{3,1},{4,6},{5,7},{6,4},{7,5},{8,10},{9,11},{10,... | collective-permute-start | bytes 6291464 | tf_op jit(solution)/shard_map/ppermute | solution.py:557
  7.8 55.2 %all-to-all-start = ((bf16[8,128,1024]{2,1,0:T(8,128)(2,1)}), bf16[8,128,1024]{2,1,0:T(8,128)(2,1)S(1)}, u32[]{:S(2)}, u32[]{:S(2)}) async-start(bf16[8,128,1024]{2,1,0:T(8,128)(2,1)} %bitcast.29), calls=%async_computation | async-start | bytes 4194304 | tf_op jit(solution)/shard_map/all_to_all | solution.py:628
  50.3 6.2 %collective-permute-start.3 = (bf16[512,2048]{1,0:T(8,128)(2,1)}, bf16[512,2048]{1,0:T(8,128)(2,1)}, u32[]{:S(2)}, u32[]{:S(2)}) collective-permute-start(bf16[512,2048]{1,0:T(8,128)(2,1)} %collective-permute-done.1.refs_1_), channel_id=1, source_target_pairs={{0,1},{1,0},{2,3},{3,2},{4,5},{5,4},{6,7},{7,6},{8,9},{9,8},{10,11... | collective-permute-start | bytes 6291464 | tf_op jit(solution)/shard_map/ppermute | solution.py:557
  63.1 1.4 copy-start.2
  63.1 7.5 %copy-start.4 = (s32[64,2]{0,1:T(2,128)S(1)}, s32[64,2]{0,1:T(2,128)}, u32[]{:S(2)}) copy-start(s32[64,2]{0,1:T(2,128)} %param.12) | copy-start | bytes 1540
  63.1 7.6 %copy-start = (s32[64,2]{1,0:T(8,128)S(1)}, s32[64,2]{1,0:T(8,128)}, u32[]{:S(2)}) copy-start(s32[64,2]{1,0:T(8,128)} %copy.43.lists_ref.refs_0_) | copy-start | bytes 1540
  63.1 7.7 %copy-start.5 = (s32[8]{0:T(128)S(1)}, s32[8]{0:T(128)}, u32[]{:S(2)}) copy-start(s32[8]{0:T(128)} %param.13) | copy-start | bytes 100
  64.4 56.6 %all-to-all-start.1 = ((bf16[8,128,1024]{2,1,0:T(8,128)(2,1)}), bf16[8,128,1024]{2,1,0:T(8,128)(2,1)S(1)}, u32[]{:S(2)}, u32[]{:S(2)}) async-start(bf16[8,128,1024]{2,1,0:T(8,128)(2,1)} %bitcast.28), calls=%async_computation.1 | async-start | bytes 4194304 | tf_op jit(solution)/shard_map/all_to_all | solution.py:628
  84.9 36.2 %collective-permute-start = (f32[1,8,1152]{2,1,0:T(8,128)S(1)}, f32[1,8,1152]{2,1,0:T(8,128)S(1)}, u32[]{:S(2)}, u32[]{:S(2)}) collective-permute-start(f32[1,8,1152]{2,1,0:T(8,128)S(1)} %maximum_bitcast_fusion), channel_id=1, source_target_pairs={{0,16},{4,20},{8,24},{12,28},{16,0},{20,4},{24,8},{28,12},{1,17},{... | collective-permute-start | bytes 110600 | tf_op jit(solution)/shard_map/ppermute | solution.py:557
  121.1 1.3 copy-start.1
  121.1 9.2 %collective-permute-start.4 = (f32[2,8,1152]{2,1,0:T(8,128)S(1)}, f32[2,8,1152]{2,1,0:T(8,128)S(1)}, u32[]{:S(2)}, u32[]{:S(2)}) collective-permute-start(f32[2,8,1152]{2,1,0:T(8,128)S(1)} %pad_maximum_fusion.2), channel_id=1, source_target_pairs={{0,8},{4,12},{8,0},{12,4},{16,24},{20,28},{24,16},{28,20},{1,9},{5... | collective-permute-start | bytes 221192 | tf_op jit(solution)/shard_map/ppermute | solution.py:557
  126.7 17.2 %all-to-all-start.2 = ((f32[8,8,1024]{2,1,0:T(8,128)}), f32[8,8,1024]{2,1,0:T(8,128)S(1)}, u32[]{:S(2)}, u32[]{:S(2)}) async-start(f32[8,8,1024]{2,1,0:T(8,128)} %row_dots.1.told_ref.dot_ref), calls=%async_computation.2 | async-start | bytes 524288 | tf_op jit(solution)/shard_map/all_to_all | solution.py:662
  130.3 12.8 %collective-permute-start.5 = (f32[4,8,1152]{2,1,0:T(8,128)S(1)}, f32[4,8,1152]{2,1,0:T(8,128)S(1)}, u32[]{:S(2)}, u32[]{:S(2)}) collective-permute-start(f32[4,8,1152]{2,1,0:T(8,128)S(1)} %pad_maximum_fusion.1), channel_id=1, source_target_pairs={{0,4},{4,0},{8,12},{12,8},{16,20},{20,16},{24,28},{28,24},{1,5},{5... | collective-permute-start | bytes 442376 | tf_op jit(solution)/shard_map/ppermute | solution.py:557
  143.8 0.7 copy-start.3
  149.6 52.2 %all-to-all-start.3 = ((bf16[8,128,1024]{2,1,0:T(8,128)(2,1)}), bf16[8,128,1024]{2,1,0:T(8,128)(2,1)S(1)}, u32[]{:S(2)}, u32[]{:S(2)}) async-start(bf16[8,128,1024]{2,1,0:T(8,128)(2,1)} %bitcast.33), calls=%async_computation.3 | async-start | bytes 4194304 | tf_op jit(solution)/shard_map/all_to_all | solution.py:628

commit v5 on v4

--- a/solution.py
+++ b/solution.py
@@ -25,13 +25,18 @@
     )
 
 
-def slot_of_place(lists_ref, base, place, entries_here, slot_cap):
-    owner = lists_ref[base + place // NEIGH, place % NEIGH] // entries_here
-    rank = 0
-    for earlier in range(place):
-        named = lists_ref[base + earlier // NEIGH, earlier % NEIGH]
-        rank = rank + jnp.where(named // entries_here == owner, 1, 0)
-    return owner * slot_cap + rank
+def slots_of_places(lists_ref, base, places, entries_here, slot_cap):
+    owners = [
+        lax.div(lists_ref[place % NEIGH, base + place // NEIGH], entries_here)
+        for place in range(places)
+    ]
+    slots = []
+    for place, owner in enumerate(owners):
+        rank = 0
+        for earlier in owners[:place]:
+            rank = rank + jnp.where(earlier == owner, 1, 0)
+        slots.append(owner * slot_cap + rank)
+    return slots
 
 
 def place_copies(lists_ref, base, rows_ref, out_refs, zero_ref, sems, places, entries_here, slot_cap):
@@ -48,9 +53,7 @@
                 blank.start()
             for blank in blanks:
                 blank.wait()
-    slot_list = [
-        slot_of_place(lists_ref, base, place, entries_here, slot_cap) for place in range(places)
-    ]
+    slot_list = slots_of_places(lists_ref, base, places, entries_here, slot_cap)
     copies = []
     for chunk, out_ref in enumerate(out_refs):
         for place, slot in enumerate(slot_list):
@@ -213,12 +216,10 @@
     def body(lists_ref, index_ref, back_ref, *refs):
         out_ref = refs[-1]
         base = index_ref[0] * (places // NEIGH)
+        slot_list = slots_of_places(lists_ref, base, places, entries_here, slot_cap)
         for block in range(blocks_here):
             total = 0.0
-            for neighbour in range(NEIGH):
-                slot = slot_of_place(
-                    lists_ref, base, block * NEIGH + neighbour, entries_here, slot_cap
-                )
+            for slot in slot_list[block * NEIGH : (block + 1) * NEIGH]:
                 total = total + back_ref[slot].astype(F32)
             out_ref[block * BLOCK : (block + 1) * BLOCK, :] = total.astype(out_ref.dtype)
 
@@ -618,7 +619,7 @@
     slot_cap = (places + n_seq - 1) // n_seq
     rows = n_seq * slot_cap * BLOCK
     feats = out_grad.shape[1]
-    lists = retrieval
+    lists = retrieval.T
     index_arr = my_index.astype(jnp.int32).reshape(1)
     key_rows = keys.reshape(entries_here * nbr_rows, head_cols)
     value_rows = values.reshape(entries_here * nbr_rows, head_cols)
@@ -655,8 +656,8 @@
     count_lanes = jnp.pad(counts.astype(F32), (0, LANES - blocks_here))
     count_lanes = jnp.broadcast_to(count_lanes[None], (lse.shape[0], LANES))
     all_lse = cube_gather(jnp.concatenate([lse, count_lanes], axis=1)[None], "seq", range(1))
-    weights, lse, seen, mean, all_lse, grad_slots = tie(
-        (weights, lse, seen, mean, all_lse, grad_slots)
+    weights, lse, seen, mean, all_lse, partner, grad_slots = tie(
+        (weights, lse, seen, mean, all_lse, partner, grad_slots)
     )
     told = row_dots(n_seq, seen, grad_slots)
     all_told = lax.all_to_all(told, "seq", 0, 0, tiled=True)

time: 205 us -> 203 us (level)
    unnamed x13 -> x11, local copies, waits for them, and re-layouts: 4.65 us -> 3.37 us
  transfers between devices with their start and end apart: 10 -> 10, of which waited for: 3 -> 3; matrix products, arithmetic and copies ran while one was open for 4% -> 3% of each run, Pallas kernels for 29% -> 29%
where the time goes in v5:
time: 203 us; the launch traced here: 202 us
  waiting for transfers between devices  97.4 us (48%)
  Pallas kernels  66.2 us (33%)
  starting transfers between devices  28.3 us (14%)
  local copies, waits for them, and re-layouts  6.37 us (3%)
  other arithmetic  2.81 us (1%)
    ppermute x6, waiting for transfers between devices, swap(): return lax.ppermute(value, axis, [(i, i ^ bits) for i in range(size)])  58.8 us
    all_to_all x3, waiting for transfers between devices, exchange(): lax.all_to_all(slot_rows.reshape(n_seq, slot_cap * BLOCK, cols), 'seq', 0...  38.6 us
    pallas_call x3, Pallas kernels, add_product(): pl.pallas_call(body, grid_spec=pltpu.PrefetchScalarGridSpec(num_scalar_pr...  23 us
    all_to_all x3, starting transfers between devices, exchange(): lax.all_to_all(slot_rows.reshape(n_seq, slot_cap * BLOCK, cols), 'seq', 0...  16.5 us
    pallas_call x1, Pallas kernels, local_softmax(): pl.pallas_call(body, grid=(heads,), out_shape=(jax.ShapeDtypeStruct((head...  11.3 us
    pallas_call x1, Pallas kernels, slope_terms(): pl.pallas_call(body, grid=(heads,), out_shape=jax.ShapeDtypeStruct((rows,...  9.08 us
    pallas_call x1, Pallas kernels, entry_grads(): pl.pallas_call(body, grid=(heads,), out_shape=[jax.ShapeDtypeStruct((entr...  9.06 us
    ppermute x6, starting transfers between devices, swap(): return lax.ppermute(value, axis, [(i, i ^ bits) for i in range(size)])  8.17 us
  transfers between devices with their start and end apart: 10, of which 3 were waited for; matrix products, arithmetic and copies ran while one was open for 3% of the time, Pallas kernels for 29%

profile of v5, /device:TPU:0, one launch (start us, length us, event | category | flops | bytes accessed | tf_op | source)
XLA Modules:
  0.0 201.9 jit_solution(11320478760383585091)
XLA Ops:
  0.6 0.5 collective-permute-start.2
  1.1 2.6 %collective-permute-start.1 = (bf16[512,2048]{1,0:T(8,128)(2,1)}, bf16[512,2048]{1,0:T(8,128)(2,1)}, u32[]{:S(2)}, u32[]{:S(2)}) collective-permute-start(bf16[512,2048]{1,0:T(8,128)(2,1)} %refs_0_.1), channel_id=1, source_target_pairs={{0,2},{1,3},{2,0},{3,1},{4,6},{5,7},{6,4},{7,5},{8,10},{9,11},{10,... | collective-permute-start | bytes 6291464 | tf_op jit(solution)/shard_map/ppermute | solution.py:558
  3.7 2.7 %place_rows.1 = bf16[16,64,1024]{2,1,0:T(8,128)(2,1)} custom-call(s32[2,64]{1,0:T(2,128)} %bitcast.24, s32[1]{0:T(128)} %bitcast.1.index_ref.refs_1_, bf16[512,1024]{1,0:T(8,128)(2,1)} %rows_ref.1), custom_call_target="tpu_custom_call" | custom-call | bytes 4194304 | tf_op jit(solution)/shard_map/place_rows/pallas_call | solution.py:91
  6.4 5.8 %all-to-all-start = ((bf16[8,128,1024]{2,1,0:T(8,128)(2,1)}), bf16[8,128,1024]{2,1,0:T(8,128)(2,1)S(1)}, u32[]{:S(2)}, u32[]{:S(2)}) async-start(bf16[8,128,1024]{2,1,0:T(8,128)(2,1)} %bitcast.33), calls=%async_computation | async-start | bytes 4194304 | tf_op jit(solution)/shard_map/all_to_all | solution.py:629
  12.3 0.6 pad_add_fusion.source_ref
  12.9 0.0 collective-permute-done.2.refs_1_
  12.9 10.2 %add_product.3.refs_0_ = f32[512,1024]{1,0:T(8,128)} custom-call(s32[2]{0:T(128)} %pad_add_fusion.source_ref, bf16[512,2048]{1,0:T(8,128)(2,1)} %refs_0_.1, bf16[512,2048]{1,0:T(8,128)(2,1)} %collective-permute-done.2.refs_1_, bf16[1024,8192]{1,0:T(8,128)(2,1)} %refs_4_.1, bf16[1024,8192]{1,0:T(8,128)(2,1)} %refs_4_.1), custom_call_target="tpu_custom_call" | custom-call | bytes 1 | tf_op jit(solution)/shard_map/add_product/pallas_call | solution.py:188
  23.0 27.2 %collective-permute-done.1.refs_1_ = bf16[512,2048]{1,0:T(8,128)(2,1)} collective-permute-done((bf16[512,2048]{1,0:T(8,128)(2,1)}, bf16[512,2048]{1,0:T(8,128)(2,1)}, u32[]{:S(2)}, u32[]{:S(2)}) %collective-permute-start.1) | collective-permute-done | bytes 2097184 | tf_op jit(solution)/shard_map/ppermute | solution.py:558
  50.3 0.0 collective-permute-start.3
  50.3 6.2 %add_product.4.refs_2_ = f32[512,1024]{1,0:T(8,128)} custom-call(s32[1]{0:T(128)} %bitcast.13.source_ref, f32[512,1024]{1,0:T(8,128)} %add_product.3.refs_0_, bf16[512,2048]{1,0:T(8,128)(2,1)} %collective-permute-done.1.refs_1_, bf16[1024,8192]{1,0:T(8,128)(2,1)} %refs_4_.1), custom_call_target="tpu_custom_call" | custom-call | bytes 1 | tf_op jit(solution)/shard_map/add_product/pallas_call | solution.py:188
  56.4 0.0 collective-permute-done.3.refs_3_
  56.4 6.7 %add_product.5 = bf16[16,64,1024]{2,1,0:T(8,128)(2,1)} custom-call(s32[1]{0:T(128)} %bitcast.10.source_ref, s32[2,64]{1,0:T(2,128)} %bitcast.25, s32[1]{0:T(128)} %bitcast.1.index_ref.refs_1_, f32[512,1024]{1,0:T(8,128)} %add_product.4.refs_2_, bf16[512,2048]{1,0:T(8,128)(2,1)} %collective-permute-done.3.refs_3_, bf16[1024,8192]{1,0:T(8,128)(2,1)} %refs_4_.1), custom_call_target="tpu_custom_call" | custom-call | bytes 1 | tf_op jit(solution)/shard_map/add_product/pallas_call | solution.py:188
  63.1 0.0 all-to-all-done
  63.1 0.0 copy-start
  63.1 0.0 copy-start.4
  63.2 1.3 copy-done.2
  64.5 6.1 %all-to-all-start.1 = ((bf16[8,128,1024]{2,1,0:T(8,128)(2,1)}), bf16[8,128,1024]{2,1,0:T(8,128)(2,1)S(1)}, u32[]{:S(2)}, u32[]{:S(2)}) async-start(bf16[8,128,1024]{2,1,0:T(8,128)(2,1)} %bitcast.32), calls=%async_computation.1 | async-start | bytes 4194304 | tf_op jit(solution)/shard_map/all_to_all | solution.py:629
  70.6 0.1 reshape.301
  70.7 0.1 copy.22
  70.8 0.1 copy.24
  70.9 0.1 copy.25
  71.0 0.1 reshape.300
  71.1 0.3 convert_reduce_fusion
  71.4 0.1 copy.27
  71.5 0.1 copy.28
  71.6 0.3 select_reduce_fusion
  71.9 0.1 copy.23
  72.0 0.1 broadcast_in_dim_reshape.4
  72.1 0.1 broadcast_in_dim.81
  72.2 0.7 broadcast_in_dim.82.entry_ref
  72.9 11.3 %local_softmax.1 = (f32[8,128,1024]{2,1,0:T(8,128)}, f32[8,1024]{1,0:T(8,128)}, f32[1024,1024]{1,0:T(8,128)}, bf16[1024,1024]{1,0:T(8,128)(2,1)}) custom-call(bf16[1024,1024]{1,0:T(8,128)(2,1)} %bitcast.30, bf16[256,1024]{1,0:T(8,128)(2,1)} %bitcast.38, bf16[256,1024]{1,0:T(8,128)(2,1)} %bitcast.34, s32[1,1024]{1,0:T(1,128)} %broadcast_in_dim.82.entry_ref), custom_call_target="tpu_custom_call" | custom-call | bytes 1 | tf_op jit(solution)/shard_map/local_softmax/pallas_call | solution.py:299
  84.2 0.8 maximum_bitcast_fusion
  84.9 2.9 %collective-permute-start = (f32[1,8,1152]{2,1,0:T(8,128)S(1)}, f32[1,8,1152]{2,1,0:T(8,128)S(1)}, u32[]{:S(2)}, u32[]{:S(2)}) collective-permute-start(f32[1,8,1152]{2,1,0:T(8,128)S(1)} %maximum_bitcast_fusion), channel_id=1, source_target_pairs={{0,16},{4,20},{8,24},{12,28},{16,0},{20,4},{24,8},{28,12},{1,17},{... | collective-permute-start | bytes 110600 | tf_op jit(solution)/shard_map/ppermute | solution.py:558
  87.9 0.1 copy.34
  88.0 0.1 stack_reshape.23
  88.0 0.1 copy.32
  88.1 0.1 stack_reshape.22
  88.2 0.1 copy.31
  88.3 0.1 stack_reshape.21
  88.4 0.1 copy.30
  88.4 0.1 stack_reshape.20
  88.5 0.1 copy.29
  88.6 0.1 stack_reshape.19
  88.7 0.1 copy.26
  88.8 0.1 stack_reshape.18
  88.9 0.6 stack.18.partner_ref
  89.5 31.6 %collective-permute-done = f32[1,8,1152]{2,1,0:T(8,128)S(1)} collective-permute-done((f32[1,8,1152]{2,1,0:T(8,128)S(1)}, f32[1,8,1152]{2,1,0:T(8,128)S(1)}, u32[]{:S(2)}, u32[]{:S(2)}) %collective-permute-start) | collective-permute-done | bytes 36896 | tf_op jit(solution)/shard_map/ppermute | solution.py:558
  121.1 0.0 all-to-all-done.1
  121.1 0.1 collective-permute-start.4
  121.2 1.2 copy-done.1
  122.4 4.2 %row_dots.1.told_ref.dot_ref = f32[8,8,1024]{2,1,0:T(8,128)} custom-call(f32[1024,1024]{1,0:T(8,128)} %get-tuple-element.35.seen_ref, bf16[1024,1024]{1,0:T(8,128)(2,1)} %bitcast.27), custom_call_target="tpu_custom_call" | custom-call | bytes 1 | tf_op jit(solution)/shard_map/row_dots/pallas_call | solution.py:390
  126.6 3.6 %all-to-all-start.2 = ((f32[8,8,1024]{2,1,0:T(8,128)}), f32[8,8,1024]{2,1,0:T(8,128)S(1)}, u32[]{:S(2)}, u32[]{:S(2)}) async-start(f32[8,8,1024]{2,1,0:T(8,128)} %row_dots.1.told_ref.dot_ref), calls=%async_computation.2 | async-start | bytes 524288 | tf_op jit(solution)/shard_map/all_to_all | solution.py:663
  130.3 0.0 collective-permute-done.4
  130.3 2.1 %collective-permute-start.5 = (f32[4,8,1152]{2,1,0:T(8,128)S(1)}, f32[4,8,1152]{2,1,0:T(8,128)S(1)}, u32[]{:S(2)}, u32[]{:S(2)}) collective-permute-start(f32[4,8,1152]{2,1,0:T(8,128)S(1)} %pad_maximum_fusion.1), channel_id=1, source_target_pairs={{0,4},{4,0},{8,12},{12,8},{16,20},{20,16},{24,28},{28,24},{1,5},{5... | collective-permute-start | bytes 442376 | tf_op jit(solution)/shard_map/ppermute | solution.py:558
  132.4 9.1 %slope_terms.1.term_ref = bf16[1024,1024]{1,0:T(8,128)(2,1)} custom-call(f32[8,128,1024]{2,1,0:T(8,128)} %get-tuple-element.38.weight_ref, f32[8,8,1024]{2,1,0:T(8,128)} %row_dots.1.told_ref.dot_ref, bf16[1024,1024]{1,0:T(8,128)(2,1)} %bitcast.28, bf16[256,1024]{1,0:T(8,128)(2,1)} %bitcast.39, bf16[256,1024]{1,0:T(8,128)(2,1)} %bitcast.35, ...), custom_call_target="tpu_custom_call" | custom-call | bytes 1 | tf_op jit(solution)/shard_map/slope_terms/pallas_call | solution.py:426
  141.5 0.0 collective-permute-done.5
  141.5 0.7 pad_maximum_fusion.all_lse_ref
  142.2 0.0 all-to-all-done.2.all_dot_ref
  142.2 0.7 copy-done.3
  142.9 5.0 %query_terms.1 = (f32[16,1024]{1,0:T(8,128)}, bf16[1024,1024]{1,0:T(8,128)(2,1)}) custom-call(s32[6,16]{1,0:T(8,128)} %stack.18.partner_ref, f32[8,1024]{1,0:T(8,128)} %get-tuple-element.34.lse_ref, f32[8,8,1024]{2,1,0:T(8,128)} %row_dots.1.told_ref.dot_ref, f32[8,8,1152]{2,1,0:T(8,128)} %pad_maximum_fusion.all_lse_ref, f32[8,8,1024]{2,1,0:T(8,128)} %copy-done.3, ...), custom_call_target="tpu_custom_call" | custom-call | bytes 1 | tf_op jit(solution)/shard_map/query_terms/pallas_call | solution.py:486
  148.0 4.5 %all-to-all-start.3 = ((bf16[8,128,1024]{2,1,0:T(8,128)(2,1)}), bf16[8,128,1024]{2,1,0:T(8,128)(2,1)S(1)}, u32[]{:S(2)}, u32[]{:S(2)}) async-start(bf16[8,128,1024]{2,1,0:T(8,128)(2,1)} %bitcast.37), calls=%async_computation.3 | async-start | bytes 4194304 | tf_op jit(solution)/shard_map/all_to_all | solution.py:629
  152.5 9.1 %entry_grads.1 = (bf16[256,1024]{1,0:T(8,128)(2,1)}, bf16[256,1024]{1,0:T(8,128)(2,1)}) custom-call(f32[8,128,1024]{2,1,0:T(8,128)} %get-tuple-element.38.weight_ref, f32[16,1024]{1,0:T(8,128)} %get-tuple-element.44.stat_ref, bf16[1024,1024]{1,0:T(8,128)(2,1)} %bitcast.31, bf16[1024,1024]{1,0:T(8,128)(2,1)} %bitcast.29, bf16[256,1024]{1,0:T(8,128)(2,1)} %bitcast.36, ...), custom_call_target="tpu_custom_call" | custom-call | bytes 1 | tf_op jit(solution)/shard_map/entry_grads/pallas_call | solution.py:538
  161.6 38.5 %all-to-all-done.3 = bf16[8,128,1024]{2,1,0:T(8,128)(2,1)S(1)} async-done(((bf16[8,128,1024]{2,1,0:T(8,128)(2,1)}), bf16[8,128,1024]{2,1,0:T(8,128)(2,1)S(1)}, u32[]{:S(2)}, u32[]{:S(2)}) %all-to-all-start.3) | async-done | bytes 2097184 | tf_op jit(solution)/shard_map/all_to_all | solution.py:629
  200.1 1.8 join_places.1
  (18 shorter events, 0.1 us)
Async XLA Ops:
  0.6 12.2 %collective-permute-start.2 = (bf16[512,2048]{1,0:T(8,128)(2,1)}, bf16[512,2048]{1,0:T(8,128)(2,1)}, u32[]{:S(2)}, u32[]{:S(2)}) collective-permute-start(bf16[512,2048]{1,0:T(8,128)(2,1)} %refs_0_.1), channel_id=1, source_target_pairs={{0,1},{1,0},{2,3},{3,2},{4,5},{5,4},{6,7},{7,6},{8,9},{9,8},{10,11... | collective-permute-start | bytes 6291464 | tf_op jit(solution)/shard_map/ppermute | solution.py:558
  1.1 49.1 %collective-permute-start.1 = (bf16[512,2048]{1,0:T(8,128)(2,1)}, bf16[512,2048]{1,0:T(8,128)(2,1)}, u32[]{:S(2)}, u32[]{:S(2)}) collective-permute-start(bf16[512,2048]{1,0:T(8,128)(2,1)} %refs_0_.1), channel_id=1, source_target_pairs={{0,2},{1,3},{2,0},{3,1},{4,6},{5,7},{6,4},{7,5},{8,10},{9,11},{10,... | collective-permute-start | bytes 6291464 | tf_op jit(solution)/shard_map/ppermute | solution.py:558
  6.4 56.7 %all-to-all-start = ((bf16[8,128,1024]{2,1,0:T(8,128)(2,1)}), bf16[8,128,1024]{2,1,0:T(8,128)(2,1)S(1)}, u32[]{:S(2)}, u32[]{:S(2)}) async-start(bf16[8,128,1024]{2,1,0:T(8,128)(2,1)} %bitcast.33), calls=%async_computation | async-start | bytes 4194304 | tf_op jit(solution)/shard_map/all_to_all | solution.py:629
  50.3 6.2 %collective-permute-start.3 = (bf16[512,2048]{1,0:T(8,128)(2,1)}, bf16[512,2048]{1,0:T(8,128)(2,1)}, u32[]{:S(2)}, u32[]{:S(2)}) collective-permute-start(bf16[512,2048]{1,0:T(8,128)(2,1)} %collective-permute-done.1.refs_1_), channel_id=1, source_target_pairs={{0,1},{1,0},{2,3},{3,2},{4,5},{5,4},{6,7},{7,6},{8,9},{9,8},{10,11... | collective-permute-start | bytes 6291464 | tf_op jit(solution)/shard_map/ppermute | solution.py:558
  63.1 1.4 copy-start.2
  63.1 7.5 %copy-start = (s32[64,2]{0,1:T(2,128)S(1)}, s32[64,2]{0,1:T(2,128)}, u32[]{:S(2)}) copy-start(s32[64,2]{0,1:T(2,128)} %param.12) | copy-start | bytes 1540
  63.1 7.6 %copy-start.4 = (s32[8]{0:T(128)S(1)}, s32[8]{0:T(128)}, u32[]{:S(2)}) copy-start(s32[8]{0:T(128)} %param.13) | copy-start | bytes 100
  64.5 56.6 %all-to-all-start.1 = ((bf16[8,128,1024]{2,1,0:T(8,128)(2,1)}), bf16[8,128,1024]{2,1,0:T(8,128)(2,1)S(1)}, u32[]{:S(2)}, u32[]{:S(2)}) async-start(bf16[8,128,1024]{2,1,0:T(8,128)(2,1)} %bitcast.32), calls=%async_computation.1 | async-start | bytes 4194304 | tf_op jit(solution)/shard_map/all_to_all | solution.py:629
  84.9 36.1 %collective-permute-start = (f32[1,8,1152]{2,1,0:T(8,128)S(1)}, f32[1,8,1152]{2,1,0:T(8,128)S(1)}, u32[]{:S(2)}, u32[]{:S(2)}) collective-permute-start(f32[1,8,1152]{2,1,0:T(8,128)S(1)} %maximum_bitcast_fusion), channel_id=1, source_target_pairs={{0,16},{4,20},{8,24},{12,28},{16,0},{20,4},{24,8},{28,12},{1,17},{... | collective-permute-start | bytes 110600 | tf_op jit(solution)/shard_map/ppermute | solution.py:558
  121.1 1.3 copy-start.1
  121.1 9.2 %collective-permute-start.4 = (f32[2,8,1152]{2,1,0:T(8,128)S(1)}, f32[2,8,1152]{2,1,0:T(8,128)S(1)}, u32[]{:S(2)}, u32[]{:S(2)}) collective-permute-start(f32[2,8,1152]{2,1,0:T(8,128)S(1)} %pad_maximum_fusion.2), channel_id=1, source_target_pairs={{0,8},{4,12},{8,0},{12,4},{16,24},{20,28},{24,16},{28,20},{1,9},{5... | collective-permute-start | bytes 221192 | tf_op jit(solution)/shard_map/ppermute | solution.py:558
  126.6 15.6 %all-to-all-start.2 = ((f32[8,8,1024]{2,1,0:T(8,128)}), f32[8,8,1024]{2,1,0:T(8,128)S(1)}, u32[]{:S(2)}, u32[]{:S(2)}) async-start(f32[8,8,1024]{2,1,0:T(8,128)} %row_dots.1.told_ref.dot_ref), calls=%async_computation.2 | async-start | bytes 524288 | tf_op jit(solution)/shard_map/all_to_all | solution.py:663
  130.3 11.2 %collective-permute-start.5 = (f32[4,8,1152]{2,1,0:T(8,128)S(1)}, f32[4,8,1152]{2,1,0:T(8,128)S(1)}, u32[]{:S(2)}, u32[]{:S(2)}) collective-permute-start(f32[4,8,1152]{2,1,0:T(8,128)S(1)} %pad_maximum_fusion.1), channel_id=1, source_target_pairs={{0,4},{4,0},{8,12},{12,8},{16,20},{20,16},{24,28},{28,24},{1,5},{5... | collective-permute-start | bytes 442376 | tf_op jit(solution)/shard_map/ppermute | solution.py:558
  142.2 0.7 copy-start.3
  148.0 52.2 %all-to-all-start.3 = ((bf16[8,128,1024]{2,1,0:T(8,128)(2,1)}), bf16[8,128,1024]{2,1,0:T(8,128)(2,1)S(1)}, u32[]{:S(2)}, u32[]{:S(2)}) async-start(bf16[8,128,1024]{2,1,0:T(8,128)(2,1)} %bitcast.37), calls=%async_computation.3 | async-start | bytes 4194304 | tf_op jit(solution)/shard_map/all_to_all | solution.py:629

commit v6 on v5

--- a/solution.py
+++ b/solution.py
@@ -398,7 +398,7 @@
         out_specs=pl.BlockSpec((n_seq, heads, rows), lambda i: (0, 0, 0)),
         scratch_shapes=[pltpu.VMEM((heads, rows), F32)],
         name="row_dots",
-        **vmem_params(moved=1, mib=60),
+        **vmem_params(moved=1, mib=32),
     )(seen, grad_rows)
 
 

time: 203 us -> 203 us (level)
    unnamed x11 -> x13, local copies, waits for them, and re-layouts: 3.37 us -> 5.02 us
  transfers between devices with their start and end apart: 10 -> 10, of which waited for: 3 -> 3; matrix products, arithmetic and copies ran while one was open for 3% -> 3% of each run, Pallas kernels for 29% -> 28%
where the time goes in v6:
time: 203 us; the launch traced here: 202 us
  waiting for transfers between devices  97.4 us (48%)
  Pallas kernels  64.2 us (32%)
  starting transfers between devices  28.3 us (14%)
  local copies, waits for them, and re-layouts  8.02 us (4%)
  other arithmetic  2.81 us (1%)
    ppermute x6, waiting for transfers between devices, swap(): return lax.ppermute(value, axis, [(i, i ^ bits) for i in range(size)])  58.9 us
    all_to_all x3, waiting for transfers between devices, exchange(): lax.all_to_all(slot_rows.reshape(n_seq, slot_cap * BLOCK, cols), 'seq', 0...  38.5 us
    pallas_call x3, Pallas kernels, add_product(): pl.pallas_call(body, grid_spec=pltpu.PrefetchScalarGridSpec(num_scalar_pr...  23 us
    all_to_all x3, starting transfers between devices, exchange(): lax.all_to_all(slot_rows.reshape(n_seq, slot_cap * BLOCK, cols), 'seq', 0...  16.5 us
    pallas_call x1, Pallas kernels, local_softmax(): pl.pallas_call(body, grid=(heads,), out_shape=(jax.ShapeDtypeStruct((head...  11.3 us
    pallas_call x1, Pallas kernels, slope_terms(): pl.pallas_call(body, grid=(heads,), out_shape=jax.ShapeDtypeStruct((rows,...  9.1 us
    pallas_call x1, Pallas kernels, entry_grads(): pl.pallas_call(body, grid=(heads,), out_shape=[jax.ShapeDtypeStruct((entr...  9.06 us
    ppermute x6, starting transfers between devices, swap(): return lax.ppermute(value, axis, [(i, i ^ bits) for i in range(size)])  8.17 us
  transfers between devices with their start and end apart: 10, of which 3 were waited for; matrix products, arithmetic and copies ran while one was open for 3% of the time, Pallas kernels for 28%

profile of v6, /device:TPU:0, one launch (start us, length us, event | category | flops | bytes accessed | tf_op | source)
XLA Modules:
  0.0 201.6 jit_solution(5535748682250977119)
XLA Ops:
  0.6 0.5 collective-permute-start.2
  1.1 2.6 %collective-permute-start.1 = (bf16[512,2048]{1,0:T(8,128)(2,1)}, bf16[512,2048]{1,0:T(8,128)(2,1)}, u32[]{:S(2)}, u32[]{:S(2)}) collective-permute-start(bf16[512,2048]{1,0:T(8,128)(2,1)} %refs_0_.1), channel_id=1, source_target_pairs={{0,2},{1,3},{2,0},{3,1},{4,6},{5,7},{6,4},{7,5},{8,10},{9,11},{10,... | collective-permute-start | bytes 6291464 | tf_op jit(solution)/shard_map/ppermute | solution.py:558
  3.7 2.7 %place_rows.1 = bf16[16,64,1024]{2,1,0:T(8,128)(2,1)} custom-call(s32[2,64]{1,0:T(2,128)} %bitcast.27, s32[1]{0:T(128)} %bitcast.1.index_ref.refs_1_, bf16[512,1024]{1,0:T(8,128)(2,1)} %rows_ref.1), custom_call_target="tpu_custom_call" | custom-call | bytes 4194304 | tf_op jit(solution)/shard_map/place_rows/pallas_call | solution.py:91
  6.4 5.9 %all-to-all-start = ((bf16[8,128,1024]{2,1,0:T(8,128)(2,1)}), bf16[8,128,1024]{2,1,0:T(8,128)(2,1)S(1)}, u32[]{:S(2)}, u32[]{:S(2)}) async-start(bf16[8,128,1024]{2,1,0:T(8,128)(2,1)} %bitcast.33), calls=%async_computation | async-start | bytes 4194304 | tf_op jit(solution)/shard_map/all_to_all | solution.py:629
  12.3 0.6 pad_add_fusion.source_ref
  12.9 0.0 collective-permute-done.2.refs_1_
  12.9 10.1 %add_product.3.refs_0_ = f32[512,1024]{1,0:T(8,128)} custom-call(s32[2]{0:T(128)} %pad_add_fusion.source_ref, bf16[512,2048]{1,0:T(8,128)(2,1)} %refs_0_.1, bf16[512,2048]{1,0:T(8,128)(2,1)} %collective-permute-done.2.refs_1_, bf16[1024,8192]{1,0:T(8,128)(2,1)} %refs_4_.1, bf16[1024,8192]{1,0:T(8,128)(2,1)} %refs_4_.1), custom_call_target="tpu_custom_call" | custom-call | bytes 1 | tf_op jit(solution)/shard_map/add_product/pallas_call | solution.py:188
  23.0 27.2 %collective-permute-done.1.refs_1_ = bf16[512,2048]{1,0:T(8,128)(2,1)} collective-permute-done((bf16[512,2048]{1,0:T(8,128)(2,1)}, bf16[512,2048]{1,0:T(8,128)(2,1)}, u32[]{:S(2)}, u32[]{:S(2)}) %collective-permute-start.1) | collective-permute-done | bytes 2097184 | tf_op jit(solution)/shard_map/ppermute | solution.py:558
  50.3 0.0 collective-permute-start.3
  50.3 6.2 %add_product.4.refs_2_ = f32[512,1024]{1,0:T(8,128)} custom-call(s32[1]{0:T(128)} %bitcast.13.source_ref, f32[512,1024]{1,0:T(8,128)} %add_product.3.refs_0_, bf16[512,2048]{1,0:T(8,128)(2,1)} %collective-permute-done.1.refs_1_, bf16[1024,8192]{1,0:T(8,128)(2,1)} %refs_4_.1), custom_call_target="tpu_custom_call" | custom-call | bytes 1 | tf_op jit(solution)/shard_map/add_product/pallas_call | solution.py:188
  56.5 0.0 collective-permute-done.3.refs_3_
  56.5 6.7 %add_product.5 = bf16[16,64,1024]{2,1,0:T(8,128)(2,1)} custom-call(s32[1]{0:T(128)} %bitcast.10.source_ref, s32[2,64]{1,0:T(2,128)} %bitcast.28, s32[1]{0:T(128)} %bitcast.1.index_ref.refs_1_, f32[512,1024]{1,0:T(8,128)} %add_product.4.refs_2_, bf16[512,2048]{1,0:T(8,128)(2,1)} %collective-permute-done.3.refs_3_, bf16[1024,8192]{1,0:T(8,128)(2,1)} %refs_4_.1), custom_call_target="tpu_custom_call" | custom-call | bytes 1 | tf_op jit(solution)/shard_map/add_product/pallas_call | solution.py:188
  63.1 0.0 all-to-all-done
  63.2 0.0 copy-start.2
  63.2 0.0 copy-start.5
  63.2 1.3 copy-done.3
  64.5 6.1 %all-to-all-start.1 = ((bf16[8,128,1024]{2,1,0:T(8,128)(2,1)}), bf16[8,128,1024]{2,1,0:T(8,128)(2,1)S(1)}, u32[]{:S(2)}, u32[]{:S(2)}) async-start(bf16[8,128,1024]{2,1,0:T(8,128)(2,1)} %bitcast.32), calls=%async_computation.1 | async-start | bytes 4194304 | tf_op jit(solution)/shard_map/all_to_all | solution.py:629
  70.6 0.1 reshape.301
  70.7 0.1 copy.22
  70.8 0.1 copy.24
  70.9 0.1 copy.25
  71.0 0.1 reshape.300
  71.1 0.3 convert_reduce_fusion
  71.4 0.1 copy.27
  71.5 0.1 copy.28
  71.6 0.3 select_reduce_fusion
  72.0 0.1 copy.23
  72.1 0.1 broadcast_in_dim_reshape.4
  72.1 0.1 broadcast_in_dim.81
  72.2 0.7 broadcast_in_dim.82.entry_ref
  72.9 11.3 %local_softmax.1 = (f32[8,128,1024]{2,1,0:T(8,128)}, f32[8,1024]{1,0:T(8,128)}, f32[1024,1024]{1,0:T(8,128)}, bf16[1024,1024]{1,0:T(8,128)(2,1)}) custom-call(bf16[1024,1024]{1,0:T(8,128)(2,1)} %bitcast.30, bf16[256,1024]{1,0:T(8,128)(2,1)} %bitcast.38, bf16[256,1024]{1,0:T(8,128)(2,1)} %bitcast.34, s32[1,1024]{1,0:T(1,128)} %broadcast_in_dim.82.entry_ref), custom_call_target="tpu_custom_call" | custom-call | bytes 1 | tf_op jit(solution)/shard_map/local_softmax/pallas_call | solution.py:299
  84.2 0.8 maximum_bitcast_fusion
  85.0 2.9 %collective-permute-start = (f32[1,8,1152]{2,1,0:T(8,128)S(1)}, f32[1,8,1152]{2,1,0:T(8,128)S(1)}, u32[]{:S(2)}, u32[]{:S(2)}) collective-permute-start(f32[1,8,1152]{2,1,0:T(8,128)S(1)} %maximum_bitcast_fusion), channel_id=1, source_target_pairs={{0,16},{4,20},{8,24},{12,28},{16,0},{20,4},{24,8},{28,12},{1,17},{... | collective-permute-start | bytes 110600 | tf_op jit(solution)/shard_map/ppermute | solution.py:558
  87.9 0.1 copy.34
  88.0 0.1 stack_reshape.23
  88.0 0.1 copy.32
  88.1 0.1 stack_reshape.22
  88.2 0.1 copy.31
  88.3 0.1 stack_reshape.21
  88.4 0.1 copy.30
  88.5 0.1 stack_reshape.20
  88.5 0.1 copy.29
  88.6 0.1 stack_reshape.19
  88.7 0.1 copy.26
  88.8 0.1 stack_reshape.18
  88.9 0.6 stack.18.partner_ref
  89.5 31.6 %collective-permute-done = f32[1,8,1152]{2,1,0:T(8,128)S(1)} collective-permute-done((f32[1,8,1152]{2,1,0:T(8,128)S(1)}, f32[1,8,1152]{2,1,0:T(8,128)S(1)}, u32[]{:S(2)}, u32[]{:S(2)}) %collective-permute-start) | collective-permute-done | bytes 36896 | tf_op jit(solution)/shard_map/ppermute | solution.py:558
  121.1 0.0 all-to-all-done.1
  121.1 0.1 collective-permute-start.4
  121.2 2.9 %copy-done.1 = f32[1024,1024]{1,0:T(8,128)S(1)} copy-done((f32[1024,1024]{1,0:T(8,128)S(1)}, f32[1024,1024]{1,0:T(8,128)}, u32[]{:S(2)}) %copy-start.1) | copy-done | bytes 4194328
  124.1 2.2 %row_dots.1.told_ref.dot_ref = f32[8,8,1024]{2,1,0:T(8,128)} custom-call(f32[1024,1024]{1,0:T(8,128)S(1)} %copy-done.1, bf16[1024,1024]{1,0:T(8,128)(2,1)S(1)} %bitcast.23), custom_call_target="tpu_custom_call" | custom-call | bytes 1 | tf_op jit(solution)/shard_map/row_dots/pallas_call | solution.py:390
  126.3 3.6 %all-to-all-start.2 = ((f32[8,8,1024]{2,1,0:T(8,128)}), f32[8,8,1024]{2,1,0:T(8,128)S(1)}, u32[]{:S(2)}, u32[]{:S(2)}) async-start(f32[8,8,1024]{2,1,0:T(8,128)} %row_dots.1.told_ref.dot_ref), calls=%async_computation.2 | async-start | bytes 524288 | tf_op jit(solution)/shard_map/all_to_all | solution.py:663
  130.0 0.0 collective-permute-done.4
  130.0 2.1 %collective-permute-start.5 = (f32[4,8,1152]{2,1,0:T(8,128)S(1)}, f32[4,8,1152]{2,1,0:T(8,128)S(1)}, u32[]{:S(2)}, u32[]{:S(2)}) collective-permute-start(f32[4,8,1152]{2,1,0:T(8,128)S(1)} %pad_maximum_fusion.1), channel_id=1, source_target_pairs={{0,4},{4,0},{8,12},{12,8},{16,20},{20,16},{24,28},{28,24},{1,5},{5... | collective-permute-start | bytes 442376 | tf_op jit(solution)/shard_map/ppermute | solution.py:558
  132.1 9.1 %slope_terms.1.term_ref = bf16[1024,1024]{1,0:T(8,128)(2,1)} custom-call(f32[8,128,1024]{2,1,0:T(8,128)} %get-tuple-element.38.weight_ref, f32[8,8,1024]{2,1,0:T(8,128)} %row_dots.1.told_ref.dot_ref, bf16[1024,1024]{1,0:T(8,128)(2,1)} %bitcast.24, bf16[256,1024]{1,0:T(8,128)(2,1)} %bitcast.39, bf16[256,1024]{1,0:T(8,128)(2,1)} %bitcast.35, ...), custom_call_target="tpu_custom_call" | custom-call | bytes 1 | tf_op jit(solution)/shard_map/slope_terms/pallas_call | solution.py:426
  141.2 0.0 collective-permute-done.5
  141.2 0.7 pad_maximum_fusion.all_lse_ref
  141.9 0.0 all-to-all-done.2.all_dot_ref
  141.9 0.7 copy-done.4
  142.6 5.1 %query_terms.1 = (f32[16,1024]{1,0:T(8,128)}, bf16[1024,1024]{1,0:T(8,128)(2,1)}) custom-call(s32[6,16]{1,0:T(8,128)} %stack.18.partner_ref, f32[8,1024]{1,0:T(8,128)} %get-tuple-element.34.lse_ref, f32[8,8,1024]{2,1,0:T(8,128)} %row_dots.1.told_ref.dot_ref, f32[8,8,1152]{2,1,0:T(8,128)} %pad_maximum_fusion.all_lse_ref, f32[8,8,1024]{2,1,0:T(8,128)} %copy-done.4, ...), custom_call_target="tpu_custom_call" | custom-call | bytes 1 | tf_op jit(solution)/shard_map/query_terms/pallas_call | solution.py:486
  147.7 4.5 %all-to-all-start.3 = ((bf16[8,128,1024]{2,1,0:T(8,128)(2,1)}), bf16[8,128,1024]{2,1,0:T(8,128)(2,1)S(1)}, u32[]{:S(2)}, u32[]{:S(2)}) async-start(bf16[8,128,1024]{2,1,0:T(8,128)(2,1)} %bitcast.37), calls=%async_computation.3 | async-start | bytes 4194304 | tf_op jit(solution)/shard_map/all_to_all | solution.py:629
  152.2 9.1 %entry_grads.1 = (bf16[256,1024]{1,0:T(8,128)(2,1)}, bf16[256,1024]{1,0:T(8,128)(2,1)}) custom-call(f32[8,128,1024]{2,1,0:T(8,128)} %get-tuple-element.38.weight_ref, f32[16,1024]{1,0:T(8,128)} %get-tuple-element.44.stat_ref, bf16[1024,1024]{1,0:T(8,128)(2,1)} %bitcast.31, bf16[1024,1024]{1,0:T(8,128)(2,1)} %bitcast.25, bf16[256,1024]{1,0:T(8,128)(2,1)} %bitcast.36, ...), custom_call_target="tpu_custom_call" | custom-call | bytes 1 | tf_op jit(solution)/shard_map/entry_grads/pallas_call | solution.py:538
  161.3 38.5 %all-to-all-done.3 = bf16[8,128,1024]{2,1,0:T(8,128)(2,1)S(1)} async-done(((bf16[8,128,1024]{2,1,0:T(8,128)(2,1)}), bf16[8,128,1024]{2,1,0:T(8,128)(2,1)S(1)}, u32[]{:S(2)}, u32[]{:S(2)}) %all-to-all-start.3) | async-done | bytes 2097184 | tf_op jit(solution)/shard_map/all_to_all | solution.py:629
  199.8 1.8 join_places.1
  (20 shorter events, 0.2 us)
Async XLA Ops:
  0.6 12.2 %collective-permute-start.2 = (bf16[512,2048]{1,0:T(8,128)(2,1)}, bf16[512,2048]{1,0:T(8,128)(2,1)}, u32[]{:S(2)}, u32[]{:S(2)}) collective-permute-start(bf16[512,2048]{1,0:T(8,128)(2,1)} %refs_0_.1), channel_id=1, source_target_pairs={{0,1},{1,0},{2,3},{3,2},{4,5},{5,4},{6,7},{7,6},{8,9},{9,8},{10,11... | collective-permute-start | bytes 6291464 | tf_op jit(solution)/shard_map/ppermute | solution.py:558
  1.1 49.1 %collective-permute-start.1 = (bf16[512,2048]{1,0:T(8,128)(2,1)}, bf16[512,2048]{1,0:T(8,128)(2,1)}, u32[]{:S(2)}, u32[]{:S(2)}) collective-permute-start(bf16[512,2048]{1,0:T(8,128)(2,1)} %refs_0_.1), channel_id=1, source_target_pairs={{0,2},{1,3},{2,0},{3,1},{4,6},{5,7},{6,4},{7,5},{8,10},{9,11},{10,... | collective-permute-start | bytes 6291464 | tf_op jit(solution)/shard_map/ppermute | solution.py:558
  6.4 56.7 %all-to-all-start = ((bf16[8,128,1024]{2,1,0:T(8,128)(2,1)}), bf16[8,128,1024]{2,1,0:T(8,128)(2,1)S(1)}, u32[]{:S(2)}, u32[]{:S(2)}) async-start(bf16[8,128,1024]{2,1,0:T(8,128)(2,1)} %bitcast.33), calls=%async_computation | async-start | bytes 4194304 | tf_op jit(solution)/shard_map/all_to_all | solution.py:629
  50.3 6.2 %collective-permute-start.3 = (bf16[512,2048]{1,0:T(8,128)(2,1)}, bf16[512,2048]{1,0:T(8,128)(2,1)}, u32[]{:S(2)}, u32[]{:S(2)}) collective-permute-start(bf16[512,2048]{1,0:T(8,128)(2,1)} %collective-permute-done.1.refs_1_), channel_id=1, source_target_pairs={{0,1},{1,0},{2,3},{3,2},{4,5},{5,4},{6,7},{7,6},{8,9},{9,8},{10,11... | collective-permute-start | bytes 6291464 | tf_op jit(solution)/shard_map/ppermute | solution.py:558
  63.2 1.4 copy-start.3
  63.2 7.5 %copy-start.2 = (s32[64,2]{0,1:T(2,128)S(1)}, s32[64,2]{0,1:T(2,128)}, u32[]{:S(2)}) copy-start(s32[64,2]{0,1:T(2,128)} %param.12) | copy-start | bytes 1540
  63.2 7.6 %copy-start.5 = (s32[8]{0:T(128)S(1)}, s32[8]{0:T(128)}, u32[]{:S(2)}) copy-start(s32[8]{0:T(128)} %param.13) | copy-start | bytes 100
  64.5 56.6 %all-to-all-start.1 = ((bf16[8,128,1024]{2,1,0:T(8,128)(2,1)}), bf16[8,128,1024]{2,1,0:T(8,128)(2,1)S(1)}, u32[]{:S(2)}, u32[]{:S(2)}) async-start(bf16[8,128,1024]{2,1,0:T(8,128)(2,1)} %bitcast.32), calls=%async_computation.1 | async-start | bytes 4194304 | tf_op jit(solution)/shard_map/all_to_all | solution.py:629
  85.0 36.2 %collective-permute-start = (f32[1,8,1152]{2,1,0:T(8,128)S(1)}, f32[1,8,1152]{2,1,0:T(8,128)S(1)}, u32[]{:S(2)}, u32[]{:S(2)}) collective-permute-start(f32[1,8,1152]{2,1,0:T(8,128)S(1)} %maximum_bitcast_fusion), channel_id=1, source_target_pairs={{0,16},{4,20},{8,24},{12,28},{16,0},{20,4},{24,8},{28,12},{1,17},{... | collective-permute-start | bytes 110600 | tf_op jit(solution)/shard_map/ppermute | solution.py:558
  121.1 5.2 %copy-start = (bf16[8,128,1024]{2,1,0:T(8,128)(2,1)}, bf16[8,128,1024]{2,1,0:T(8,128)(2,1)S(1)}, u32[]{:S(2)}) copy-start(bf16[8,128,1024]{2,1,0:T(8,128)(2,1)S(1)} %all-to-all-done.1) | copy-start | bytes 6291460
  121.1 8.8 %collective-permute-start.4 = (f32[2,8,1152]{2,1,0:T(8,128)S(1)}, f32[2,8,1152]{2,1,0:T(8,128)S(1)}, u32[]{:S(2)}, u32[]{:S(2)}) collective-permute-start(f32[2,8,1152]{2,1,0:T(8,128)S(1)} %pad_maximum_fusion.2), channel_id=1, source_target_pairs={{0,8},{4,12},{8,0},{12,4},{16,24},{20,28},{24,16},{28,20},{1,9},{5... | collective-permute-start | bytes 221192 | tf_op jit(solution)/shard_map/ppermute | solution.py:558
  121.2 2.9 %copy-start.1 = (f32[1024,1024]{1,0:T(8,128)S(1)}, f32[1024,1024]{1,0:T(8,128)}, u32[]{:S(2)}) copy-start(f32[1024,1024]{1,0:T(8,128)} %get-tuple-element.35.seen_ref) | copy-start | bytes 12582916
  126.3 15.6 %all-to-all-start.2 = ((f32[8,8,1024]{2,1,0:T(8,128)}), f32[8,8,1024]{2,1,0:T(8,128)S(1)}, u32[]{:S(2)}, u32[]{:S(2)}) async-start(f32[8,8,1024]{2,1,0:T(8,128)} %row_dots.1.told_ref.dot_ref), calls=%async_computation.2 | async-start | bytes 524288 | tf_op jit(solution)/shard_map/all_to_all | solution.py:663
  130.0 11.2 %collective-permute-start.5 = (f32[4,8,1152]{2,1,0:T(8,128)S(1)}, f32[4,8,1152]{2,1,0:T(8,128)S(1)}, u32[]{:S(2)}, u32[]{:S(2)}) collective-permute-start(f32[4,8,1152]{2,1,0:T(8,128)S(1)} %pad_maximum_fusion.1), channel_id=1, source_target_pairs={{0,4},{4,0},{8,12},{12,8},{16,20},{20,16},{24,28},{28,24},{1,5},{5... | collective-permute-start | bytes 442376 | tf_op jit(solution)/shard_map/ppermute | solution.py:558
  141.9 0.7 copy-start.4
  147.7 52.2 %all-to-all-start.3 = ((bf16[8,128,1024]{2,1,0:T(8,128)(2,1)}), bf16[8,128,1024]{2,1,0:T(8,128)(2,1)S(1)}, u32[]{:S(2)}, u32[]{:S(2)}) async-start(bf16[8,128,1024]{2,1,0:T(8,128)(2,1)} %bitcast.37), calls=%async_computation.3 | async-start | bytes 4194304 | tf_op jit(solution)/shard_map/all_to_all | solution.py:629
